TPU v7x, 32 devices: a whole 2x2x4 slice. The times are simulated.
32 devices in a mesh: date: 8 (over z, core), path: 4 (over y, x).
Axes of the slice: x: 2, y: 2, z: 4, core: 2. Of those that a mesh axis runs over, the one named last changes fastest.
Arguments:
- features: bfloat16 [16, 512, 2048], P('date', 'path'), may hold values from -6 to 6
- payoff: float32 [16, 512, 256], P('date', 'path'), may hold values from -8 to 64
- coefficients: bfloat16 [2048, 256], replicated, may hold values from -0.02734375 to 0.02734375
- exercise: int32 [16, 256], P('date'), may hold values from 0 to 1, as said below
Outputs:
- gradient: float32 [2048, 256], P(('date', 'path'))
- bound: float32 [256], replicated
- spread: float32 [256], replicated
Inputs may be any that keep to these rules, and one draw needn't show every extreme that they name: `exercise`: every contract may be exercised at the first and at the last date.
All inputs are finite; a program needn't handle non-finite values.
Results may differ from a plain program's by a relative error of at most 0.0017.
Values sent between devices are 32-bit elements; how exact they have to be, the bound alone decides.
No kernel may reach another device: no remote copies, remote signals or barrier semaphores. Data moves between devices by JAX's collectives and lax.ppermute only.
A program may use at most 64 MiB of HBM per device.

v0:
```python
import jax
import jax.numpy as jnp
from jax import lax
from jax.sharding import PartitionSpec as P

TEMP = 0.25
NEG = -1e30


def entering(value, axis, join, neutral, backward):
    count, mine = (lax.axis_size(axis), lax.axis_index(axis))
    pieces = lax.all_gather(value, axis)
    if backward:
        pieces = pieces[::-1]
        mine = count - 1 - mine
    total = jnp.full_like(value, 0) + jnp.asarray(neutral, value.dtype)

    def hop(position, total):
        longer = join(total, pieces[position])
        return jnp.where(position < mine, longer, total)

    return lax.fori_loop(0, count - 1, hop, total)


def shards(features, payoff, coefficients, exercise):
    dates_dev, paths_dev, width = features.shape
    contracts = coefficients.shape[1]
    paths_total = paths_dev * lax.axis_size("path")
    flat = features.reshape(-1, width)
    increments = jnp.dot(flat, coefficients, preferred_element_type=jnp.float32).reshape(
        dates_dev, paths_dev, contracts
    )
    local_sums = jnp.cumsum(increments, axis=0)
    block_total = local_sums[-1]
    earlier = entering(block_total, "date", lambda a, b: a + b, jnp.zeros_like(block_total), False)
    martingale = local_sums + earlier[None]
    allowed = exercise[:, None, :] > 0
    score = jnp.where(allowed, (payoff - martingale) / TEMP, NEG)
    local_peak = jnp.max(score, axis=0)
    peak = lax.pmax(local_peak, "date")
    shifted = jnp.exp(score - peak[None])
    total = lax.psum(jnp.sum(shifted, axis=0), "date")
    smoothed = TEMP * (peak + jnp.log(total))
    weight = shifted / total[None]
    local_tail = jnp.flip(jnp.cumsum(jnp.flip(weight, 0), axis=0), 0)
    later = entering(local_tail[0], "date", lambda a, b: a + b, jnp.zeros_like(local_tail[0]), True)
    tail = (local_tail + later[None]).astype(jnp.bfloat16).reshape(-1, contracts)
    columns = features.reshape(-1, width // lax.axis_size("date") * lax.axis_size("date"))
    product = jnp.dot(columns.T, tail, preferred_element_type=jnp.float32)
    partial_rows = lax.psum_scatter(-product / paths_total, "date", scatter_dimension=0, tiled=True)
    gradient = lax.psum_scatter(partial_rows, "path", scatter_dimension=0, tiled=True)
    first_sum, second_sum = lax.psum(
        (jnp.sum(smoothed, axis=0), jnp.sum(smoothed * smoothed, axis=0)), "path"
    )
    bound = first_sum / paths_total
    spread = second_sum / paths_total - bound * bound
    return (gradient, bound, spread)


def solution(mesh):
    placed = (P("date", "path", None), P("date", "path", None), P(), P("date", None))
    return jax.shard_map(
        shards,
        mesh=mesh,
        in_specs=placed,
        out_specs=(P(("date", "path"), None), P(), P()),
        check_vma=False,
    )
```

profile of v0, /device:TPU:0, one launch (start us, length us, event | category | flops | bytes accessed | tf_op | source)
XLA Modules:
  0.0 248.2 jit_solution(10332294215667335601)
XLA Ops:
  7.2 0.0 copy-start
  7.2 0.0 copy-start.4
  7.2 0.0 all-gather.3.cloned.1.call-start
  7.2 1.2 copy-done
  8.4 1.7 fusion.3
  10.1 0.0 copy-start.3
  10.1 0.1 fusion.9
  10.2 0.7 slice.9
  10.9 0.0 all-gather.3.cloned.1.call-update
  10.9 0.0 all-reduce.4.cloned.1.call-start
  11.0 0.0 copy-done.4
  11.0 24.9 %all-gather.3.cloned.1.call-done = f32[8,128,256]{2,1,0:T(8,128)} async-done(((f32[1,128,256]{2,1,0:T(8,128)}), f32[8,128,256]{2,1,0:T(8,128)}) %all-gather.3.cloned.1.call-update) | async-done | bytes 1048592 | tf_op jit(solution)/shard_map/all_gather | solution.py:12
  35.8 6.8 %while.28 = (s32[]{:T(128)}, f32[128,256]{1,0:T(8,128)S(1)}, s32[]{:T(128)}, f32[8,128,256]{2,1,0:T(8,128)}, s32[]{:T(128)}, /*index=5*/s32[]{:T(128)}) while((s32[]{:T(128)}, f32[128,256]{1,0:T(8,128)S(1)}, s32[]{:T(128)}, f32[8,128,256]{2,1,0:T(8,128)}, s32[]{:T(128)}, /*index=5*/s32[]{:T(128)}) %tuple.68), condition=%wide.region_2.3_spmd.clone, body=%wide.region_1.2_spmd.clone.sunk | while | flops 98308 | bytes 393309 | solution.py:22
  35.8 0.9 add_select_fusion.4
  36.8 0.9 add_select_fusion.4
  37.8 0.9 add_select_fusion.4
  38.8 0.9 add_select_fusion.4
  39.7 0.9 add_select_fusion.4
  40.7 0.9 add_select_fusion.4
  41.7 0.9 add_select_fusion.4
  42.6 0.0 copy-done.3
  42.6 0.7 fusion.8
  43.3 0.0 all-reduce.4.cloned.1.call-update
  43.4 0.0 all-reduce.6.cloned.1.call-start
  43.4 54.0 %all-reduce.4.cloned.1.call-done = f32[128,256]{1,0:T(8,128)} async-done(((f32[128,256]{1,0:T(8,128)}), f32[128,256]{1,0:T(8,128)}) %all-reduce.4.cloned.1.call-update) | async-done | bytes 131088 | tf_op jit(solution)/shard_map/pmax | solution.py:40
  97.4 1.6 fusion.6
  99.0 0.0 all-reduce.6.cloned.1.call-update
  99.0 0.0 all-gather.5.cloned.1.call-start
  99.1 54.1 %all-reduce.6.cloned.1.call-done = f32[128,256]{1,0:T(8,128)} async-done(((f32[128,256]{1,0:T(8,128)}), f32[128,256]{1,0:T(8,128)}) %all-reduce.6.cloned.1.call-update) | async-done | bytes 131088 | tf_op jit(solution)/shard_map/psum | solution.py:42
  153.1 1.0 fusion.5
  154.2 0.1 fusion.10
  154.3 0.7 slice.10
  155.0 0.0 all-gather.5.cloned.1.call-update
  155.0 0.0 reduce-scatter.5.cloned.1.call-start
  155.0 21.2 %all-gather.5.cloned.1.call-done = f32[8,128,256]{2,1,0:T(8,128)} async-done(((f32[1,128,256]{2,1,0:T(8,128)}), f32[8,128,256]{2,1,0:T(8,128)}) %all-gather.5.cloned.1.call-update) | async-done | bytes 1048592 | tf_op jit(solution)/shard_map/all_gather | solution.py:12
  176.2 1.3 rev.12
  177.6 0.5 while.29
  178.1 1.8 fusion.2
  179.9 0.0 reduce-scatter.5.cloned.1.call-update
  179.9 0.0 reduce-scatter.7.cloned.1.call-start
  180.0 35.5 %reduce-scatter.5.cloned.1.call-done = f32[256,256]{0,1:T(8,128)} async-done(((f32[2048,256]{0,1:T(8,128)}), f32[256,256]{0,1:T(8,128)}) %reduce-scatter.5.cloned.1.call-update) | async-done | bytes 262160 | tf_op jit(solution)/shard_map/reduce_scatter | solution.py:50
  215.4 1.8 copy.12
  217.2 0.0 reduce-scatter.7.cloned.1.call-update
  217.2 0.0 copy-done.1
  217.3 0.1 multiply_reduce_fusion
  217.3 9.9 %all-reduce = (f32[256]{0:T(256)S(1)}, f32[256]{0:T(256)S(1)}) all-reduce(f32[256]{0:T(256)S(1)} %get-tuple-element.200, f32[256]{0:T(256)S(1)} %get-tuple-element.199), channel_id=1, replica_groups=mesh['date'=8,'path'=4] {'path'}, use_global_device_ids=true, to_apply=%region_13.14 | all-reduce | flops 512 | bytes 4096 | tf_op jit(solution)/shard_map/psum | solution.py:52
  227.2 0.6 multiply_subtract_fusion
  227.8 13.5 %reduce-scatter.7.cloned.1.call-done = f32[64,256]{1,0:T(8,128)} async-done(((f32[256,256]{1,0:T(8,128)}), f32[64,256]{1,0:T(8,128)}) %reduce-scatter.7.cloned.1.call-update) | async-done | bytes 65552
  (15 shorter events, 0.3 us)
Async XLA Ops:
  7.2 1.2 copy-start
  7.2 3.8 %copy-start.4 = (s32[2,256]{1,0:T(2,128)S(1)}, s32[2,256]{1,0:T(2,128)}, u32[]{:S(2)}) copy-start(s32[2,256]{1,0:T(2,128)} %param.11) | copy-start | bytes 6148
  7.2 28.7 %all-gather.3.cloned.1.call-start = ((), (), s32[]{:S(2)}) async-start(), calls=%async_computation.2 | async-start | bytes 1179648 | tf_op jit(solution)/shard_map/all_gather | solution.py:12
  10.1 32.6 %copy-start.3 = (f32[2,128,256]{2,1,0:T(8,128)S(1)}, f32[2,128,256]{2,1,0:T(8,128)}, u32[]{:S(2)}) copy-start(f32[2,128,256]{2,1,0:T(8,128)} %param.9) | copy-start | bytes 786436
  10.9 86.5 %all-reduce.4.cloned.1.call-start = ((), (), s32[]{:S(2)}) async-start(), calls=%async_computation.3 | async-start | bytes 262144 | tf_op jit(solution)/shard_map/pmax | solution.py:40
  43.4 109.7 %all-reduce.6.cloned.1.call-start = ((), (), s32[]{:S(2)}) async-start(), calls=%async_computation.4 | async-start | bytes 262144 | tf_op jit(solution)/shard_map/psum | solution.py:42
  99.0 77.2 %all-gather.5.cloned.1.call-start = ((), (), s32[]{:S(2)}) async-start(), calls=%async_computation.5 | async-start | bytes 1179648 | tf_op jit(solution)/shard_map/all_gather | solution.py:12
  155.0 60.5 %reduce-scatter.5.cloned.1.call-start = ((), (), s32[]{:S(2)}) async-start(), calls=%async_computation.6 | async-start | bytes 2359296 | tf_op jit(solution)/shard_map/reduce_scatter | solution.py:50
  179.9 37.4 %copy-start.1 = (f32[128,256]{1,0:T(8,128)S(1)}, f32[128,256]{1,0:T(8,128)}, u32[]{:S(2)}) copy-start(f32[128,256]{1,0:T(8,128)} %all-reduce.4.cloned.1.call-done) | copy-start | bytes 393220
  179.9 37.4 %copy-start.2 = (f32[128,256]{1,0:T(8,128)S(1)}, f32[128,256]{1,0:T(8,128)}, u32[]{:S(2)}) copy-start(f32[128,256]{1,0:T(8,128)} %all-reduce.6.cloned.1.call-done) | copy-start | bytes 393220
  179.9 61.4 %reduce-scatter.7.cloned.1.call-start = ((), (), s32[]{:S(2)}) async-start(), calls=%async_computation.7 | async-start | bytes 327680
Sparse Core Ops, SparseCore 0:
  11.0 24.7 all-gather.2
  43.5 53.8 all-reduce.3
  99.8 53.2 all-reduce.5
  155.1 21.0 all-gather.4
  180.0 35.3 reduce-scatter.4
  218.6 22.6 reduce-scatter.6
where the time goes:
time: 249 us; the launch traced here: 248 us
  waiting for transfers between devices  203 us (82%)
  between operations  14.3 us (6%)
  other arithmetic  11.2 us (4%)
  blocking collectives  9.92 us (4%)
  local copies, waits for them, and re-layouts  5.61 us (2%)
  matrix products  3.47 us (1%)
    psum x1, waiting for transfers between devices, shards(): total = lax.psum(jnp.sum(shifted, axis=0), 'date')  54.1 us
    pmax x1, waiting for transfers between devices, shards(): peak = lax.pmax(local_peak, 'date')  54 us
    all_gather x2, waiting for transfers between devices, entering(): pieces = lax.all_gather(value, axis)  46.1 us
    reduce_scatter x1, waiting for transfers between devices, shards(): lax.psum_scatter(-product / paths_total, 'date', scatter_dimension=0, til...  35.5 us
    unnamed x7, waiting for transfers between devices  13.6 us
    psum x1, blocking collectives, shards(): lax.psum((jnp.sum(smoothed, axis=0), jnp.sum(smoothed * smoothed, axis=0)...  9.92 us
    select_n x14, other arithmetic, hop(): return jnp.where(position < mine, longer, total)  6.93 us
  transfers between devices with their start and end apart: 6, of which 6 were waited for; matrix products, arithmetic and copies ran while one was open for 0% of the time, Pallas kernels for 0%

commit v1 on v0

v1 whole, which is shorter than its diff:
```python
import functools

import jax
import jax.numpy as jnp
from jax import lax
from jax.experimental import pallas as pl
from jax.experimental.pallas import tpu as pltpu
from jax.sharding import PartitionSpec as P

INVERSE_TEMP = 4.0
TEMP = 0.25
NEG = -1e30
STAT_ROWS = 8
VMEM_LIMIT = 16 << 20
f32 = jnp.float32
bf16 = jnp.bfloat16


def core_of():
    return lax.axis_index("date") % 2


def chip_of():
    return lax.axis_index("date") // 2


def call(body, outs, *operands, scratch=(), flops=0, unread=0):
    whole = pl.BlockSpec(memory_space=pltpu.VMEM)
    anywhere = pl.BlockSpec(memory_space=pl.ANY)
    read = len(operands) - unread

    def kernel(*refs):
        body(*refs[:read], *refs[read + unread :])

    return pl.pallas_call(
        kernel,
        out_shape=[jax.ShapeDtypeStruct(*o) for o in outs],
        in_specs=[whole] * read + [anywhere] * unread,
        out_specs=[whole] * len(outs),
        scratch_shapes=list(scratch),
        compiler_params=pltpu.CompilerParams(vmem_limit_bytes=VMEM_LIMIT),
        cost_estimate=pl.CostEstimate(flops=flops, bytes_accessed=0, transcendentals=0),
    )(*operands)


def log_add(a, b):
    return jnp.maximum(a, b) + jnp.log(1.0 + jnp.exp(-jnp.abs(a - b)))


def increments_body(features, coefficients, payoff, exercise, keep, send, inc):
    dates, paths, width = features.shape
    half = paths // 2
    product = jnp.dot(features[...].reshape(dates * paths, width), coefficients[...], preferred_element_type=f32)
    inc[...] = (INVERSE_TEMP * product).reshape(inc.shape)
    mine = pl.multiple_of(core_of() * half, half)
    theirs = pl.multiple_of((1 - core_of()) * half, half)
    for out, at in ((keep, mine), (send, theirs)):
        out[0:dates] = inc[:, pl.ds(at, half)]
        for d in range(dates):
            allowed = exercise[d : d + 1, :] > 0
            out[dates + d] = jnp.where(allowed, INVERSE_TEMP * payoff[d, pl.ds(at, half)], NEG)


def message_of(level, total, left, last):
    if last:
        return [jnp.where(left, level + total, level)]
    return [level, total]


def local_body(rounds, keep, other, score, level, total, message):
    dates = keep.shape[0] // 2
    first = core_of() == 0
    run = jnp.zeros(keep.shape[1:], f32)
    scores = []
    for part in (0, 1):
        for d in range(dates):
            inc, base = (
                jnp.where(first == (part == 0), keep[at], other[at]) for at in (d, dates + d)
            )
            run = run + inc
            scores.append(base - run)
    peak = functools.reduce(jnp.maximum, scores)
    lev = peak + jnp.log(sum(jnp.exp(s - peak) for s in scores))
    for i, s in enumerate(scores):
        score[i] = s
    level[...] = lev
    total[...] = run
    left = chip_of() % 2 == 0
    for i, m in enumerate(message_of(lev, run, left, rounds == 1)):
        message[i] = m


def merge_body(step, rounds, level, total, state, got, level2, total2, state2, message):
    left = (chip_of() >> step) % 2 == 0
    lev, tot, other_lev, other_tot = level[...], total[...], got[0], got[1]
    if state is None:
        zero = jnp.zeros_like(lev)
        before, after, sum_before, sum_after = zero + NEG, zero + NEG, zero, zero
    else:
        before, after, sum_before, sum_after = (state[i] for i in range(4))
    state2[0] = jnp.where(left, before, log_add(before, other_lev + other_tot + sum_before))
    state2[1] = jnp.where(left, log_add(after, other_lev - sum_after), after)
    state2[2] = jnp.where(left, sum_before, sum_before + other_tot)
    state2[3] = jnp.where(left, sum_after + other_tot, sum_after)
    first_lev, first_tot = jnp.where(left, lev, other_lev), jnp.where(left, tot, other_tot)
    second_lev = jnp.where(left, other_lev, lev)
    lev2 = log_add(first_lev, second_lev - first_tot)
    tot2 = tot + other_tot
    level2[...] = lev2
    total2[...] = tot2
    next_left = (chip_of() >> (step + 1)) % 2 == 0
    for i, m in enumerate(message_of(lev2, tot2, next_left, step + 2 == rounds)):
        message[i] = m


def tail_body(rounds, score, level, total, state, got, out):
    lev, tot = level[...], total[...]
    zero = jnp.zeros_like(lev)
    if state is None:
        before, after, sum_before, sum_after = zero + NEG, zero + NEG, zero, zero
    else:
        before, after, sum_before, sum_after = (state[i] for i in range(4))
    if got is not None:
        left = (chip_of() >> (rounds - 1)) % 2 == 0
        other = got[0]
        before = jnp.where(left, before, log_add(before, other + sum_before))
        after = jnp.where(left, log_add(after, other - sum_after), after)
    later = after - tot
    norm = log_add(log_add(before, lev), later)
    run = jnp.exp(later - norm)
    half = score.shape[1]
    for i in reversed(range(score.shape[0])):
        run = run + jnp.exp(score[i] - norm)
        out[i * half : (i + 1) * half, :] = run.astype(bf16).astype(f32)
    smoothed = jnp.where(chip_of() == 0, TEMP * norm, 0.0)
    at = score.shape[0] * half
    out[at : at + STAT_ROWS, :] = jnp.zeros((STAT_ROWS, smoothed.shape[1]), f32)
    out[at : at + 1, :] = jnp.sum(smoothed, axis=0, keepdims=True)
    out[at + 1 : at + 2, :] = jnp.sum(smoothed * smoothed, axis=0, keepdims=True)


def halves_body(chips, features, send):
    width = features.shape[2] // (2 * chips)
    for z in range(chips):
        at = pl.multiple_of((2 * z + 1 - core_of()) * width, width)
        send[:, :, z * width : (z + 1) * width] = features[:, :, pl.ds(at, width)].astype(f32)


def columns_body(chips, features, got, columns):
    dates, paths, whole = features.shape
    width = whole // (2 * chips)
    mine, theirs = core_of() * dates, (1 - core_of()) * dates
    for z in range(chips):
        at = pl.multiple_of((2 * z + core_of()) * width, width)
        rows = slice(z * width, (z + 1) * width)
        for d in range(dates):
            own = features[d, :, pl.ds(at, width)].T
            columns[rows, pl.ds(pl.multiple_of((mine + d) * paths, paths), paths)] = own
            other = got[d, :, rows].astype(bf16).T
            columns[rows, pl.ds(pl.multiple_of((theirs + d) * paths, paths), paths)] = other


def product_body(scale, paths_count, columns, own, got, keep, *rest):
    messages, (tail, product) = rest[: paths_count - 1], rest[paths_count - 1 :]
    dates, paths, contracts = tail.shape
    half = paths // 2
    for source, at in ((own, core_of()), (got, 1 - core_of())):
        rows = pl.ds(pl.multiple_of(at * half, half), half)
        for d in range(dates):
            tail[d, rows] = source[d * half : (d + 1) * half, :].astype(bf16)
    right = tail[...].reshape(dates * paths, contracts)
    chips, count, rows, _ = product.shape
    width = count * rows
    for z in range(chips):
        block = jnp.dot(columns[z * width : (z + 1) * width, :], right, preferred_element_type=f32)
        product[z] = (scale * block).reshape(count, rows, contracts)
    stats = own[dates * half :, :] + got[dates * half :, :]
    me = lax.axis_index("path")
    for j, out in enumerate((keep, *messages)):
        for z in range(chips):
            out[z * rows : (z + 1) * rows, :] = product[z, partner(me, j, count)]
        out[chips * rows :, :] = stats


def partner(me, j, count):
    if count & (count - 1) == 0:
        return me ^ j
    return lax.rem(me + j, count)


def pairs(count, j):
    if count & (count - 1) == 0:
        return [(i, i ^ j) for i in range(count)]
    return [(i, (i + j) % count) for i in range(count)]


def date_pairs(chips, j):
    return [(2 * a + core, 2 * b + core) for a, b in pairs(chips, j) for core in range(2)]


def path_sum_body(count, chips, *refs):
    parts, (keep, *messages), (total,) = refs[:count], refs[count : count + chips], refs[count + chips :]
    total[...] = functools.reduce(lambda a, b: a + b, (p[...] for p in parts))
    rows = (total.shape[0] - STAT_ROWS) // chips
    for j, out in enumerate((keep, *messages)):
        at = pl.multiple_of(partner(chip_of(), j, chips) * rows, rows)
        out[0:rows, :] = total[pl.ds(at, rows), :]
        out[rows:, :] = total[chips * rows :, :]


def date_sum_body(chips, paths_total, *refs):
    parts, (gradient, bound, spread) = refs[:chips], refs[chips:]
    total = functools.reduce(lambda a, b: a + b, (p[...] for p in parts))
    rows = gradient.shape[0]
    gradient[...] = total[:rows, :]
    mean = total[rows : rows + 1, :] * (1.0 / paths_total)
    bound[...] = mean
    spread[...] = total[rows + 1 : rows + 2, :] * (1.0 / paths_total) - mean * mean


def shards(features, payoff, coefficients, exercise):
    dates, paths, width = features.shape
    contracts = coefficients.shape[1]
    chips, count = lax.axis_size("date") // 2, lax.axis_size("path")
    rounds = chips.bit_length() - 1
    assert chips == 1 << rounds
    half, paths_total = paths // 2, paths * count
    rows = width // (2 * chips * count)
    cores = [(2 * z + c, 2 * z + 1 - c) for z in range(chips) for c in range(2)]
    plane = (half, contracts)

    keep, send = call(
        increments_body,
        [((2 * dates, *plane), f32)] * 2,
        features,
        coefficients,
        payoff,
        exercise,
        scratch=[pltpu.VMEM((dates, paths, contracts), f32)],
        flops=2 * dates * paths * width * contracts,
    )
    other = lax.ppermute(send, "date", cores)
    sizes = [1 if step + 1 == rounds else 2 for step in range(rounds)] or [2]
    score, level, total, message = call(
        functools.partial(local_body, rounds),
        [((2 * dates, *plane), f32), (plane, f32), (plane, f32), ((sizes[0], *plane), f32)],
        keep,
        other,
    )
    (columns_send,) = call(
        functools.partial(halves_body, chips),
        [((dates, paths, width // 2), f32)],
        features,
        message,
        unread=1,
        flops=1 << 26,
    )
    own_level, own_total, state, got = level, total, None, None
    columns_got = lax.ppermute(columns_send, "date", cores)
    for step in range(rounds):
        got = lax.ppermute(message, "date", date_pairs(chips, 1 << step))
        if step + 1 == rounds:
            break
        body = functools.partial(merge_body, step, rounds)
        if state is None:
            body = lambda a, b, c, *o, body=body: body(a, b, None, c, *o)
        operands = [level, total, got] if state is None else [level, total, state, got]
        level, total, state, message = call(
            body,
            [(plane, f32), (plane, f32), ((4, *plane), f32), ((sizes[step + 1], *plane), f32)],
            *operands,
        )
    (columns,) = call(
        functools.partial(columns_body, chips),
        [((width // 2, 2 * dates * paths), bf16)],
        features,
        columns_got,
        message,
        unread=1,
        flops=1 << 27,
    )
    extra = [x for x in (state, got) if x is not None]

    def tail_kernel(score, level, total, *rest):
        rest = list(rest)
        given = rest.pop(0) if state is not None else None
        arrived = rest.pop(0) if got is not None else None
        tail_body(rounds, score, level, total, given, arrived, *rest)

    (tail,) = call(
        tail_kernel,
        [((2 * dates * half + STAT_ROWS, contracts), f32)],
        score,
        own_level,
        own_total,
        *extra,
    )
    tail_other = lax.ppermute(tail, "date", cores)
    partial_shape = ((chips * rows + STAT_ROWS, contracts), f32)
    pieces = call(
        functools.partial(product_body, -1.0 / paths_total, count),
        [partial_shape] * count,
        columns,
        tail,
        tail_other,
        scratch=[
            pltpu.VMEM((2 * dates, paths, contracts), bf16),
            pltpu.VMEM((chips, count, rows, contracts), f32),
        ],
        flops=2 * dates * paths * width * contracts,
    )
    pieces = [pieces[0]] + [lax.ppermute(m, "path", pairs(count, j)) for j, m in enumerate(pieces) if j]
    pieces = call(
        functools.partial(path_sum_body, count, chips),
        [((rows + STAT_ROWS, contracts), f32)] * chips,
        *pieces,
        scratch=[pltpu.VMEM(*partial_shape)],
    )
    pieces = [pieces[0]] + [lax.ppermute(m, "date", date_pairs(chips, j)) for j, m in enumerate(pieces) if j]
    gradient, bound, spread = call(
        functools.partial(date_sum_body, chips, paths_total),
        [((rows, contracts), f32), ((1, contracts), f32), ((1, contracts), f32)],
        *pieces,
    )
    return gradient, bound.reshape(contracts), spread.reshape(contracts)


def solution(mesh):
    placed = (P("date", "path", None), P("date", "path", None), P(), P("date", None))
    return jax.shard_map(
        shards,
        mesh=mesh,
        in_specs=placed,
        out_specs=(P(("date", "path"), None), P(), P()),
        check_vma=False,
    )
```

time: 249 us -> 50.3 us (0.20)
  waiting for transfers between devices: 203 us -> 27.4 us
  starting transfers between devices: 0.25 us -> 14.6 us
  between operations: 14.3 us -> 0.72 us
  other arithmetic: 11.2 us -> 0 us
  blocking collectives: 9.92 us -> 0 us
  matrix products: 3.47 us -> 0 us
  Pallas kernels: 0 us -> 3.24 us
    psum x1 -> x0, waiting for transfers between devices: 54.1 us -> none  [shards(): total = lax.psum(jnp.sum(shifted, axis=0), 'date')]
    pmax x1 -> x0, waiting for transfers between devices: 54 us -> none  [shards(): peak = lax.pmax(local_peak, 'date')]
    all_gather x2 -> x0, waiting for transfers between devices: 46.1 us -> none  [entering(): pieces = lax.all_gather(value, axis)]
    reduce_scatter x1 -> x0, waiting for transfers between devices: 35.5 us -> none  [shards(): lax.psum_scatter(-product / paths_total, 'date', scatter_dimension=0, til...]
    ppermute x0 -> x11, waiting for transfers between devices: none -> 27.4 us  [the longest x3 12 us: shards(): lax.ppermute(m, 'path', pairs(count, j))]
    ppermute x0 -> x11, starting transfers between devices: none -> 14.6 us  [the longest x2 5.48 us: shards(): got = lax.ppermute(message, 'date', date_pairs(chips, 1 << step))]
    unnamed x7 -> x0, waiting for transfers between devices: 13.6 us -> none
    psum x1 -> x0, blocking collectives: 9.92 us -> none  [shards(): lax.psum((jnp.sum(smoothed, axis=0), jnp.sum(smoothed * smoothed, axis=0)...]
  transfers between devices with their start and end apart: 6 -> 11, of which waited for: 6 -> 9; matrix products, arithmetic and copies ran while one was open for 0% -> 0% of each run, Pallas kernels for 0% -> 2%
where the time goes in v1:
time: 50.3 us; the launch traced here: 50 us
  waiting for transfers between devices  27.4 us (54%)
  starting transfers between devices  14.6 us (29%)
  local copies, waits for them, and re-layouts  4.08 us (8%)
  Pallas kernels  3.24 us (6%)
  between operations  0.72 us (1%)
    ppermute x3, waiting for transfers between devices, shards(): lax.ppermute(m, 'path', pairs(count, j))  12 us
    ppermute x2, waiting for transfers between devices, shards(): got = lax.ppermute(message, 'date', date_pairs(chips, 1 << step))  6.89 us
    ppermute x3, waiting for transfers between devices, shards(): lax.ppermute(m, 'date', date_pairs(chips, j))  6.15 us
    ppermute x2, starting transfers between devices, shards(): got = lax.ppermute(message, 'date', date_pairs(chips, 1 << step))  5.48 us
    ppermute x3, starting transfers between devices, shards(): lax.ppermute(m, 'date', date_pairs(chips, j))  4.52 us
    unnamed x10, local copies, waits for them, and re-layouts  4.08 us
    ppermute x3, starting transfers between devices, shards(): lax.ppermute(m, 'path', pairs(count, j))  3.55 us
    pallas_call x9, Pallas kernels, call(): pl.pallas_call(kernel, out_shape=[jax.ShapeDtypeStruct(*o) for o in outs]...  3.24 us
  transfers between devices with their start and end apart: 11, of which 9 were waited for; matrix products, arithmetic and copies ran while one was open for 0% of the time, Pallas kernels for 2%

profile of v1, /device:TPU:0, one launch (start us, length us, event | category | flops | bytes accessed | tf_op | source)
XLA Modules:
  0.0 50.0 jit_solution(3399542592504925150)
XLA Ops:
  0.6 0.0 copy-start
  0.6 1.2 %copy-done = bf16[2,128,2048]{2,1,0:T(8,128)(2,1)S(1)} copy-done((bf16[2,128,2048]{2,1,0:T(8,128)(2,1)S(1)}, bf16[2,128,2048]{2,1,0:T(8,128)(2,1)}, u32[]{:S(2)}) %copy-start) | copy-done | bytes 1048600
  1.9 0.0 copy-start.2
  1.9 1.2 %copy-done.2 = bf16[2048,256]{1,0:T(8,128)(2,1)S(1)} copy-done((bf16[2048,256]{1,0:T(8,128)(2,1)S(1)}, bf16[2048,256]{1,0:T(8,128)(2,1)}, u32[]{:S(2)}) %copy-start.2) | copy-done | bytes 1048600
  3.1 0.0 copy-start.3
  3.1 0.9 %copy-done.3 = f32[2,128,256]{2,1,0:T(8,128)S(1)} copy-done((f32[2,128,256]{2,1,0:T(8,128)S(1)}, f32[2,128,256]{2,1,0:T(8,128)}, u32[]{:S(2)}) %copy-start.3) | copy-done | bytes 262168
  4.0 0.0 copy-start.4
  4.0 0.7 %copy-done.4 = s32[2,256]{1,0:T(2,128)S(1)} copy-done((s32[2,256]{1,0:T(2,128)S(1)}, s32[2,256]{1,0:T(2,128)}, u32[]{:S(2)}) %copy-start.4) | copy-done | bytes 2072
  4.7 0.0 copy-start.1
  4.7 0.5 shard_map.67
  5.2 0.5 %collective-permute-start = (f32[4,64,256]{2,1,0:T(8,128)S(1)}, f32[4,64,256]{2,1,0:T(8,128)S(1)}, u32[]{:S(2)}, u32[]{:S(2)}) collective-permute-start(f32[4,64,256]{2,1,0:T(8,128)S(1)} %get-tuple-element.23), channel_id=1, source_target_pairs={{0,4},{4,0},{8,12},{12,8},{16,20},{20,16},{24,28},{28,24},{1,5},{5... | collective-permute-start | bytes 786440 | tf_op jit(solution)/shard_map/ppermute | solution.py:242
  5.7 1.2 %collective-permute-done.refs_1_ = f32[4,64,256]{2,1,0:T(8,128)S(1)} collective-permute-done((f32[4,64,256]{2,1,0:T(8,128)S(1)}, f32[4,64,256]{2,1,0:T(8,128)S(1)}, u32[]{:S(2)}, u32[]{:S(2)}) %collective-permute-start) | collective-permute-done | bytes 262176 | tf_op jit(solution)/shard_map/ppermute | solution.py:242
  6.9 0.1 shard_map.68
  7.0 0.0 copy-done.1
  7.0 0.1 shard_map.69
  7.1 0.4 collective-permute-start.1
  7.6 2.7 %collective-permute-start.2 = (f32[2,64,256]{2,1,0:T(8,128)S(1)}, f32[2,64,256]{2,1,0:T(8,128)S(1)}, u32[]{:S(2)}, u32[]{:S(2)}) collective-permute-start(f32[2,64,256]{2,1,0:T(8,128)S(1)} %get-tuple-element.24.refs_1_), channel_id=1, source_target_pairs={{0,8},{4,12},{8,0},{12,4},{16,24},{20,28},{24,16},{28,20},{1,9},{5... | collective-permute-start | bytes 393224 | tf_op jit(solution)/shard_map/ppermute | solution.py:261
  10.3 4.0 %collective-permute-done.2.refs_2_ = f32[2,64,256]{2,1,0:T(8,128)S(1)} collective-permute-done((f32[2,64,256]{2,1,0:T(8,128)S(1)}, f32[2,64,256]{2,1,0:T(8,128)S(1)}, u32[]{:S(2)}, u32[]{:S(2)}) %collective-permute-start.2) | collective-permute-done | bytes 131104 | tf_op jit(solution)/shard_map/ppermute | solution.py:261
  14.3 0.7 %shard_map.70 = (f32[64,256]{1,0:T(8,128)}, f32[64,256]{1,0:T(8,128)}, f32[4,64,256]{2,1,0:T(8,128)S(1)}, f32[1,64,256]{2,1,0:T(8,128)S(1)}) custom-call(f32[64,256]{1,0:T(8,128)S(1)} %get-tuple-element.25.refs_0_.refs_1_, f32[64,256]{1,0:T(8,128)S(1)} %get-tuple-element.26.refs_1_.refs_2_, f32[2,64,256]{2,1,0:T(8,128)S(1)} %collective-permute-done.2.refs_2_), custom_call_target="tpu_custom_call" | custom-call | tf_op jit(solution)/shard_map/pallas_call | solution.py:35
  15.0 2.8 %collective-permute-start.3 = (f32[1,64,256]{2,1,0:T(8,128)S(1)}, f32[1,64,256]{2,1,0:T(8,128)S(1)}, u32[]{:S(2)}, u32[]{:S(2)}) collective-permute-start(f32[1,64,256]{2,1,0:T(8,128)S(1)} %get-tuple-element.27.refs_2_), channel_id=1, source_target_pairs={{0,16},{4,20},{8,24},{12,28},{16,0},{20,4},{24,8},{28,12},{1,17},{... | collective-permute-start | bytes 196616 | tf_op jit(solution)/shard_map/ppermute | solution.py:261
  17.8 2.9 %collective-permute-done.3.refs_4_ = f32[1,64,256]{2,1,0:T(8,128)S(1)} collective-permute-done((f32[1,64,256]{2,1,0:T(8,128)S(1)}, f32[1,64,256]{2,1,0:T(8,128)S(1)}, u32[]{:S(2)}, u32[]{:S(2)}) %collective-permute-start.3) | collective-permute-done | bytes 65568 | tf_op jit(solution)/shard_map/ppermute | solution.py:261
  20.7 0.2 shard_map.72.refs_1_
  20.9 0.1 collective-permute-start.4
  20.9 0.0 collective-permute-done.1.refs_1_
  20.9 0.3 shard_map.71.refs_0_
  21.3 1.2 %collective-permute-done.4.refs_2_ = f32[264,256]{1,0:T(8,128)S(1)} collective-permute-done((f32[264,256]{1,0:T(8,128)S(1)}, f32[264,256]{1,0:T(8,128)S(1)}, u32[]{:S(2)}, u32[]{:S(2)}) %collective-permute-start.4) | collective-permute-done | bytes 270368 | tf_op jit(solution)/shard_map/ppermute | solution.py:298
  22.5 0.5 %shard_map.73 = (f32[264,256]{1,0:T(8,128)S(1)}, f32[264,256]{1,0:T(8,128)S(1)}, f32[264,256]{1,0:T(8,128)S(1)}, f32[264,256]{1,0:T(8,128)S(1)}) custom-call(bf16[1024,512]{1,0:T(8,128)(2,1)S(1)} %shard_map.71.refs_0_, f32[264,256]{1,0:T(8,128)S(1)} %shard_map.72.refs_1_, f32[264,256]{1,0:T(8,128)S(1)} %collective-permute-done.4.refs_2_), custom_call_target="tpu_custom_call" | custom-call | flops 268435456 | tf_op jit(solution)/shard_map/pallas_call | solution.py:35
  23.0 1.6 %collective-permute-start.5 = (f32[264,256]{1,0:T(8,128)S(1)}, f32[264,256]{1,0:T(8,128)S(1)}, u32[]{:S(2)}, u32[]{:S(2)}) collective-permute-start(f32[264,256]{1,0:T(8,128)S(1)} %get-tuple-element.31), channel_id=1, source_target_pairs={{0,1},{1,0},{2,3},{3,2},{4,5},{5,4},{6,7},{7,6},{8,9},{9,8},{10,11... | collective-permute-start | bytes 811016 | tf_op jit(solution)/shard_map/ppermute | solution.py:312
  24.6 1.5 %collective-permute-start.6 = (f32[264,256]{1,0:T(8,128)S(1)}, f32[264,256]{1,0:T(8,128)S(1)}, u32[]{:S(2)}, u32[]{:S(2)}) collective-permute-start(f32[264,256]{1,0:T(8,128)S(1)} %get-tuple-element.32), channel_id=1, source_target_pairs={{0,2},{1,3},{2,0},{3,1},{4,6},{5,7},{6,4},{7,5},{8,10},{9,11},{10,... | collective-permute-start | bytes 811016 | tf_op jit(solution)/shard_map/ppermute | solution.py:312
  26.1 0.5 collective-permute-start.7
  26.6 5.8 %collective-permute-done.5.refs_1_ = f32[264,256]{1,0:T(8,128)S(1)} collective-permute-done((f32[264,256]{1,0:T(8,128)S(1)}, f32[264,256]{1,0:T(8,128)S(1)}, u32[]{:S(2)}, u32[]{:S(2)}) %collective-permute-start.5) | collective-permute-done | bytes 270368 | tf_op jit(solution)/shard_map/ppermute | solution.py:312
  32.4 6.2 %collective-permute-done.6.refs_2_ = f32[264,256]{1,0:T(8,128)S(1)} collective-permute-done((f32[264,256]{1,0:T(8,128)S(1)}, f32[264,256]{1,0:T(8,128)S(1)}, u32[]{:S(2)}, u32[]{:S(2)}) %collective-permute-start.6) | collective-permute-done | bytes 270368 | tf_op jit(solution)/shard_map/ppermute | solution.py:312
  38.6 0.0 collective-permute-done.7.refs_3_
  38.6 0.1 shard_map.74
  38.7 1.3 %collective-permute-start.8 = (f32[72,256]{1,0:T(8,128)S(1)}, f32[72,256]{1,0:T(8,128)S(1)}, u32[]{:S(2)}, u32[]{:S(2)}) collective-permute-start(f32[72,256]{1,0:T(8,128)S(1)} %get-tuple-element.35), channel_id=1, source_target_pairs={{0,8},{4,12},{8,0},{12,4},{16,24},{20,28},{24,16},{28,20},{1,9},{5... | collective-permute-start | bytes 221192 | tf_op jit(solution)/shard_map/ppermute | solution.py:319
  40.1 3.2 %collective-permute-start.9 = (f32[72,256]{1,0:T(8,128)S(1)}, f32[72,256]{1,0:T(8,128)S(1)}, u32[]{:S(2)}, u32[]{:S(2)}) collective-permute-start(f32[72,256]{1,0:T(8,128)S(1)} %get-tuple-element.36), channel_id=1, source_target_pairs={{0,16},{4,20},{8,24},{12,28},{16,0},{20,4},{24,8},{28,12},{1,17},{... | collective-permute-start | bytes 221192 | tf_op jit(solution)/shard_map/ppermute | solution.py:319
  43.2 0.0 collective-permute-start.10
  43.2 0.5 %collective-permute-done.8.refs_1_ = f32[72,256]{1,0:T(8,128)S(1)} collective-permute-done((f32[72,256]{1,0:T(8,128)S(1)}, f32[72,256]{1,0:T(8,128)S(1)}, u32[]{:S(2)}, u32[]{:S(2)}) %collective-permute-start.8) | collective-permute-done | bytes 73760 | tf_op jit(solution)/shard_map/ppermute | solution.py:319
  43.7 3.9 %collective-permute-done.9.refs_2_ = f32[72,256]{1,0:T(8,128)S(1)} collective-permute-done((f32[72,256]{1,0:T(8,128)S(1)}, f32[72,256]{1,0:T(8,128)S(1)}, u32[]{:S(2)}, u32[]{:S(2)}) %collective-permute-start.9) | collective-permute-done | bytes 73760 | tf_op jit(solution)/shard_map/ppermute | solution.py:319
  47.6 1.7 %collective-permute-done.10.refs_3_ = f32[72,256]{1,0:T(8,128)S(1)} collective-permute-done((f32[72,256]{1,0:T(8,128)S(1)}, f32[72,256]{1,0:T(8,128)S(1)}, u32[]{:S(2)}, u32[]{:S(2)}) %collective-permute-start.10) | collective-permute-done | bytes 73760 | tf_op jit(solution)/shard_map/ppermute | solution.py:319
  49.4 0.7 %shard_map.75 = (f32[64,256]{1,0:T(8,128)}, f32[1,256]{1,0:T(1,128)}, f32[1,256]{1,0:T(1,128)}) custom-call(f32[72,256]{1,0:T(8,128)S(1)} %get-tuple-element.34.refs_0_, f32[72,256]{1,0:T(8,128)S(1)} %collective-permute-done.8.refs_1_, f32[72,256]{1,0:T(8,128)S(1)} %collective-permute-done.9.refs_2_, f32[72,256]{1,0:T(8,128)S(1)} %collective-permute-done.10.refs_3_), custom_call_target="tpu_custom_call" | custom-call | tf_op jit(solution)/shard_map/pallas_call | solution.py:35
Async XLA Ops:
  0.6 1.2 %copy-start = (bf16[2,128,2048]{2,1,0:T(8,128)(2,1)S(1)}, bf16[2,128,2048]{2,1,0:T(8,128)(2,1)}, u32[]{:S(2)}) copy-start(bf16[2,128,2048]{2,1,0:T(8,128)(2,1)} %refs_0_.5) | copy-start | bytes 3145732
  1.9 1.2 %copy-start.2 = (bf16[2048,256]{1,0:T(8,128)(2,1)S(1)}, bf16[2048,256]{1,0:T(8,128)(2,1)}, u32[]{:S(2)}) copy-start(bf16[2048,256]{1,0:T(8,128)(2,1)} %refs_1_.1) | copy-start | bytes 3145732
  3.1 0.9 %copy-start.3 = (f32[2,128,256]{2,1,0:T(8,128)S(1)}, f32[2,128,256]{2,1,0:T(8,128)}, u32[]{:S(2)}) copy-start(f32[2,128,256]{2,1,0:T(8,128)} %refs_2_.1) | copy-start | bytes 786436
  4.0 0.7 %copy-start.4 = (s32[2,256]{1,0:T(2,128)S(1)}, s32[2,256]{1,0:T(2,128)}, u32[]{:S(2)}) copy-start(s32[2,256]{1,0:T(2,128)} %refs_3_.1) | copy-start | bytes 6148
  4.7 2.3 %copy-start.1 = (bf16[2,128,2048]{2,1,0:T(8,128)(2,1)S(1)}, bf16[2,128,2048]{2,1,0:T(8,128)(2,1)}, u32[]{:S(2)}) copy-start(bf16[2,128,2048]{2,1,0:T(8,128)(2,1)} %refs_0_.5) | copy-start | bytes 3145732
  5.2 1.7 %collective-permute-start = (f32[4,64,256]{2,1,0:T(8,128)S(1)}, f32[4,64,256]{2,1,0:T(8,128)S(1)}, u32[]{:S(2)}, u32[]{:S(2)}) collective-permute-start(f32[4,64,256]{2,1,0:T(8,128)S(1)} %get-tuple-element.23), channel_id=1, source_target_pairs={{0,4},{4,0},{8,12},{12,8},{16,20},{20,16},{24,28},{28,24},{1,5},{5... | collective-permute-start | bytes 786440 | tf_op jit(solution)/shard_map/ppermute | solution.py:242
  7.1 13.8 %collective-permute-start.1 = (f32[2,128,1024]{2,1,0:T(8,128)S(1)}, f32[2,128,1024]{2,1,0:T(8,128)S(1)}, u32[]{:S(2)}, u32[]{:S(2)}) collective-permute-start(f32[2,128,1024]{2,1,0:T(8,128)S(1)} %shard_map.69), channel_id=1, source_target_pairs={{0,4},{4,0},{8,12},{12,8},{16,20},{20,16},{24,28},{28,24},{1,5},{5... | collective-permute-start | bytes 3145736 | tf_op jit(solution)/shard_map/ppermute | solution.py:259
  7.6 6.7 %collective-permute-start.2 = (f32[2,64,256]{2,1,0:T(8,128)S(1)}, f32[2,64,256]{2,1,0:T(8,128)S(1)}, u32[]{:S(2)}, u32[]{:S(2)}) collective-permute-start(f32[2,64,256]{2,1,0:T(8,128)S(1)} %get-tuple-element.24.refs_1_), channel_id=1, source_target_pairs={{0,8},{4,12},{8,0},{12,4},{16,24},{20,28},{24,16},{28,20},{1,9},{5... | collective-permute-start | bytes 393224 | tf_op jit(solution)/shard_map/ppermute | solution.py:261
  15.0 5.6 %collective-permute-start.3 = (f32[1,64,256]{2,1,0:T(8,128)S(1)}, f32[1,64,256]{2,1,0:T(8,128)S(1)}, u32[]{:S(2)}, u32[]{:S(2)}) collective-permute-start(f32[1,64,256]{2,1,0:T(8,128)S(1)} %get-tuple-element.27.refs_2_), channel_id=1, source_target_pairs={{0,16},{4,20},{8,24},{12,28},{16,0},{20,4},{24,8},{28,12},{1,17},{... | collective-permute-start | bytes 196616 | tf_op jit(solution)/shard_map/ppermute | solution.py:261
  20.9 1.6 %collective-permute-start.4 = (f32[264,256]{1,0:T(8,128)S(1)}, f32[264,256]{1,0:T(8,128)S(1)}, u32[]{:S(2)}, u32[]{:S(2)}) collective-permute-start(f32[264,256]{1,0:T(8,128)S(1)} %shard_map.72.refs_1_), channel_id=1, source_target_pairs={{0,4},{4,0},{8,12},{12,8},{16,20},{20,16},{24,28},{28,24},{1,5},{5... | collective-permute-start | bytes 811016 | tf_op jit(solution)/shard_map/ppermute | solution.py:298
  23.0 9.4 %collective-permute-start.5 = (f32[264,256]{1,0:T(8,128)S(1)}, f32[264,256]{1,0:T(8,128)S(1)}, u32[]{:S(2)}, u32[]{:S(2)}) collective-permute-start(f32[264,256]{1,0:T(8,128)S(1)} %get-tuple-element.31), channel_id=1, source_target_pairs={{0,1},{1,0},{2,3},{3,2},{4,5},{5,4},{6,7},{7,6},{8,9},{9,8},{10,11... | collective-permute-start | bytes 811016 | tf_op jit(solution)/shard_map/ppermute | solution.py:312
  24.6 14.0 %collective-permute-start.6 = (f32[264,256]{1,0:T(8,128)S(1)}, f32[264,256]{1,0:T(8,128)S(1)}, u32[]{:S(2)}, u32[]{:S(2)}) collective-permute-start(f32[264,256]{1,0:T(8,128)S(1)} %get-tuple-element.32), channel_id=1, source_target_pairs={{0,2},{1,3},{2,0},{3,1},{4,6},{5,7},{6,4},{7,5},{8,10},{9,11},{10,... | collective-permute-start | bytes 811016 | tf_op jit(solution)/shard_map/ppermute | solution.py:312
  26.1 12.5 %collective-permute-start.7 = (f32[264,256]{1,0:T(8,128)S(1)}, f32[264,256]{1,0:T(8,128)S(1)}, u32[]{:S(2)}, u32[]{:S(2)}) collective-permute-start(f32[264,256]{1,0:T(8,128)S(1)} %get-tuple-element.33), channel_id=1, source_target_pairs={{0,3},{1,2},{2,1},{3,0},{4,7},{5,6},{6,5},{7,4},{8,11},{9,10},{10,... | collective-permute-start | bytes 811016 | tf_op jit(solution)/shard_map/ppermute | solution.py:312
  38.7 5.0 %collective-permute-start.8 = (f32[72,256]{1,0:T(8,128)S(1)}, f32[72,256]{1,0:T(8,128)S(1)}, u32[]{:S(2)}, u32[]{:S(2)}) collective-permute-start(f32[72,256]{1,0:T(8,128)S(1)} %get-tuple-element.35), channel_id=1, source_target_pairs={{0,8},{4,12},{8,0},{12,4},{16,24},{20,28},{24,16},{28,20},{1,9},{5... | collective-permute-start | bytes 221192 | tf_op jit(solution)/shard_map/ppermute | solution.py:319
  40.1 7.6 %collective-permute-start.9 = (f32[72,256]{1,0:T(8,128)S(1)}, f32[72,256]{1,0:T(8,128)S(1)}, u32[]{:S(2)}, u32[]{:S(2)}) collective-permute-start(f32[72,256]{1,0:T(8,128)S(1)} %get-tuple-element.36), channel_id=1, source_target_pairs={{0,16},{4,20},{8,24},{12,28},{16,0},{20,4},{24,8},{28,12},{1,17},{... | collective-permute-start | bytes 221192 | tf_op jit(solution)/shard_map/ppermute | solution.py:319
  43.2 6.2 %collective-permute-start.10 = (f32[72,256]{1,0:T(8,128)S(1)}, f32[72,256]{1,0:T(8,128)S(1)}, u32[]{:S(2)}, u32[]{:S(2)}) collective-permute-start(f32[72,256]{1,0:T(8,128)S(1)} %get-tuple-element.37), channel_id=1, source_target_pairs={{0,24},{4,28},{8,16},{12,20},{16,8},{20,12},{24,0},{28,4},{1,25},{... | collective-permute-start | bytes 221192 | tf_op jit(solution)/shard_map/ppermute | solution.py:319

commit v2 on v1

--- a/solution.py
+++ b/solution.py
@@ -11,6 +11,7 @@
 TEMP = 0.25
 NEG = -1e30
 STAT_ROWS = 8
+PIECES = 4
 VMEM_LIMIT = 16 << 20
 f32 = jnp.float32
 bf16 = jnp.bfloat16
@@ -24,10 +25,12 @@
     return lax.axis_index("date") // 2
 
 
-def call(body, outs, *operands, scratch=(), flops=0, unread=0):
-    whole = pl.BlockSpec(memory_space=pltpu.VMEM)
+def call(body, outs, *operands, scratch=(), flops=0, unread=0, place=pltpu.VMEM):
+    given, whole = pl.BlockSpec(memory_space=place), pl.BlockSpec(memory_space=pltpu.VMEM)
     anywhere = pl.BlockSpec(memory_space=pl.ANY)
     read = len(operands) - unread
+    if place is pltpu.HBM:
+        operands = [pltpu.with_memory_space_constraint(x, place) for x in operands]
 
     def kernel(*refs):
         body(*refs[:read], *refs[read + unread :])
@@ -35,7 +38,7 @@
     return pl.pallas_call(
         kernel,
         out_shape=[jax.ShapeDtypeStruct(*o) for o in outs],
-        in_specs=[whole] * read + [anywhere] * unread,
+        in_specs=[given] * read + [anywhere] * unread,
         out_specs=[whole] * len(outs),
         scratch_shapes=list(scratch),
         compiler_params=pltpu.CompilerParams(vmem_limit_bytes=VMEM_LIMIT),
@@ -47,18 +50,34 @@
     return jnp.maximum(a, b) + jnp.log(1.0 + jnp.exp(-jnp.abs(a - b)))
 
 
-def increments_body(features, coefficients, payoff, exercise, keep, send, inc):
+def increments_body(features, coefficients, payoff, exercise, keep, send, held, inc, weights, pay, may, sems):
     dates, paths, width = features.shape
-    half = paths // 2
-    product = jnp.dot(features[...].reshape(dates * paths, width), coefficients[...], preferred_element_type=f32)
-    inc[...] = (INVERSE_TEMP * product).reshape(inc.shape)
+    half, step = paths // 2, width // PIECES
+    copies = []
+    for i in range(PIECES):
+        at = slice(i * step, (i + 1) * step)
+        copies.append(pltpu.make_async_copy(features.at[:, :, at], held.at[:, :, at], sems.at[2 * i]))
+        copies.append(pltpu.make_async_copy(coefficients.at[at, :], weights.at[at, :], sems.at[2 * i + 1]))
+    copies.append(pltpu.make_async_copy(payoff, pay, sems.at[2 * PIECES]))
+    copies.append(pltpu.make_async_copy(exercise, may, sems.at[2 * PIECES + 1]))
+    for c in copies:
+        c.start()
+    for i in range(PIECES):
+        at = slice(i * step, (i + 1) * step)
+        copies[2 * i].wait()
+        copies[2 * i + 1].wait()
+        left = held[:, :, at].reshape(dates * paths, step)
+        part = jnp.dot(left, weights[at, :], preferred_element_type=f32).reshape(inc.shape)
+        inc[...] = part if i == 0 else inc[...] + part
+    copies[-2].wait()
+    copies[-1].wait()
     mine = pl.multiple_of(core_of() * half, half)
     theirs = pl.multiple_of((1 - core_of()) * half, half)
     for out, at in ((keep, mine), (send, theirs)):
-        out[0:dates] = inc[:, pl.ds(at, half)]
+        out[0:dates] = INVERSE_TEMP * inc[:, pl.ds(at, half)]
         for d in range(dates):
-            allowed = exercise[d : d + 1, :] > 0
-            out[dates + d] = jnp.where(allowed, INVERSE_TEMP * payoff[d, pl.ds(at, half)], NEG)
+            allowed = may[d : d + 1, :] > 0
+            out[dates + d] = jnp.where(allowed, INVERSE_TEMP * pay[d, pl.ds(at, half)], NEG)
 
 
 def message_of(level, total, left, last):
@@ -90,7 +109,7 @@
         message[i] = m
 
 
-def merge_body(step, rounds, level, total, state, got, level2, total2, state2, message):
+def merge_body(step, rounds, level, total, state, got, state2, message, *group):
     left = (chip_of() >> step) % 2 == 0
     lev, tot, other_lev, other_tot = level[...], total[...], got[0], got[1]
     if state is None:
@@ -106,8 +125,8 @@
     second_lev = jnp.where(left, other_lev, lev)
     lev2 = log_add(first_lev, second_lev - first_tot)
     tot2 = tot + other_tot
-    level2[...] = lev2
-    total2[...] = tot2
+    for out, value in zip(group, (lev2, tot2)):
+        out[...] = value
     next_left = (chip_of() >> (step + 1)) % 2 == 0
     for i, m in enumerate(message_of(lev2, tot2, next_left, step + 2 == rounds)):
         message[i] = m
@@ -229,15 +248,22 @@
     cores = [(2 * z + c, 2 * z + 1 - c) for z in range(chips) for c in range(2)]
     plane = (half, contracts)
 
-    keep, send = call(
+    keep, send, held = call(
         increments_body,
-        [((2 * dates, *plane), f32)] * 2,
+        [((2 * dates, *plane), f32), ((2 * dates, *plane), f32), (features.shape, bf16)],
         features,
         coefficients,
         payoff,
         exercise,
-        scratch=[pltpu.VMEM((dates, paths, contracts), f32)],
+        scratch=[
+            pltpu.VMEM((dates, paths, contracts), f32),
+            pltpu.VMEM(coefficients.shape, bf16),
+            pltpu.VMEM(payoff.shape, f32),
+            pltpu.VMEM(exercise.shape, jnp.int32),
+            pltpu.SemaphoreType.DMA((2 * PIECES + 2,)),
+        ],
         flops=2 * dates * paths * width * contracts,
+        place=pltpu.HBM,
     )
     other = lax.ppermute(send, "date", cores)
     sizes = [1 if step + 1 == rounds else 2 for step in range(rounds)] or [2]
@@ -250,7 +276,7 @@
     (columns_send,) = call(
         functools.partial(halves_body, chips),
         [((dates, paths, width // 2), f32)],
-        features,
+        held,
         message,
         unread=1,
         flops=1 << 26,
@@ -265,15 +291,13 @@
         if state is None:
             body = lambda a, b, c, *o, body=body: body(a, b, None, c, *o)
         operands = [level, total, got] if state is None else [level, total, state, got]
-        level, total, state, message = call(
-            body,
-            [(plane, f32), (plane, f32), ((4, *plane), f32), ((sizes[step + 1], *plane), f32)],
-            *operands,
-        )
+        group = [(plane, f32)] * (0 if step + 2 == rounds else 2)
+        state, message, *group = call(body, [((4, *plane), f32), ((sizes[step + 1], *plane), f32)] + group, *operands)
+        level, total = group or (level, total)
     (columns,) = call(
         functools.partial(columns_body, chips),
         [((width // 2, 2 * dates * paths), bf16)],
-        features,
+        held,
         columns_got,
         message,
         unread=1,

time: 50.3 us -> 47.2 us (0.938)
  local copies, waits for them, and re-layouts: 4.08 us -> 0 us
  Pallas kernels: 3.24 us -> 4.25 us
    unnamed x10 -> x0, local copies, waits for them, and re-layouts: 4.08 us -> none
    pallas_call x9, Pallas kernels: 3.24 us -> 4.25 us  [call(): pl.pallas_call(kernel, out_shape=[jax.ShapeDtypeStruct(*o) for o in outs]...]
  transfers between devices with their start and end apart: 11 -> 11, of which waited for: 9 -> 9; matrix products, arithmetic and copies ran while one was open for 0% -> 0% of each run, Pallas kernels for 2% -> 1%
where the time goes in v2:
time: 47.2 us; the launch traced here: 47 us
  waiting for transfers between devices  27.4 us (58%)
  starting transfers between devices  14.6 us (31%)
  Pallas kernels  4.25 us (9%)
  between operations  0.7 us (1%)
    ppermute x3, waiting for transfers between devices, shards(): lax.ppermute(m, 'path', pairs(count, j))  12 us
    ppermute x2, waiting for transfers between devices, shards(): got = lax.ppermute(message, 'date', date_pairs(chips, 1 << step))  6.89 us
    ppermute x3, waiting for transfers between devices, shards(): lax.ppermute(m, 'date', date_pairs(chips, j))  6.15 us
    ppermute x2, starting transfers between devices, shards(): got = lax.ppermute(message, 'date', date_pairs(chips, 1 << step))  5.54 us
    ppermute x3, starting transfers between devices, shards(): lax.ppermute(m, 'date', date_pairs(chips, j))  4.52 us
    pallas_call x9, Pallas kernels, call(): pl.pallas_call(kernel, out_shape=[jax.ShapeDtypeStruct(*o) for o in outs]...  4.25 us
    ppermute x3, starting transfers between devices, shards(): lax.ppermute(m, 'path', pairs(count, j))  3.55 us
    ppermute x1, waiting for transfers between devices, shards(): tail_other = lax.ppermute(tail, 'date', cores)  1.18 us
  transfers between devices with their start and end apart: 11, of which 9 were waited for; matrix products, arithmetic and copies ran while one was open for 0% of the time, Pallas kernels for 1%

profile of v2, /device:TPU:0, one launch (start us, length us, event | category | flops | bytes accessed | tf_op | source)
XLA Modules:
  0.0 47.0 jit_solution(5135589228099291601)
XLA Ops:
  0.6 2.1 %shard_map.67 = (f32[4,64,256]{2,1,0:T(8,128)S(1)}, f32[4,64,256]{2,1,0:T(8,128)S(1)}, bf16[2,128,2048]{2,1,0:T(8,128)(2,1)S(1)}) custom-call(bf16[2,128,2048]{2,1,0:T(8,128)(2,1)} %refs_0_.1, bf16[2048,256]{1,0:T(8,128)(2,1)} %refs_1_.1, f32[2,128,256]{2,1,0:T(8,128)} %refs_2_.1, s32[2,256]{1,0:T(2,128)} %refs_3_.1), custom_call_target="tpu_custom_call" | custom-call | flops 268435456 | tf_op jit(solution)/shard_map/pallas_call | solution.py:38
  2.7 0.5 %collective-permute-start = (f32[4,64,256]{2,1,0:T(8,128)S(1)}, f32[4,64,256]{2,1,0:T(8,128)S(1)}, u32[]{:S(2)}, u32[]{:S(2)}) collective-permute-start(f32[4,64,256]{2,1,0:T(8,128)S(1)} %get-tuple-element.25), channel_id=1, source_target_pairs={{0,4},{4,0},{8,12},{12,8},{16,20},{20,16},{24,28},{28,24},{1,5},{5... | collective-permute-start | bytes 786440 | tf_op jit(solution)/shard_map/ppermute | solution.py:268
  3.2 1.2 %collective-permute-done.refs_1_ = f32[4,64,256]{2,1,0:T(8,128)S(1)} collective-permute-done((f32[4,64,256]{2,1,0:T(8,128)S(1)}, f32[4,64,256]{2,1,0:T(8,128)S(1)}, u32[]{:S(2)}, u32[]{:S(2)}) %collective-permute-start) | collective-permute-done | bytes 262176 | tf_op jit(solution)/shard_map/ppermute | solution.py:268
  4.4 0.1 shard_map.68
  4.5 0.1 shard_map.69
  4.7 0.4 collective-permute-start.1
  5.1 2.7 %collective-permute-start.2 = (f32[2,64,256]{2,1,0:T(8,128)S(1)}, f32[2,64,256]{2,1,0:T(8,128)S(1)}, u32[]{:S(2)}, u32[]{:S(2)}) collective-permute-start(f32[2,64,256]{2,1,0:T(8,128)S(1)} %get-tuple-element.26.refs_1_), channel_id=1, source_target_pairs={{0,8},{4,12},{8,0},{12,4},{16,24},{20,28},{24,16},{28,20},{1,9},{5... | collective-permute-start | bytes 393224 | tf_op jit(solution)/shard_map/ppermute | solution.py:287
  7.8 4.0 %collective-permute-done.2.refs_2_ = f32[2,64,256]{2,1,0:T(8,128)S(1)} collective-permute-done((f32[2,64,256]{2,1,0:T(8,128)S(1)}, f32[2,64,256]{2,1,0:T(8,128)S(1)}, u32[]{:S(2)}, u32[]{:S(2)}) %collective-permute-start.2) | collective-permute-done | bytes 131104 | tf_op jit(solution)/shard_map/ppermute | solution.py:287
  11.8 0.1 shard_map.70
  12.0 2.8 %collective-permute-start.3 = (f32[1,64,256]{2,1,0:T(8,128)S(1)}, f32[1,64,256]{2,1,0:T(8,128)S(1)}, u32[]{:S(2)}, u32[]{:S(2)}) collective-permute-start(f32[1,64,256]{2,1,0:T(8,128)S(1)} %get-tuple-element.29.refs_2_), channel_id=1, source_target_pairs={{0,16},{4,20},{8,24},{12,28},{16,0},{20,4},{24,8},{28,12},{1,17},{... | collective-permute-start | bytes 196616 | tf_op jit(solution)/shard_map/ppermute | solution.py:287
  14.8 2.9 %collective-permute-done.3.refs_4_ = f32[1,64,256]{2,1,0:T(8,128)S(1)} collective-permute-done((f32[1,64,256]{2,1,0:T(8,128)S(1)}, f32[1,64,256]{2,1,0:T(8,128)S(1)}, u32[]{:S(2)}, u32[]{:S(2)}) %collective-permute-start.3) | collective-permute-done | bytes 65568 | tf_op jit(solution)/shard_map/ppermute | solution.py:287
  17.7 0.2 shard_map.72.refs_1_
  17.8 0.1 collective-permute-start.4
  17.9 0.0 collective-permute-done.1.refs_1_
  17.9 0.3 shard_map.71.refs_0_
  18.3 1.2 %collective-permute-done.4.refs_2_ = f32[264,256]{1,0:T(8,128)S(1)} collective-permute-done((f32[264,256]{1,0:T(8,128)S(1)}, f32[264,256]{1,0:T(8,128)S(1)}, u32[]{:S(2)}, u32[]{:S(2)}) %collective-permute-start.4) | collective-permute-done | bytes 270368 | tf_op jit(solution)/shard_map/ppermute | solution.py:322
  19.5 0.5 %shard_map.73 = (f32[264,256]{1,0:T(8,128)S(1)}, f32[264,256]{1,0:T(8,128)S(1)}, f32[264,256]{1,0:T(8,128)S(1)}, f32[264,256]{1,0:T(8,128)S(1)}) custom-call(bf16[1024,512]{1,0:T(8,128)(2,1)S(1)} %shard_map.71.refs_0_, f32[264,256]{1,0:T(8,128)S(1)} %shard_map.72.refs_1_, f32[264,256]{1,0:T(8,128)S(1)} %collective-permute-done.4.refs_2_), custom_call_target="tpu_custom_call" | custom-call | flops 268435456 | tf_op jit(solution)/shard_map/pallas_call | solution.py:38
  20.0 1.6 %collective-permute-start.5 = (f32[264,256]{1,0:T(8,128)S(1)}, f32[264,256]{1,0:T(8,128)S(1)}, u32[]{:S(2)}, u32[]{:S(2)}) collective-permute-start(f32[264,256]{1,0:T(8,128)S(1)} %get-tuple-element.33), channel_id=1, source_target_pairs={{0,1},{1,0},{2,3},{3,2},{4,5},{5,4},{6,7},{7,6},{8,9},{9,8},{10,11... | collective-permute-start | bytes 811016 | tf_op jit(solution)/shard_map/ppermute | solution.py:336
  21.6 1.5 %collective-permute-start.6 = (f32[264,256]{1,0:T(8,128)S(1)}, f32[264,256]{1,0:T(8,128)S(1)}, u32[]{:S(2)}, u32[]{:S(2)}) collective-permute-start(f32[264,256]{1,0:T(8,128)S(1)} %get-tuple-element.34), channel_id=1, source_target_pairs={{0,2},{1,3},{2,0},{3,1},{4,6},{5,7},{6,4},{7,5},{8,10},{9,11},{10,... | collective-permute-start | bytes 811016 | tf_op jit(solution)/shard_map/ppermute | solution.py:336
  23.1 0.5 %collective-permute-start.7 = (f32[264,256]{1,0:T(8,128)S(1)}, f32[264,256]{1,0:T(8,128)S(1)}, u32[]{:S(2)}, u32[]{:S(2)}) collective-permute-start(f32[264,256]{1,0:T(8,128)S(1)} %get-tuple-element.35), channel_id=1, source_target_pairs={{0,3},{1,2},{2,1},{3,0},{4,7},{5,6},{6,5},{7,4},{8,11},{9,10},{10,... | collective-permute-start | bytes 811016 | tf_op jit(solution)/shard_map/ppermute | solution.py:336
  23.6 5.8 %collective-permute-done.5.refs_1_ = f32[264,256]{1,0:T(8,128)S(1)} collective-permute-done((f32[264,256]{1,0:T(8,128)S(1)}, f32[264,256]{1,0:T(8,128)S(1)}, u32[]{:S(2)}, u32[]{:S(2)}) %collective-permute-start.5) | collective-permute-done | bytes 270368 | tf_op jit(solution)/shard_map/ppermute | solution.py:336
  29.4 6.2 %collective-permute-done.6.refs_2_ = f32[264,256]{1,0:T(8,128)S(1)} collective-permute-done((f32[264,256]{1,0:T(8,128)S(1)}, f32[264,256]{1,0:T(8,128)S(1)}, u32[]{:S(2)}, u32[]{:S(2)}) %collective-permute-start.6) | collective-permute-done | bytes 270368 | tf_op jit(solution)/shard_map/ppermute | solution.py:336
  35.6 0.0 collective-permute-done.7.refs_3_
  35.6 0.1 shard_map.74
  35.7 1.3 %collective-permute-start.8 = (f32[72,256]{1,0:T(8,128)S(1)}, f32[72,256]{1,0:T(8,128)S(1)}, u32[]{:S(2)}, u32[]{:S(2)}) collective-permute-start(f32[72,256]{1,0:T(8,128)S(1)} %get-tuple-element.37), channel_id=1, source_target_pairs={{0,8},{4,12},{8,0},{12,4},{16,24},{20,28},{24,16},{28,20},{1,9},{5... | collective-permute-start | bytes 221192 | tf_op jit(solution)/shard_map/ppermute | solution.py:343
  37.0 3.2 %collective-permute-start.9 = (f32[72,256]{1,0:T(8,128)S(1)}, f32[72,256]{1,0:T(8,128)S(1)}, u32[]{:S(2)}, u32[]{:S(2)}) collective-permute-start(f32[72,256]{1,0:T(8,128)S(1)} %get-tuple-element.38), channel_id=1, source_target_pairs={{0,16},{4,20},{8,24},{12,28},{16,0},{20,4},{24,8},{28,12},{1,17},{... | collective-permute-start | bytes 221192 | tf_op jit(solution)/shard_map/ppermute | solution.py:343
  40.2 0.0 collective-permute-start.10
  40.2 0.5 %collective-permute-done.8.refs_1_ = f32[72,256]{1,0:T(8,128)S(1)} collective-permute-done((f32[72,256]{1,0:T(8,128)S(1)}, f32[72,256]{1,0:T(8,128)S(1)}, u32[]{:S(2)}, u32[]{:S(2)}) %collective-permute-start.8) | collective-permute-done | bytes 73760 | tf_op jit(solution)/shard_map/ppermute | solution.py:343
  40.7 3.9 %collective-permute-done.9.refs_2_ = f32[72,256]{1,0:T(8,128)S(1)} collective-permute-done((f32[72,256]{1,0:T(8,128)S(1)}, f32[72,256]{1,0:T(8,128)S(1)}, u32[]{:S(2)}, u32[]{:S(2)}) %collective-permute-start.9) | collective-permute-done | bytes 73760 | tf_op jit(solution)/shard_map/ppermute | solution.py:343
  44.6 1.8 %collective-permute-done.10.refs_3_ = f32[72,256]{1,0:T(8,128)S(1)} collective-permute-done((f32[72,256]{1,0:T(8,128)S(1)}, f32[72,256]{1,0:T(8,128)S(1)}, u32[]{:S(2)}, u32[]{:S(2)}) %collective-permute-start.10) | collective-permute-done | bytes 73760 | tf_op jit(solution)/shard_map/ppermute | solution.py:343
  46.4 0.7 %shard_map.75 = (f32[64,256]{1,0:T(8,128)}, f32[1,256]{1,0:T(1,128)}, f32[1,256]{1,0:T(1,128)}) custom-call(f32[72,256]{1,0:T(8,128)S(1)} %get-tuple-element.36.refs_0_, f32[72,256]{1,0:T(8,128)S(1)} %collective-permute-done.8.refs_1_, f32[72,256]{1,0:T(8,128)S(1)} %collective-permute-done.9.refs_2_, f32[72,256]{1,0:T(8,128)S(1)} %collective-permute-done.10.refs_3_), custom_call_target="tpu_custom_call" | custom-call | tf_op jit(solution)/shard_map/pallas_call | solution.py:38
Async XLA Ops:
  2.7 1.7 %collective-permute-start = (f32[4,64,256]{2,1,0:T(8,128)S(1)}, f32[4,64,256]{2,1,0:T(8,128)S(1)}, u32[]{:S(2)}, u32[]{:S(2)}) collective-permute-start(f32[4,64,256]{2,1,0:T(8,128)S(1)} %get-tuple-element.25), channel_id=1, source_target_pairs={{0,4},{4,0},{8,12},{12,8},{16,20},{20,16},{24,28},{28,24},{1,5},{5... | collective-permute-start | bytes 786440 | tf_op jit(solution)/shard_map/ppermute | solution.py:268
  4.7 13.3 %collective-permute-start.1 = (f32[2,128,1024]{2,1,0:T(8,128)S(1)}, f32[2,128,1024]{2,1,0:T(8,128)S(1)}, u32[]{:S(2)}, u32[]{:S(2)}) collective-permute-start(f32[2,128,1024]{2,1,0:T(8,128)S(1)} %shard_map.69), channel_id=1, source_target_pairs={{0,4},{4,0},{8,12},{12,8},{16,20},{20,16},{24,28},{28,24},{1,5},{5... | collective-permute-start | bytes 3145736 | tf_op jit(solution)/shard_map/ppermute | solution.py:285
  5.1 6.7 %collective-permute-start.2 = (f32[2,64,256]{2,1,0:T(8,128)S(1)}, f32[2,64,256]{2,1,0:T(8,128)S(1)}, u32[]{:S(2)}, u32[]{:S(2)}) collective-permute-start(f32[2,64,256]{2,1,0:T(8,128)S(1)} %get-tuple-element.26.refs_1_), channel_id=1, source_target_pairs={{0,8},{4,12},{8,0},{12,4},{16,24},{20,28},{24,16},{28,20},{1,9},{5... | collective-permute-start | bytes 393224 | tf_op jit(solution)/shard_map/ppermute | solution.py:287
  12.0 5.7 %collective-permute-start.3 = (f32[1,64,256]{2,1,0:T(8,128)S(1)}, f32[1,64,256]{2,1,0:T(8,128)S(1)}, u32[]{:S(2)}, u32[]{:S(2)}) collective-permute-start(f32[1,64,256]{2,1,0:T(8,128)S(1)} %get-tuple-element.29.refs_2_), channel_id=1, source_target_pairs={{0,16},{4,20},{8,24},{12,28},{16,0},{20,4},{24,8},{28,12},{1,17},{... | collective-permute-start | bytes 196616 | tf_op jit(solution)/shard_map/ppermute | solution.py:287
  17.8 1.6 %collective-permute-start.4 = (f32[264,256]{1,0:T(8,128)S(1)}, f32[264,256]{1,0:T(8,128)S(1)}, u32[]{:S(2)}, u32[]{:S(2)}) collective-permute-start(f32[264,256]{1,0:T(8,128)S(1)} %shard_map.72.refs_1_), channel_id=1, source_target_pairs={{0,4},{4,0},{8,12},{12,8},{16,20},{20,16},{24,28},{28,24},{1,5},{5... | collective-permute-start | bytes 811016 | tf_op jit(solution)/shard_map/ppermute | solution.py:322
  20.0 9.4 %collective-permute-start.5 = (f32[264,256]{1,0:T(8,128)S(1)}, f32[264,256]{1,0:T(8,128)S(1)}, u32[]{:S(2)}, u32[]{:S(2)}) collective-permute-start(f32[264,256]{1,0:T(8,128)S(1)} %get-tuple-element.33), channel_id=1, source_target_pairs={{0,1},{1,0},{2,3},{3,2},{4,5},{5,4},{6,7},{7,6},{8,9},{9,8},{10,11... | collective-permute-start | bytes 811016 | tf_op jit(solution)/shard_map/ppermute | solution.py:336
  21.6 14.0 %collective-permute-start.6 = (f32[264,256]{1,0:T(8,128)S(1)}, f32[264,256]{1,0:T(8,128)S(1)}, u32[]{:S(2)}, u32[]{:S(2)}) collective-permute-start(f32[264,256]{1,0:T(8,128)S(1)} %get-tuple-element.34), channel_id=1, source_target_pairs={{0,2},{1,3},{2,0},{3,1},{4,6},{5,7},{6,4},{7,5},{8,10},{9,11},{10,... | collective-permute-start | bytes 811016 | tf_op jit(solution)/shard_map/ppermute | solution.py:336
  23.1 12.5 %collective-permute-start.7 = (f32[264,256]{1,0:T(8,128)S(1)}, f32[264,256]{1,0:T(8,128)S(1)}, u32[]{:S(2)}, u32[]{:S(2)}) collective-permute-start(f32[264,256]{1,0:T(8,128)S(1)} %get-tuple-element.35), channel_id=1, source_target_pairs={{0,3},{1,2},{2,1},{3,0},{4,7},{5,6},{6,5},{7,4},{8,11},{9,10},{10,... | collective-permute-start | bytes 811016 | tf_op jit(solution)/shard_map/ppermute | solution.py:336
  35.7 5.0 %collective-permute-start.8 = (f32[72,256]{1,0:T(8,128)S(1)}, f32[72,256]{1,0:T(8,128)S(1)}, u32[]{:S(2)}, u32[]{:S(2)}) collective-permute-start(f32[72,256]{1,0:T(8,128)S(1)} %get-tuple-element.37), channel_id=1, source_target_pairs={{0,8},{4,12},{8,0},{12,4},{16,24},{20,28},{24,16},{28,20},{1,9},{5... | collective-permute-start | bytes 221192 | tf_op jit(solution)/shard_map/ppermute | solution.py:343
  37.0 7.6 %collective-permute-start.9 = (f32[72,256]{1,0:T(8,128)S(1)}, f32[72,256]{1,0:T(8,128)S(1)}, u32[]{:S(2)}, u32[]{:S(2)}) collective-permute-start(f32[72,256]{1,0:T(8,128)S(1)} %get-tuple-element.38), channel_id=1, source_target_pairs={{0,16},{4,20},{8,24},{12,28},{16,0},{20,4},{24,8},{28,12},{1,17},{... | collective-permute-start | bytes 221192 | tf_op jit(solution)/shard_map/ppermute | solution.py:343
  40.2 6.2 %collective-permute-start.10 = (f32[72,256]{1,0:T(8,128)S(1)}, f32[72,256]{1,0:T(8,128)S(1)}, u32[]{:S(2)}, u32[]{:S(2)}) collective-permute-start(f32[72,256]{1,0:T(8,128)S(1)} %get-tuple-element.39), channel_id=1, source_target_pairs={{0,24},{4,28},{8,16},{12,20},{16,8},{20,12},{24,0},{28,4},{1,25},{... | collective-permute-start | bytes 221192 | tf_op jit(solution)/shard_map/ppermute | solution.py:343

commit v3 on v2

--- a/solution.py
+++ b/solution.py
@@ -179,26 +179,74 @@
             columns[rows, pl.ds(pl.multiple_of((theirs + d) * paths, paths), paths)] = other
 
 
-def product_body(scale, paths_count, columns, own, got, keep, *rest):
-    messages, (tail, product) = rest[: paths_count - 1], rest[paths_count - 1 :]
-    dates, paths, contracts = tail.shape
+def gather_body(own, got, tail, stats):
+    dates, paths, _ = tail.shape
     half = paths // 2
     for source, at in ((own, core_of()), (got, 1 - core_of())):
         rows = pl.ds(pl.multiple_of(at * half, half), half)
         for d in range(dates):
             tail[d, rows] = source[d * half : (d + 1) * half, :].astype(bf16)
+    stats[...] = own[dates * half :, :] + got[dates * half :, :]
+
+
+def product_body(scale, first_chip, columns, *refs):
+    if first_chip == 0:
+        own, got, keep, message, tail, stats, product = refs
+        gather_body(own, got, tail, stats)
+    else:
+        tail, stats, keep, message, product = refs
+    dates, paths, contracts = tail.shape
     right = tail[...].reshape(dates * paths, contracts)
     chips, count, rows, _ = product.shape
     width = count * rows
     for z in range(chips):
-        block = jnp.dot(columns[z * width : (z + 1) * width, :], right, preferred_element_type=f32)
+        at = (first_chip + z) * width
+        block = jnp.dot(columns[at : at + width, :], right, preferred_element_type=f32)
         product[z] = (scale * block).reshape(count, rows, contracts)
-    stats = own[dates * half :, :] + got[dates * half :, :]
-    me = lax.axis_index("path")
-    for j, out in enumerate((keep, *messages)):
+    halve(0, product, stats[...], keep, message)
+
+
+def path_bits(count):
+    bits = list(range(count.bit_length() - 1))
+    return bits, bits[len(bits) // 2 :] + bits[: len(bits) // 2]
+
+
+def halve(step, product, stats, keep, message):
+    chips, n, rows, _ = product.shape
+    first, second = path_bits(lax.axis_size("path"))
+    bit, place = (
+        jnp.where(core_of() == 0, a, b)
+        for a, b in (
+            (first[step], second[step]),
+            tuple(sum(x < order[step] for x in order[step + 1 :]) for order in (first, second)),
+        )
+    )
+    mine = (lax.axis_index("path") >> bit) & 1
+    for out, value in ((keep, mine), (message, 1 - mine)):
         for z in range(chips):
-            out[z * rows : (z + 1) * rows, :] = product[z, partner(me, j, count)]
-        out[chips * rows :, :] = stats
+            for i in range(n // 2):
+                low = i & ((1 << place) - 1)
+                at = ((i - low) << 1) + (value << place) + low
+                start = (z * (n // 2) + i) * rows
+                out[start : start + rows, :] = product[z, at]
+        out[chips * (n // 2) * rows :, :] = stats
+
+
+def path_pairs(chips, count, step):
+    first, second = path_bits(count)
+    return [
+        ((2 * z + core) * count + p, (2 * z + core) * count + (p ^ (1 << order[step])))
+        for z in range(chips)
+        for core, order in enumerate((first, second))
+        for p in range(count)
+    ]
+
+
+def path_sum_body(step, mine, got, keep, message, product):
+    chips, n, rows, contracts = product.shape
+    size = chips * n * rows
+    product[...] = (mine[:size, :] + got[:size, :]).reshape(product.shape)
+    halve(step, product, mine[size:, :] + got[size:, :], keep, message)
 
 
 def partner(me, j, count):
@@ -217,10 +265,16 @@
     return [(2 * a + core, 2 * b + core) for a, b in pairs(chips, j) for core in range(2)]
 
 
-def path_sum_body(count, chips, *refs):
-    parts, (keep, *messages), (total,) = refs[:count], refs[count : count + chips], refs[count + chips :]
-    total[...] = functools.reduce(lambda a, b: a + b, (p[...] for p in parts))
+def chip_sum_body(chips, shares, *refs):
+    given, (keep, *messages), (total,) = refs[: -chips - 1], refs[-chips - 1 : -1], refs[-1:]
     rows = (total.shape[0] - STAT_ROWS) // chips
+    at = 0
+    for part, share in enumerate(shares):
+        mine, got = given[2 * part : 2 * part + 2]
+        size = share * rows
+        total[at : at + size, :] = mine[:size, :] + got[:size, :]
+        at += size
+    total[at:, :] = mine[size:, :] + got[size:, :]
     for j, out in enumerate((keep, *messages)):
         at = pl.multiple_of(partner(chip_of(), j, chips) * rows, rows)
         out[0:rows, :] = total[pl.ds(at, rows), :]
@@ -320,27 +374,49 @@
         *extra,
     )
     tail_other = lax.ppermute(tail, "date", cores)
-    partial_shape = ((chips * rows + STAT_ROWS, contracts), f32)
+    steps = count.bit_length() - 1
+    assert count == 1 << steps and steps > 0
+    shares = (chips - chips // 4, chips // 4) if chips >= 4 else (chips,)
+
+    def piece(n, chips):
+        return ((chips * n * rows + STAT_ROWS, contracts), f32)
+
+    sent = []
+    for part, share in enumerate(shares):
+        first = part == 0
+        joined = [((2 * dates, paths, contracts), bf16), ((STAT_ROWS, contracts), f32)]
+        keep, message, *made = call(
+            functools.partial(product_body, -1.0 / paths_total, sum(shares[:part])),
+            [piece(count // 2, share)] * 2 + (joined if first else []),
+            columns,
+            *([tail, tail_other] if first else gathered),
+            scratch=[pltpu.VMEM((share, count, rows, contracts), f32)],
+            flops=2 * dates * paths * width * contracts * share // chips,
+        )
+        gathered = made or gathered
+        sent.append((keep, message))
+    for step in range(steps):
+        sent = [(keep, lax.ppermute(m, ("date", "path"), path_pairs(chips, count, step))) for keep, m in sent]
+        if step + 1 == steps:
+            break
+        n = count >> (step + 1)
+        sent = [
+            call(
+                functools.partial(path_sum_body, step + 1),
+                [piece(n // 2, share)] * 2,
+                *pair,
+                scratch=[pltpu.VMEM((share, n, rows, contracts), f32)],
+            )
+            for share, pair in zip(shares, sent)
+        ]
     pieces = call(
-        functools.partial(product_body, -1.0 / paths_total, count),
-        [partial_shape] * count,
-        columns,
-        tail,
-        tail_other,
-        scratch=[
-            pltpu.VMEM((2 * dates, paths, contracts), bf16),
-            pltpu.VMEM((chips, count, rows, contracts), f32),
-        ],
-        flops=2 * dates * paths * width * contracts,
-    )
-    pieces = [pieces[0]] + [lax.ppermute(m, "path", pairs(count, j)) for j, m in enumerate(pieces) if j]
-    pieces = call(
-        functools.partial(path_sum_body, count, chips),
+        functools.partial(chip_sum_body, chips, shares),
         [((rows + STAT_ROWS, contracts), f32)] * chips,
-        *pieces,
-        scratch=[pltpu.VMEM(*partial_shape)],
-    )
-    pieces = [pieces[0]] + [lax.ppermute(m, "date", date_pairs(chips, j)) for j, m in enumerate(pieces) if j]
+        *[x for pair in sent for x in pair],
+        scratch=[pltpu.VMEM(*piece(1, chips))],
+    )
+    order = sorted(range(1, chips), key=lambda j: (-j.bit_length(), j))
+    pieces = [pieces[0]] + [lax.ppermute(pieces[j], "date", date_pairs(chips, j)) for j in order]
     gradient, bound, spread = call(
         functools.partial(date_sum_body, chips, paths_total),
         [((rows, contracts), f32), ((1, contracts), f32), ((1, contracts), f32)],

time: 47.2 us -> 44.6 us (0.945)
  waiting for transfers between devices: 27.4 us -> 23 us
  starting transfers between devices: 14.6 us -> 16.2 us
    ppermute x6 -> x7, waiting for transfers between devices: 18.2 us -> 13.8 us  [the longest x4 9.1 us: shards(): lax.ppermute(m, ('date', 'path'), path_pairs(chips, count, step))]
    ppermute x6 -> x7, starting transfers between devices: 8.07 us -> 9.68 us  [the longest x4 5.16 us: shards(): lax.ppermute(m, ('date', 'path'), path_pairs(chips, count, step))]
    pallas_call x9 -> x12, Pallas kernels: 4.25 us -> 4.47 us  [call(): pl.pallas_call(kernel, out_shape=[jax.ShapeDtypeStruct(*o) for o in outs]...]
  transfers between devices with their start and end apart: 11 -> 12, of which waited for: 9 -> 9; matrix products, arithmetic and copies ran while one was open for 0% -> 0% of each run, Pallas kernels for 1% -> 2%
where the time goes in v3:
time: 44.6 us; the launch traced here: 44.4 us
  waiting for transfers between devices  23 us (52%)
  starting transfers between devices  16.2 us (36%)
  Pallas kernels  4.47 us (10%)
  between operations  0.71 us (2%)
    ppermute x4, waiting for transfers between devices, shards(): lax.ppermute(m, ('date', 'path'), path_pairs(chips, count, step))  9.1 us
    ppermute x2, waiting for transfers between devices, shards(): got = lax.ppermute(message, 'date', date_pairs(chips, 1 << step))  6.89 us
    ppermute x2, starting transfers between devices, shards(): got = lax.ppermute(message, 'date', date_pairs(chips, 1 << step))  5.54 us
    ppermute x4, starting transfers between devices, shards(): lax.ppermute(m, ('date', 'path'), path_pairs(chips, count, step))  5.16 us
    ppermute x3, waiting for transfers between devices, shards(): lax.ppermute(pieces[j], 'date', date_pairs(chips, j))  4.65 us
    ppermute x3, starting transfers between devices, shards(): lax.ppermute(pieces[j], 'date', date_pairs(chips, j))  4.52 us
    pallas_call x12, Pallas kernels, call(): pl.pallas_call(kernel, out_shape=[jax.ShapeDtypeStruct(*o) for o in outs]...  4.47 us
    ppermute x1, waiting for transfers between devices, shards(): tail_other = lax.ppermute(tail, 'date', cores)  1.18 us
  transfers between devices with their start and end apart: 12, of which 9 were waited for; matrix products, arithmetic and copies ran while one was open for 0% of the time, Pallas kernels for 2%

profile of v3, /device:TPU:0, one launch (start us, length us, event | category | flops | bytes accessed | tf_op | source)
XLA Modules:
  0.0 44.4 jit_solution(10129203200483402874)
XLA Ops:
  0.6 2.1 %shard_map.67 = (f32[4,64,256]{2,1,0:T(8,128)S(1)}, f32[4,64,256]{2,1,0:T(8,128)S(1)}, bf16[2,128,2048]{2,1,0:T(8,128)(2,1)S(1)}) custom-call(bf16[2,128,2048]{2,1,0:T(8,128)(2,1)} %refs_0_.1, bf16[2048,256]{1,0:T(8,128)(2,1)} %refs_1_.1, f32[2,128,256]{2,1,0:T(8,128)} %refs_2_.1, s32[2,256]{1,0:T(2,128)} %refs_3_.1), custom_call_target="tpu_custom_call" | custom-call | flops 268435456 | tf_op jit(solution)/shard_map/pallas_call | solution.py:38
  2.7 0.5 %collective-permute-start = (f32[4,64,256]{2,1,0:T(8,128)S(1)}, f32[4,64,256]{2,1,0:T(8,128)S(1)}, u32[]{:S(2)}, u32[]{:S(2)}) collective-permute-start(f32[4,64,256]{2,1,0:T(8,128)S(1)} %get-tuple-element.31), channel_id=1, source_target_pairs={{0,4},{4,0},{8,12},{12,8},{16,20},{20,16},{24,28},{28,24},{1,5},{5... | collective-permute-start | bytes 786440 | tf_op jit(solution)/shard_map/ppermute | solution.py:322
  3.3 1.2 %collective-permute-done.refs_1_ = f32[4,64,256]{2,1,0:T(8,128)S(1)} collective-permute-done((f32[4,64,256]{2,1,0:T(8,128)S(1)}, f32[4,64,256]{2,1,0:T(8,128)S(1)}, u32[]{:S(2)}, u32[]{:S(2)}) %collective-permute-start) | collective-permute-done | bytes 262176 | tf_op jit(solution)/shard_map/ppermute | solution.py:322
  4.4 0.1 shard_map.68
  4.6 0.1 shard_map.69
  4.7 0.4 collective-permute-start.1
  5.1 2.7 %collective-permute-start.2 = (f32[2,64,256]{2,1,0:T(8,128)S(1)}, f32[2,64,256]{2,1,0:T(8,128)S(1)}, u32[]{:S(2)}, u32[]{:S(2)}) collective-permute-start(f32[2,64,256]{2,1,0:T(8,128)S(1)} %get-tuple-element.32.refs_1_), channel_id=1, source_target_pairs={{0,8},{4,12},{8,0},{12,4},{16,24},{20,28},{24,16},{28,20},{1,9},{5... | collective-permute-start | bytes 393224 | tf_op jit(solution)/shard_map/ppermute | solution.py:341
  7.8 4.0 %collective-permute-done.2.refs_2_ = f32[2,64,256]{2,1,0:T(8,128)S(1)} collective-permute-done((f32[2,64,256]{2,1,0:T(8,128)S(1)}, f32[2,64,256]{2,1,0:T(8,128)S(1)}, u32[]{:S(2)}, u32[]{:S(2)}) %collective-permute-start.2) | collective-permute-done | bytes 131104 | tf_op jit(solution)/shard_map/ppermute | solution.py:341
  11.8 0.1 shard_map.70
  11.9 2.8 %collective-permute-start.3 = (f32[1,64,256]{2,1,0:T(8,128)S(1)}, f32[1,64,256]{2,1,0:T(8,128)S(1)}, u32[]{:S(2)}, u32[]{:S(2)}) collective-permute-start(f32[1,64,256]{2,1,0:T(8,128)S(1)} %get-tuple-element.35.refs_2_), channel_id=1, source_target_pairs={{0,16},{4,20},{8,24},{12,28},{16,0},{20,4},{24,8},{28,12},{1,17},{... | collective-permute-start | bytes 196616 | tf_op jit(solution)/shard_map/ppermute | solution.py:341
  14.8 2.9 %collective-permute-done.3.refs_4_ = f32[1,64,256]{2,1,0:T(8,128)S(1)} collective-permute-done((f32[1,64,256]{2,1,0:T(8,128)S(1)}, f32[1,64,256]{2,1,0:T(8,128)S(1)}, u32[]{:S(2)}, u32[]{:S(2)}) %collective-permute-start.3) | collective-permute-done | bytes 65568 | tf_op jit(solution)/shard_map/ppermute | solution.py:341
  17.6 0.2 shard_map.72.refs_1_
  17.8 0.1 collective-permute-start.4
  17.9 0.0 collective-permute-done.1.refs_1_
  17.9 0.3 shard_map.71.refs_0_
  18.3 1.2 %collective-permute-done.4.refs_2_ = f32[264,256]{1,0:T(8,128)S(1)} collective-permute-done((f32[264,256]{1,0:T(8,128)S(1)}, f32[264,256]{1,0:T(8,128)S(1)}, u32[]{:S(2)}, u32[]{:S(2)}) %collective-permute-start.4) | collective-permute-done | bytes 270368 | tf_op jit(solution)/shard_map/ppermute | solution.py:376
  19.4 0.5 %shard_map.73 = (f32[392,256]{1,0:T(8,128)S(1)}, f32[392,256]{1,0:T(8,128)S(1)}, bf16[4,128,256]{2,1,0:T(8,128)(2,1)S(1)}, f32[8,256]{1,0:T(8,128)S(1)}) custom-call(bf16[1024,512]{1,0:T(8,128)(2,1)S(1)} %shard_map.71.refs_0_, f32[264,256]{1,0:T(8,128)S(1)} %shard_map.72.refs_1_, f32[264,256]{1,0:T(8,128)S(1)} %collective-permute-done.4.refs_2_), custom_call_target="tpu_custom_call" | custom-call | flops 201326592 | tf_op jit(solution)/shard_map/pallas_call | solution.py:38
  19.9 1.6 %collective-permute-start.5 = (f32[392,256]{1,0:T(8,128)S(1)}, f32[392,256]{1,0:T(8,128)S(1)}, u32[]{:S(2)}, u32[]{:S(2)}) collective-permute-start(f32[392,256]{1,0:T(8,128)S(1)} %get-tuple-element.39), channel_id=1, source_target_pairs={{0,1},{1,0},{2,3},{3,2},{4,6},{5,7},{6,4},{7,5},{8,9},{9,8},{10,11... | collective-permute-start | bytes 1204232 | tf_op jit(solution)/shard_map/ppermute | solution.py:399
  21.5 0.2 shard_map.75
  21.7 0.6 %collective-permute-start.7 = (f32[136,256]{1,0:T(8,128)S(1)}, f32[136,256]{1,0:T(8,128)S(1)}, u32[]{:S(2)}, u32[]{:S(2)}) collective-permute-start(f32[136,256]{1,0:T(8,128)S(1)} %get-tuple-element.45), channel_id=1, source_target_pairs={{0,1},{1,0},{2,3},{3,2},{4,6},{5,7},{6,4},{7,5},{8,9},{9,8},{10,11... | collective-permute-start | bytes 417800 | tf_op jit(solution)/shard_map/ppermute | solution.py:399
  22.3 5.5 %collective-permute-done.5.refs_1_ = f32[392,256]{1,0:T(8,128)S(1)} collective-permute-done((f32[392,256]{1,0:T(8,128)S(1)}, f32[392,256]{1,0:T(8,128)S(1)}, u32[]{:S(2)}, u32[]{:S(2)}) %collective-permute-start.5) | collective-permute-done | bytes 401440 | tf_op jit(solution)/shard_map/ppermute | solution.py:399
  27.8 0.1 shard_map.74
  27.9 1.6 %collective-permute-start.6 = (f32[200,256]{1,0:T(8,128)S(1)}, f32[200,256]{1,0:T(8,128)S(1)}, u32[]{:S(2)}, u32[]{:S(2)}) collective-permute-start(f32[200,256]{1,0:T(8,128)S(1)} %get-tuple-element.41), channel_id=1, source_target_pairs={{0,2},{1,3},{2,0},{3,1},{4,5},{5,4},{6,7},{7,6},{8,10},{9,11},{10,... | collective-permute-start | bytes 614408 | tf_op jit(solution)/shard_map/ppermute | solution.py:399
  29.5 0.0 collective-permute-done.7.refs_1_
  29.6 1.4 %collective-permute-start.8 = (f32[72,256]{1,0:T(8,128)S(1)}, f32[72,256]{1,0:T(8,128)S(1)}, u32[]{:S(2)}, u32[]{:S(2)}) collective-permute-start(f32[72,256]{1,0:T(8,128)S(1)} %get-tuple-element.47), channel_id=1, source_target_pairs={{0,2},{1,3},{2,0},{3,1},{4,5},{5,4},{6,7},{7,6},{8,10},{9,11},{10,... | collective-permute-start | bytes 221192 | tf_op jit(solution)/shard_map/ppermute | solution.py:399
  31.0 3.6 %collective-permute-done.8.refs_3_ = f32[72,256]{1,0:T(8,128)S(1)} collective-permute-done((f32[72,256]{1,0:T(8,128)S(1)}, f32[72,256]{1,0:T(8,128)S(1)}, u32[]{:S(2)}, u32[]{:S(2)}) %collective-permute-start.8) | collective-permute-done | bytes 73760 | tf_op jit(solution)/shard_map/ppermute | solution.py:399
  34.5 0.0 collective-permute-done.6.refs_1_
  34.5 0.1 shard_map.77
  34.6 2.4 %collective-permute-start.9 = (f32[72,256]{1,0:T(8,128)S(1)}, f32[72,256]{1,0:T(8,128)S(1)}, u32[]{:S(2)}, u32[]{:S(2)}) collective-permute-start(f32[72,256]{1,0:T(8,128)S(1)} %get-tuple-element.49), channel_id=1, source_target_pairs={{0,16},{4,20},{8,24},{12,28},{16,0},{20,4},{24,8},{28,12},{1,17},{... | collective-permute-start | bytes 221192 | tf_op jit(solution)/shard_map/ppermute | solution.py:419
  37.0 1.6 %collective-permute-start.10 = (f32[72,256]{1,0:T(8,128)S(1)}, f32[72,256]{1,0:T(8,128)S(1)}, u32[]{:S(2)}, u32[]{:S(2)}) collective-permute-start(f32[72,256]{1,0:T(8,128)S(1)} %get-tuple-element.50), channel_id=1, source_target_pairs={{0,24},{4,28},{8,16},{12,20},{16,8},{20,12},{24,0},{28,4},{1,25},{... | collective-permute-start | bytes 221192 | tf_op jit(solution)/shard_map/ppermute | solution.py:419
  38.6 0.5 %collective-permute-start.11 = (f32[72,256]{1,0:T(8,128)S(1)}, f32[72,256]{1,0:T(8,128)S(1)}, u32[]{:S(2)}, u32[]{:S(2)}) collective-permute-start(f32[72,256]{1,0:T(8,128)S(1)} %get-tuple-element.51), channel_id=1, source_target_pairs={{0,8},{4,12},{8,0},{12,4},{16,24},{20,28},{24,16},{28,20},{1,9},{5... | collective-permute-start | bytes 221192 | tf_op jit(solution)/shard_map/ppermute | solution.py:419
  39.1 3.0 %collective-permute-done.9.refs_1_ = f32[72,256]{1,0:T(8,128)S(1)} collective-permute-done((f32[72,256]{1,0:T(8,128)S(1)}, f32[72,256]{1,0:T(8,128)S(1)}, u32[]{:S(2)}, u32[]{:S(2)}) %collective-permute-start.9) | collective-permute-done | bytes 73760 | tf_op jit(solution)/shard_map/ppermute | solution.py:419
  42.1 1.2 %collective-permute-done.10.refs_2_ = f32[72,256]{1,0:T(8,128)S(1)} collective-permute-done((f32[72,256]{1,0:T(8,128)S(1)}, f32[72,256]{1,0:T(8,128)S(1)}, u32[]{:S(2)}, u32[]{:S(2)}) %collective-permute-start.10) | collective-permute-done | bytes 73760 | tf_op jit(solution)/shard_map/ppermute | solution.py:419
  43.3 0.5 %collective-permute-done.11.refs_3_ = f32[72,256]{1,0:T(8,128)S(1)} collective-permute-done((f32[72,256]{1,0:T(8,128)S(1)}, f32[72,256]{1,0:T(8,128)S(1)}, u32[]{:S(2)}, u32[]{:S(2)}) %collective-permute-start.11) | collective-permute-done | bytes 73760 | tf_op jit(solution)/shard_map/ppermute | solution.py:419
  43.8 0.7 %shard_map.78 = (f32[64,256]{1,0:T(8,128)}, f32[1,256]{1,0:T(1,128)}, f32[1,256]{1,0:T(1,128)}) custom-call(f32[72,256]{1,0:T(8,128)S(1)} %get-tuple-element.48.refs_0_, f32[72,256]{1,0:T(8,128)S(1)} %collective-permute-done.9.refs_1_, f32[72,256]{1,0:T(8,128)S(1)} %collective-permute-done.10.refs_2_, f32[72,256]{1,0:T(8,128)S(1)} %collective-permute-done.11.refs_3_), custom_call_target="tpu_custom_call" | custom-call | tf_op jit(solution)/shard_map/pallas_call | solution.py:38
  (1 shorter events, 0.0 us)
Async XLA Ops:
  2.7 1.7 %collective-permute-start = (f32[4,64,256]{2,1,0:T(8,128)S(1)}, f32[4,64,256]{2,1,0:T(8,128)S(1)}, u32[]{:S(2)}, u32[]{:S(2)}) collective-permute-start(f32[4,64,256]{2,1,0:T(8,128)S(1)} %get-tuple-element.31), channel_id=1, source_target_pairs={{0,4},{4,0},{8,12},{12,8},{16,20},{20,16},{24,28},{28,24},{1,5},{5... | collective-permute-start | bytes 786440 | tf_op jit(solution)/shard_map/ppermute | solution.py:322
  4.7 13.3 %collective-permute-start.1 = (f32[2,128,1024]{2,1,0:T(8,128)S(1)}, f32[2,128,1024]{2,1,0:T(8,128)S(1)}, u32[]{:S(2)}, u32[]{:S(2)}) collective-permute-start(f32[2,128,1024]{2,1,0:T(8,128)S(1)} %shard_map.69), channel_id=1, source_target_pairs={{0,4},{4,0},{8,12},{12,8},{16,20},{20,16},{24,28},{28,24},{1,5},{5... | collective-permute-start | bytes 3145736 | tf_op jit(solution)/shard_map/ppermute | solution.py:339
  5.1 6.7 %collective-permute-start.2 = (f32[2,64,256]{2,1,0:T(8,128)S(1)}, f32[2,64,256]{2,1,0:T(8,128)S(1)}, u32[]{:S(2)}, u32[]{:S(2)}) collective-permute-start(f32[2,64,256]{2,1,0:T(8,128)S(1)} %get-tuple-element.32.refs_1_), channel_id=1, source_target_pairs={{0,8},{4,12},{8,0},{12,4},{16,24},{20,28},{24,16},{28,20},{1,9},{5... | collective-permute-start | bytes 393224 | tf_op jit(solution)/shard_map/ppermute | solution.py:341
  11.9 5.7 %collective-permute-start.3 = (f32[1,64,256]{2,1,0:T(8,128)S(1)}, f32[1,64,256]{2,1,0:T(8,128)S(1)}, u32[]{:S(2)}, u32[]{:S(2)}) collective-permute-start(f32[1,64,256]{2,1,0:T(8,128)S(1)} %get-tuple-element.35.refs_2_), channel_id=1, source_target_pairs={{0,16},{4,20},{8,24},{12,28},{16,0},{20,4},{24,8},{28,12},{1,17},{... | collective-permute-start | bytes 196616 | tf_op jit(solution)/shard_map/ppermute | solution.py:341
  17.8 1.6 %collective-permute-start.4 = (f32[264,256]{1,0:T(8,128)S(1)}, f32[264,256]{1,0:T(8,128)S(1)}, u32[]{:S(2)}, u32[]{:S(2)}) collective-permute-start(f32[264,256]{1,0:T(8,128)S(1)} %shard_map.72.refs_1_), channel_id=1, source_target_pairs={{0,4},{4,0},{8,12},{12,8},{16,20},{20,16},{24,28},{28,24},{1,5},{5... | collective-permute-start | bytes 811016 | tf_op jit(solution)/shard_map/ppermute | solution.py:376
  19.9 7.9 %collective-permute-start.5 = (f32[392,256]{1,0:T(8,128)S(1)}, f32[392,256]{1,0:T(8,128)S(1)}, u32[]{:S(2)}, u32[]{:S(2)}) collective-permute-start(f32[392,256]{1,0:T(8,128)S(1)} %get-tuple-element.39), channel_id=1, source_target_pairs={{0,1},{1,0},{2,3},{3,2},{4,6},{5,7},{6,4},{7,5},{8,9},{9,8},{10,11... | collective-permute-start | bytes 1204232 | tf_op jit(solution)/shard_map/ppermute | solution.py:399
  21.7 7.8 %collective-permute-start.7 = (f32[136,256]{1,0:T(8,128)S(1)}, f32[136,256]{1,0:T(8,128)S(1)}, u32[]{:S(2)}, u32[]{:S(2)}) collective-permute-start(f32[136,256]{1,0:T(8,128)S(1)} %get-tuple-element.45), channel_id=1, source_target_pairs={{0,1},{1,0},{2,3},{3,2},{4,6},{5,7},{6,4},{7,5},{8,9},{9,8},{10,11... | collective-permute-start | bytes 417800 | tf_op jit(solution)/shard_map/ppermute | solution.py:399
  27.9 6.6 %collective-permute-start.6 = (f32[200,256]{1,0:T(8,128)S(1)}, f32[200,256]{1,0:T(8,128)S(1)}, u32[]{:S(2)}, u32[]{:S(2)}) collective-permute-start(f32[200,256]{1,0:T(8,128)S(1)} %get-tuple-element.41), channel_id=1, source_target_pairs={{0,2},{1,3},{2,0},{3,1},{4,5},{5,4},{6,7},{7,6},{8,10},{9,11},{10,... | collective-permute-start | bytes 614408 | tf_op jit(solution)/shard_map/ppermute | solution.py:399
  29.6 5.0 %collective-permute-start.8 = (f32[72,256]{1,0:T(8,128)S(1)}, f32[72,256]{1,0:T(8,128)S(1)}, u32[]{:S(2)}, u32[]{:S(2)}) collective-permute-start(f32[72,256]{1,0:T(8,128)S(1)} %get-tuple-element.47), channel_id=1, source_target_pairs={{0,2},{1,3},{2,0},{3,1},{4,5},{5,4},{6,7},{7,6},{8,10},{9,11},{10,... | collective-permute-start | bytes 221192 | tf_op jit(solution)/shard_map/ppermute | solution.py:399
  34.6 7.5 %collective-permute-start.9 = (f32[72,256]{1,0:T(8,128)S(1)}, f32[72,256]{1,0:T(8,128)S(1)}, u32[]{:S(2)}, u32[]{:S(2)}) collective-permute-start(f32[72,256]{1,0:T(8,128)S(1)} %get-tuple-element.49), channel_id=1, source_target_pairs={{0,16},{4,20},{8,24},{12,28},{16,0},{20,4},{24,8},{28,12},{1,17},{... | collective-permute-start | bytes 221192 | tf_op jit(solution)/shard_map/ppermute | solution.py:419
  37.0 6.3 %collective-permute-start.10 = (f32[72,256]{1,0:T(8,128)S(1)}, f32[72,256]{1,0:T(8,128)S(1)}, u32[]{:S(2)}, u32[]{:S(2)}) collective-permute-start(f32[72,256]{1,0:T(8,128)S(1)} %get-tuple-element.50), channel_id=1, source_target_pairs={{0,24},{4,28},{8,16},{12,20},{16,8},{20,12},{24,0},{28,4},{1,25},{... | collective-permute-start | bytes 221192 | tf_op jit(solution)/shard_map/ppermute | solution.py:419
  38.6 5.1 %collective-permute-start.11 = (f32[72,256]{1,0:T(8,128)S(1)}, f32[72,256]{1,0:T(8,128)S(1)}, u32[]{:S(2)}, u32[]{:S(2)}) collective-permute-start(f32[72,256]{1,0:T(8,128)S(1)} %get-tuple-element.51), channel_id=1, source_target_pairs={{0,8},{4,12},{8,0},{12,4},{16,24},{20,28},{24,16},{28,20},{1,9},{5... | collective-permute-start | bytes 221192 | tf_op jit(solution)/shard_map/ppermute | solution.py:419

commit v4 on v3

v4 whole, which is shorter than its diff:
```python
import functools

import jax
import jax.numpy as jnp
from jax import lax
from jax.experimental import pallas as pl
from jax.experimental.pallas import tpu as pltpu
from jax.sharding import PartitionSpec as P

INVERSE_TEMP = 4.0
TEMP = 0.25
NEG = -1e30
STAT_ROWS = 8
PIECES = 2
FIRST = 4
VMEM_LIMIT = 16 << 20
f32 = jnp.float32
bf16 = jnp.bfloat16


def core_of():
    return lax.axis_index("date") % 2


def chip_of():
    return lax.axis_index("date") // 2


def in_hbm(x):
    return pltpu.with_memory_space_constraint(x, pltpu.HBM)


def call(body, outs, *operands, scratch=(), flops=0, unread=0, place=()):
    whole = pl.BlockSpec(memory_space=pltpu.VMEM)
    anywhere = pl.BlockSpec(memory_space=pl.ANY)
    read = len(operands) - unread

    def kernel(*refs):
        body(*refs[:read], *refs[read + unread :])

    specs = [pl.BlockSpec(memory_space=p) for p in place]
    return pl.pallas_call(
        kernel,
        out_shape=[jax.ShapeDtypeStruct(*o) for o in outs],
        in_specs=specs + [whole] * (read - len(specs)) + [anywhere] * unread,
        out_specs=[whole] * len(outs),
        scratch_shapes=list(scratch),
        compiler_params=pltpu.CompilerParams(vmem_limit_bytes=VMEM_LIMIT),
        cost_estimate=pl.CostEstimate(flops=flops, bytes_accessed=0, transcendentals=0),
    )(*operands)


def log_add(a, b):
    return jnp.maximum(a, b) + jnp.log(1.0 + jnp.exp(-jnp.abs(a - b)))


def fill(out, inc, pay, may):
    dates = inc.shape[0]
    out[0:dates] = INVERSE_TEMP * inc
    for d in range(dates):
        out[dates + d] = jnp.where(may[d : d + 1, :] > 0, INVERSE_TEMP * pay[d], NEG)


def theirs_body(features, coefficients, payoff, exercise, send, held, weights, pay, may, sems, others):
    dates, paths, width = features.shape
    half, step = paths // 2, width // PIECES
    rows = pl.ds(pl.multiple_of((1 - core_of()) * half, half), half)
    parts = [slice(i * step, (i + 1) * step) for i in range(PIECES)]
    copies = [
        (
            pltpu.make_async_copy(features.at[:, rows, at], held.at[:, :, at], sems.at[2 * i]),
            pltpu.make_async_copy(coefficients.at[at, :], weights.at[at, :], sems.at[2 * i + 1]),
        )
        for i, at in enumerate(parts)
    ]
    small = (
        pltpu.make_async_copy(payoff.at[:, rows, :], pay, others.at[0]),
        pltpu.make_async_copy(exercise, may, others.at[1]),
    )
    for c in (*(c for pair in copies for c in pair), *small):
        c.start()
    inc = None
    for pair, at in zip(copies, parts):
        for c in pair:
            c.wait()
        left = held[:, :, at].reshape(dates * half, step)
        part = jnp.dot(left, weights[at, :], preferred_element_type=f32)
        inc = part if inc is None else inc + part
    for c in small:
        c.wait()
    fill(send, inc.reshape(dates, half, -1), pay, may)


def mine_body(features, payoff, exercise, weights, theirs, keep, held, pay, may, sems):
    dates, paths, width = features.shape
    half = paths // 2
    rows = pl.ds(pl.multiple_of(core_of() * half, half), half)
    copies = (
        pltpu.make_async_copy(features.at[:, rows, :], held.at[:, rows, :], sems.at[0]),
        pltpu.make_async_copy(payoff.at[:, rows, :], pay, sems.at[1]),
        pltpu.make_async_copy(exercise, may, sems.at[2]),
    )
    for c in copies:
        c.start()
    held[:, pl.ds(pl.multiple_of((1 - core_of()) * half, half), half), :] = theirs[...]
    for c in copies:
        c.wait()
    inc = jnp.dot(held[:, rows, :].reshape(dates * half, width), weights[...], preferred_element_type=f32)
    fill(keep, inc.reshape(dates, half, -1), pay, may)


def message_of(level, total, left, last):
    if last:
        return [jnp.where(left, level + total, level)]
    return [level, total]


def local_body(rounds, keep, other, score, level, total, message):
    dates = keep.shape[0] // 2
    first = core_of() == 0
    run = jnp.zeros(keep.shape[1:], f32)
    scores = []
    for part in (0, 1):
        for d in range(dates):
            inc, base = (
                jnp.where(first == (part == 0), keep[at], other[at]) for at in (d, dates + d)
            )
            run = run + inc
            scores.append(base - run)
    peak = functools.reduce(jnp.maximum, scores)
    lev = peak + jnp.log(sum(jnp.exp(s - peak) for s in scores))
    for i, s in enumerate(scores):
        score[i] = s
    level[...] = lev
    total[...] = run
    left = chip_of() % 2 == 0
    if rounds == 2:
        message[0] = jnp.where(left, lev + run, lev)
        return
    for i, m in enumerate(message_of(lev, run, left, rounds == 1)):
        message[i] = m


def pair_body(total, message, near, out):
    both = log_add(message[0], near[0])
    own = total[...]
    out[0] = both + jnp.where(chip_of() == 1, own, jnp.where(chip_of() == 2, -own, 0.0))


def merge_body(step, rounds, level, total, state, got, state2, message, *group):
    left = (chip_of() >> step) % 2 == 0
    lev, tot, other_lev, other_tot = level[...], total[...], got[0], got[1]
    if state is None:
        zero = jnp.zeros_like(lev)
        before, after, sum_before, sum_after = zero + NEG, zero + NEG, zero, zero
    else:
        before, after, sum_before, sum_after = (state[i] for i in range(4))
    state2[0] = jnp.where(left, before, log_add(before, other_lev + other_tot + sum_before))
    state2[1] = jnp.where(left, log_add(after, other_lev - sum_after), after)
    state2[2] = jnp.where(left, sum_before, sum_before + other_tot)
    state2[3] = jnp.where(left, sum_after + other_tot, sum_after)
    first_lev, first_tot = jnp.where(left, lev, other_lev), jnp.where(left, tot, other_tot)
    second_lev = jnp.where(left, other_lev, lev)
    lev2 = log_add(first_lev, second_lev - first_tot)
    tot2 = tot + other_tot
    for out, value in zip(group, (lev2, tot2)):
        out[...] = value
    next_left = (chip_of() >> (step + 1)) % 2 == 0
    for i, m in enumerate(message_of(lev2, tot2, next_left, step + 2 == rounds)):
        message[i] = m


def joined(rounds, state, got, zero):
    if state is None:
        before, after, sum_before, sum_after = zero + NEG, zero + NEG, zero, zero
    else:
        before, after, sum_before, sum_after = (state[i] for i in range(4))
    if got is not None:
        left = (chip_of() >> (rounds - 1)) % 2 == 0
        other = got[0]
        before = jnp.where(left, before, log_add(before, other + sum_before))
        after = jnp.where(left, log_add(after, other - sum_after), after)
    return before, after, sum_before


def joined_four(near, far, beside, across):
    first, left = chip_of() % 2 == 0, chip_of() < 2
    shift = jnp.where(first == left, beside[...], across[...])
    near, far = near[0], far[0] + jnp.where(left, -shift, shift)
    both, none = log_add(near, far), jnp.zeros_like(near) + NEG
    before = jnp.where(left, jnp.where(first, none, near), jnp.where(first, far, both))
    after = jnp.where(left, jnp.where(first, both, far), jnp.where(first, near, none))
    return before, after, jnp.where(first, 0.0, beside[...])


def tail_body(join, score, level, total, *refs):
    *given, out = refs
    lev, tot = level[...], total[...]
    before, after, sum_before = join(*given, jnp.zeros_like(lev))
    later = after - tot
    norm = log_add(log_add(before, lev), later)
    run = jnp.exp(later - norm)
    half = score.shape[1]
    for i in reversed(range(score.shape[0])):
        run = run + jnp.exp(score[i] - norm)
        out[i * half : (i + 1) * half, :] = run.astype(bf16).astype(f32)
    smoothed = TEMP * (norm - sum_before)
    at = score.shape[0] * half
    out[at : at + STAT_ROWS, :] = jnp.zeros((STAT_ROWS, smoothed.shape[1]), f32)
    out[at : at + 1, :] = jnp.sum(smoothed, axis=0, keepdims=True)
    out[at + 1 : at + 2, :] = jnp.sum(smoothed * smoothed, axis=0, keepdims=True)


def halves_body(chips, features, send):
    width = features.shape[2] // (2 * chips)
    for z in range(chips):
        at = pl.multiple_of((2 * z + 1 - core_of()) * width, width)
        send[:, :, z * width : (z + 1) * width] = features[:, :, pl.ds(at, width)].astype(f32)


def columns_body(chips, features, got, columns):
    dates, paths, whole = features.shape
    half, width = paths // 2, whole // (2 * chips)
    size = dates * half
    for z in range(chips):
        at = pl.multiple_of((2 * z + core_of()) * width, width)
        rows = slice(z * width, (z + 1) * width)
        for h in range(2):
            span = slice(h * half, (h + 1) * half)
            own = features[:, span, pl.ds(at, width)].reshape(size, width).T
            columns[rows, pl.ds(pl.multiple_of((2 * h + core_of()) * size, size), size)] = own
            other = got[:, span, rows].astype(bf16).reshape(size, width).T
            columns[rows, pl.ds(pl.multiple_of((2 * h + 1 - core_of()) * size, size), size)] = other


def side(columns, rows, half):
    size = columns.shape[1] // 2
    return columns[rows, pl.ds(pl.multiple_of(half * size, size), size)]


def first_body(scale, columns, own, out):
    size = columns.shape[1] // 2
    right = own[:size, :].astype(bf16)
    step = columns.shape[0] // FIRST
    for i in range(FIRST):
        rows = slice(i * step, (i + 1) * step)
        out[rows, :] = scale * jnp.dot(side(columns, rows, core_of()), right, preferred_element_type=f32)


def product_body(scale, first_chip, columns, begun, own, got, keep, message, product):
    size = columns.shape[1] // 2
    right = got[:size, :].astype(bf16)
    chips, count, rows, contracts = product.shape
    width = count * rows
    for z in range(chips):
        at = slice((first_chip + z) * width, (first_chip + z + 1) * width)
        block = scale * jnp.dot(side(columns, at, 1 - core_of()), right, preferred_element_type=f32)
        product[z] = (begun[at, :] + block).reshape(count, rows, contracts)
    halve(0, product, own[size:, :] + got[size:, :], keep, message)


def path_bits(count):
    bits = list(range(count.bit_length() - 1))
    return bits, bits[len(bits) // 2 :] + bits[: len(bits) // 2]


def halve(step, product, stats, keep, message):
    chips, n, rows, _ = product.shape
    first, second = path_bits(lax.axis_size("path"))
    bit, place = (
        jnp.where(core_of() == 0, a, b)
        for a, b in (
            (first[step], second[step]),
            tuple(sum(x < order[step] for x in order[step + 1 :]) for order in (first, second)),
        )
    )
    mine = (lax.axis_index("path") >> bit) & 1
    for out, value in ((keep, mine), (message, 1 - mine)):
        for z in range(chips):
            for i in range(n // 2):
                low = i & ((1 << place) - 1)
                at = ((i - low) << 1) + (value << place) + low
                start = (z * (n // 2) + i) * rows
                out[start : start + rows, :] = product[z, at]
        out[chips * (n // 2) * rows :, :] = stats


def path_pairs(chips, count, step):
    first, second = path_bits(count)
    return [
        ((2 * z + core) * count + p, (2 * z + core) * count + (p ^ (1 << order[step])))
        for z in range(chips)
        for core, order in enumerate((first, second))
        for p in range(count)
    ]


def path_sum_body(step, mine, got, keep, message, product):
    chips, n, rows, contracts = product.shape
    size = chips * n * rows
    product[...] = (mine[:size, :] + got[:size, :]).reshape(product.shape)
    halve(step, product, mine[size:, :] + got[size:, :], keep, message)


def partner(me, j, count):
    if count & (count - 1) == 0:
        return me ^ j
    return lax.rem(me + j, count)


def pairs(count, j):
    if count & (count - 1) == 0:
        return [(i, i ^ j) for i in range(count)]
    return [(i, (i + j) % count) for i in range(count)]


def date_pairs(chips, j):
    return [(2 * a + core, 2 * b + core) for a, b in pairs(chips, j) for core in range(2)]


def chip_sum_body(chips, shares, *refs):
    given, (keep, *messages), (total,) = refs[: -chips - 1], refs[-chips - 1 : -1], refs[-1:]
    rows = (total.shape[0] - STAT_ROWS) // chips
    at = 0
    for part, share in enumerate(shares):
        mine, got = given[2 * part : 2 * part + 2]
        size = share * rows
        total[at : at + size, :] = mine[:size, :] + got[:size, :]
        at += size
    total[at:, :] = mine[size:, :] + got[size:, :]
    for j, out in enumerate((keep, *messages)):
        at = pl.multiple_of(partner(chip_of(), j, chips) * rows, rows)
        out[0:rows, :] = total[pl.ds(at, rows), :]
        if out.shape[0] > rows:
            out[rows:, :] = total[chips * rows :, :]


def date_sum_body(chips, paths_total, *refs):
    parts, (gradient, bound, spread) = refs[:chips], refs[chips:]
    rows = gradient.shape[0]
    gradient[...] = functools.reduce(lambda a, b: a + b, (p[:rows, :] for p in parts))
    first = chip_of() < max(chips // 2, 1)
    across = parts[([0] + chip_order(chips)).index(chips // 2)]
    stats = jnp.where(first, parts[0][rows:, :], across[rows:, :])
    mean = stats[0:1, :] * (1.0 / paths_total)
    bound[...] = mean
    spread[...] = stats[1:2, :] * (1.0 / paths_total) - mean * mean


def chip_order(chips):
    return sorted(range(1, chips), key=lambda j: (-j.bit_length(), j))


def shards(features, payoff, coefficients, exercise):
    dates, paths, width = features.shape
    contracts = coefficients.shape[1]
    chips, count = lax.axis_size("date") // 2, lax.axis_size("path")
    rounds = chips.bit_length() - 1
    assert chips == 1 << rounds
    half, paths_total = paths // 2, paths * count
    rows = width // (2 * chips * count)
    cores = [(2 * z + c, 2 * z + 1 - c) for z in range(chips) for c in range(2)]
    plane = (half, contracts)

    halves = (dates, half, width)
    send, theirs, weights = call(
        theirs_body,
        [((2 * dates, *plane), f32), (halves, bf16), (coefficients.shape, bf16)],
        *(in_hbm(x) for x in (features, coefficients, payoff, exercise)),
        scratch=[
            pltpu.VMEM((dates, half, contracts), f32),
            pltpu.VMEM(exercise.shape, jnp.int32),
            pltpu.SemaphoreType.DMA((2 * PIECES,)),
            pltpu.SemaphoreType.DMA((2,)),
        ],
        place=[pltpu.HBM] * 4,
    )
    other = lax.ppermute(send, "date", cores)
    keep, held = call(
        mine_body,
        [((2 * dates, *plane), f32), (features.shape, bf16)],
        *(in_hbm(x) for x in (features, payoff, exercise)),
        weights,
        theirs,
        scratch=[
            pltpu.VMEM((dates, half, contracts), f32),
            pltpu.VMEM(exercise.shape, jnp.int32),
            pltpu.SemaphoreType.DMA((3,)),
        ],
        place=[pltpu.HBM] * 3,
    )
    sizes = [1 if step + 1 == rounds or rounds == 2 else 2 for step in range(rounds)] or [2]
    score, level, total, message = call(
        functools.partial(local_body, rounds),
        [((2 * dates, *plane), f32), (plane, f32), (plane, f32), ((sizes[0], *plane), f32)],
        keep,
        other,
    )
    (columns_send,) = call(
        functools.partial(halves_body, chips),
        [((dates, paths, width // 2), f32)],
        held,
        message,
        unread=1,
    )
    columns_got = lax.ppermute(columns_send, "date", cores)
    own_level, own_total, state, got = level, total, None, None
    if rounds == 2:
        near = lax.ppermute(message, "date", date_pairs(chips, 1))
        beside = lax.ppermute(total, "date", date_pairs(chips, 1))
        across = lax.ppermute(total, "date", [(2 * a + c, 6 - 2 * a + c) for a in (1, 2) for c in range(2)])
        (message,) = call(pair_body, [((1, *plane), f32)], total, message, near)
        far = lax.ppermute(message, "date", date_pairs(chips, 2))
        given, turn = [near, far, beside, across], [beside, across]
        join = lambda *refs: joined_four(*refs[:4])
    else:
        for step in range(rounds):
            got = lax.ppermute(message, "date", date_pairs(chips, 1 << step))
            if step + 1 == rounds:
                break
            body = functools.partial(merge_body, step, rounds)
            if state is None:
                body = lambda a, b, c, *o, body=body: body(a, b, None, c, *o)
            operands = [level, total, got] if state is None else [level, total, state, got]
            group = [(plane, f32)] * (0 if step + 2 == rounds else 2)
            state, message, *group = call(
                body, [((4, *plane), f32), ((sizes[step + 1], *plane), f32)] + group, *operands
            )
            level, total = group or (level, total)
        given, turn = [x for x in (state, got) if x is not None], [message]

        def join(*refs, joined=joined):
            *refs, zero = refs
            held = refs[0] if state is not None else None
            return joined(rounds, held, refs[-1] if got is not None else None, zero)

    (columns,) = call(
        functools.partial(columns_body, chips),
        [((width // 2, 2 * dates * paths), bf16)],
        held,
        columns_got,
        *turn,
        unread=len(turn),
        flops=1 << 27,
    )
    (tail,) = call(
        functools.partial(tail_body, join),
        [((2 * dates * half + STAT_ROWS, contracts), f32)],
        score,
        own_level,
        own_total,
        *given,
        columns,
        unread=1,
    )
    tail_other = lax.ppermute(tail, "date", cores)
    steps = count.bit_length() - 1
    assert count == 1 << steps and steps > 0
    shares = (chips - chips // 4, chips // 4) if chips >= 4 else (chips,)

    def piece(n, chips):
        return ((chips * n * rows + STAT_ROWS, contracts), f32)

    (begun,) = call(
        functools.partial(first_body, -1.0 / paths_total),
        [((width // 2, contracts), f32)],
        columns,
        tail,
        flops=dates * paths * width * contracts,
    )
    sent = [
        call(
            functools.partial(product_body, -1.0 / paths_total, sum(shares[:part])),
            [piece(count // 2, share)] * 2,
            columns,
            begun,
            tail,
            tail_other,
            scratch=[pltpu.VMEM((share, count, rows, contracts), f32)],
            flops=dates * paths * width * contracts * share // chips,
        )
        for part, share in enumerate(shares)
    ]
    for step in range(steps):
        sent = [(keep, lax.ppermute(m, ("date", "path"), path_pairs(chips, count, step))) for keep, m in sent]
        if step + 1 == steps:
            break
        n = count >> (step + 1)
        sent = [
            call(
                functools.partial(path_sum_body, step + 1),
                [piece(n // 2, share)] * 2,
                *pair,
                scratch=[pltpu.VMEM((share, n, rows, contracts), f32)],
            )
            for share, pair in zip(shares, sent)
        ]
    pieces = call(
        functools.partial(chip_sum_body, chips, shares),
        [((rows + (STAT_ROWS if j in (0, chips // 2) else 0), contracts), f32) for j in range(chips)],
        *[x for pair in sent for x in pair],
        scratch=[pltpu.VMEM(*piece(1, chips))],
    )
    over = {j: lax.ppermute(pieces[j], "date", date_pairs(chips, j)) for j in chip_order(chips)}
    pieces = [pieces[0]] + list(over.values())
    gradient, bound, spread = call(
        functools.partial(date_sum_body, chips, paths_total),
        [((rows, contracts), f32), ((1, contracts), f32), ((1, contracts), f32)],
        *pieces,
    )
    return gradient, bound.reshape(contracts), spread.reshape(contracts)


def solution(mesh):
    placed = (P("date", "path", None), P("date", "path", None), P(), P("date", None))
    return jax.shard_map(
        shards,
        mesh=mesh,
        in_specs=placed,
        out_specs=(P(("date", "path"), None), P(), P()),
        check_vma=False,
    )
```

time: 44.6 us -> 43.3 us (0.971)
  waiting for transfers between devices: 23 us -> 19.5 us
  Pallas kernels: 4.47 us -> 5.67 us
  starting transfers between devices: 16.2 us -> 17.2 us
    ppermute x2 -> x4, waiting for transfers between devices: 6.89 us -> 4.53 us  [the longest x1 2.88 us: shards(): far = lax.ppermute(message, 'date', date_pairs(chips, 2))]
    ppermute x2 -> x4, starting transfers between devices: 5.54 us -> 7.1 us  [the longest x1 3.4 us: shards(): far = lax.ppermute(message, 'date', date_pairs(chips, 2))]
    pallas_call x12 -> x14, Pallas kernels: 4.47 us -> 5.67 us  [call(): pl.pallas_call(kernel, out_shape=[jax.ShapeDtypeStruct(*o) for o in outs]...]
    ppermute x1, waiting for transfers between devices: 1.16 us -> 0.01 us  [shards(): other = lax.ppermute(send, 'date', cores)]
  transfers between devices with their start and end apart: 12 -> 14, of which waited for: 9 -> 7; matrix products, arithmetic and copies ran while one was open for 0% -> 0% of each run, Pallas kernels for 2% -> 6%
where the time goes in v4:
time: 43.3 us; the launch traced here: 43.1 us
  waiting for transfers between devices  19.5 us (45%)
  starting transfers between devices  17.2 us (40%)
  Pallas kernels  5.67 us (13%)
  between operations  0.75 us (2%)
    ppermute x4, waiting for transfers between devices, shards(): lax.ppermute(m, ('date', 'path'), path_pairs(chips, count, step))  9.11 us
    pallas_call x14, Pallas kernels, call(): pl.pallas_call(kernel, out_shape=[jax.ShapeDtypeStruct(*o) for o in outs]...  5.67 us
    ppermute x4, starting transfers between devices, shards(): lax.ppermute(m, ('date', 'path'), path_pairs(chips, count, step))  5.19 us
    ppermute x3, waiting for transfers between devices, shards(): lax.ppermute(pieces[j], 'date', date_pairs(chips, j))  4.64 us
    ppermute x3, starting transfers between devices, shards(): lax.ppermute(pieces[j], 'date', date_pairs(chips, j))  4.21 us
    ppermute x1, starting transfers between devices, shards(): far = lax.ppermute(message, 'date', date_pairs(chips, 2))  3.4 us
    ppermute x1, starting transfers between devices, shards(): near = lax.ppermute(message, 'date', date_pairs(chips, 1))  3.01 us
    ppermute x1, waiting for transfers between devices, shards(): far = lax.ppermute(message, 'date', date_pairs(chips, 2))  2.88 us
  transfers between devices with their start and end apart: 14, of which 7 were waited for; matrix products, arithmetic and copies ran while one was open for 0% of the time, Pallas kernels for 6%

profile of v4, /device:TPU:0, one launch (start us, length us, event | category | flops | bytes accessed | tf_op | source)
XLA Modules:
  0.0 43.1 jit_solution(10301114584143513847)
XLA Ops:
  0.6 1.8 %shard_map.67 = (f32[4,64,256]{2,1,0:T(8,128)S(1)}, bf16[2,64,2048]{2,1,0:T(8,128)(2,1)S(1)}, bf16[2048,256]{1,0:T(8,128)(2,1)S(1)}) custom-call(bf16[2,128,2048]{2,1,0:T(8,128)(2,1)} %refs_0_.3, bf16[2048,256]{1,0:T(8,128)(2,1)} %refs_1_.2, f32[2,128,256]{2,1,0:T(8,128)} %refs_1_.3, s32[2,256]{1,0:T(2,128)} %refs_2_.3), custom_call_target="tpu_custom_call" | custom-call | tf_op jit(solution)/shard_map/pallas_call | solution.py:42
  2.4 0.5 %collective-permute-start = (f32[4,64,256]{2,1,0:T(8,128)S(1)}, f32[4,64,256]{2,1,0:T(8,128)S(1)}, u32[]{:S(2)}, u32[]{:S(2)}) collective-permute-start(f32[4,64,256]{2,1,0:T(8,128)S(1)} %get-tuple-element.31), channel_id=1, source_target_pairs={{0,4},{4,0},{8,12},{12,8},{16,20},{20,16},{24,28},{28,24},{1,5},{5... | collective-permute-start | bytes 786440 | tf_op jit(solution)/shard_map/ppermute | solution.py:378
  3.0 1.4 %shard_map.68 = (f32[4,64,256]{2,1,0:T(8,128)S(1)}, bf16[2,128,2048]{2,1,0:T(8,128)(2,1)S(1)}) custom-call(bf16[2,128,2048]{2,1,0:T(8,128)(2,1)} %refs_0_.3, f32[2,128,256]{2,1,0:T(8,128)} %refs_1_.3, s32[2,256]{1,0:T(2,128)} %refs_2_.3, bf16[2048,256]{1,0:T(8,128)(2,1)S(1)} %get-tuple-element.27.refs_3_, bf16[2,64,2048]{2,1,0:T(8,128)(2,1)S(1)} %get-tuple-element.28.refs_4_), custom_call_target="tpu_custom_call" | custom-call | tf_op jit(solution)/shard_map/pallas_call | solution.py:42
  4.4 0.0 collective-permute-done.refs_1_
  4.4 0.1 shard_map.69
  4.6 0.1 shard_map.70
  4.7 0.1 collective-permute-start.1
  4.8 3.0 %collective-permute-start.4 = (f32[1,64,256]{2,1,0:T(8,128)S(1)}, f32[1,64,256]{2,1,0:T(8,128)S(1)}, u32[]{:S(2)}, u32[]{:S(2)}) collective-permute-start(f32[1,64,256]{2,1,0:T(8,128)S(1)} %get-tuple-element.32.refs_1_), channel_id=1, source_target_pairs={{0,8},{4,12},{8,0},{12,4},{16,24},{20,28},{24,16},{28,20},{1,9},{5... | collective-permute-start | bytes 196616 | tf_op jit(solution)/shard_map/ppermute | solution.py:409
  7.8 0.0 collective-permute-start.2
  7.9 0.7 %collective-permute-start.3 = (f32[64,256]{1,0:T(8,128)S(1)}, f32[64,256]{1,0:T(8,128)S(1)}, u32[]{:S(2)}, u32[]{:S(2)}) collective-permute-start(f32[64,256]{1,0:T(8,128)S(1)} %get-tuple-element.33.refs_0_.refs_2_), channel_id=1, source_target_pairs={{8,16},{12,20},{16,8},{20,12},{9,17},{13,21},{17,9},{21,13},{10,18... | collective-permute-start | bytes 196616 | tf_op jit(solution)/shard_map/ppermute | solution.py:411
  8.5 1.6 %collective-permute-done.4.refs_2_.refs_3_ = f32[1,64,256]{2,1,0:T(8,128)S(1)} collective-permute-done((f32[1,64,256]{2,1,0:T(8,128)S(1)}, f32[1,64,256]{2,1,0:T(8,128)S(1)}, u32[]{:S(2)}, u32[]{:S(2)}) %collective-permute-start.4) | collective-permute-done | bytes 65568 | tf_op jit(solution)/shard_map/ppermute | solution.py:409
  10.2 3.4 %collective-permute-start.5 = (f32[1,64,256]{2,1,0:T(8,128)S(1)}, f32[1,64,256]{2,1,0:T(8,128)S(1)}, u32[]{:S(2)}, u32[]{:S(2)}) collective-permute-start(f32[1,64,256]{2,1,0:T(8,128)S(1)} %shard_map.72), channel_id=1, source_target_pairs={{0,16},{4,20},{8,24},{12,28},{16,0},{20,4},{24,8},{28,12},{1,17},{... | collective-permute-start | bytes 196616 | tf_op jit(solution)/shard_map/ppermute | solution.py:413
  13.6 0.0 collective-permute-done.2.refs_2_.refs_5_
  13.6 0.0 collective-permute-done.3.refs_3_.refs_6_
  13.6 0.0 collective-permute-done.1.refs_1_
  13.6 0.3 shard_map.71.refs_7_.refs_0_
  14.0 2.9 %collective-permute-done.5.refs_4_ = f32[1,64,256]{2,1,0:T(8,128)S(1)} collective-permute-done((f32[1,64,256]{2,1,0:T(8,128)S(1)}, f32[1,64,256]{2,1,0:T(8,128)S(1)}, u32[]{:S(2)}, u32[]{:S(2)}) %collective-permute-start.5) | collective-permute-done | bytes 65568 | tf_op jit(solution)/shard_map/ppermute | solution.py:413
  16.8 0.2 shard_map.73.refs_1_.refs_2_
  17.0 0.1 collective-permute-start.6
  17.1 0.3 shard_map.74.refs_1_
  17.4 1.2 %collective-permute-done.6.refs_3_ = f32[264,256]{1,0:T(8,128)S(1)} collective-permute-done((f32[264,256]{1,0:T(8,128)S(1)}, f32[264,256]{1,0:T(8,128)S(1)}, u32[]{:S(2)}, u32[]{:S(2)}) %collective-permute-start.6) | collective-permute-done | bytes 270368 | tf_op jit(solution)/shard_map/ppermute | solution.py:456
  18.6 0.3 shard_map.75
  19.0 1.6 %collective-permute-start.7 = (f32[392,256]{1,0:T(8,128)S(1)}, f32[392,256]{1,0:T(8,128)S(1)}, u32[]{:S(2)}, u32[]{:S(2)}) collective-permute-start(f32[392,256]{1,0:T(8,128)S(1)} %get-tuple-element.37), channel_id=1, source_target_pairs={{0,1},{1,0},{2,3},{3,2},{4,6},{5,7},{6,4},{7,5},{8,9},{9,8},{10,11... | collective-permute-start | bytes 1204232 | tf_op jit(solution)/shard_map/ppermute | solution.py:485
  20.5 0.2 shard_map.77
  20.8 0.6 %collective-permute-start.9 = (f32[136,256]{1,0:T(8,128)S(1)}, f32[136,256]{1,0:T(8,128)S(1)}, u32[]{:S(2)}, u32[]{:S(2)}) collective-permute-start(f32[136,256]{1,0:T(8,128)S(1)} %get-tuple-element.41), channel_id=1, source_target_pairs={{0,1},{1,0},{2,3},{3,2},{4,6},{5,7},{6,4},{7,5},{8,9},{9,8},{10,11... | collective-permute-start | bytes 417800 | tf_op jit(solution)/shard_map/ppermute | solution.py:485
  21.3 5.6 %collective-permute-done.7.refs_1_ = f32[392,256]{1,0:T(8,128)S(1)} collective-permute-done((f32[392,256]{1,0:T(8,128)S(1)}, f32[392,256]{1,0:T(8,128)S(1)}, u32[]{:S(2)}, u32[]{:S(2)}) %collective-permute-start.7) | collective-permute-done | bytes 401440 | tf_op jit(solution)/shard_map/ppermute | solution.py:485
  26.9 0.1 shard_map.76
  27.0 1.6 %collective-permute-start.8 = (f32[200,256]{1,0:T(8,128)S(1)}, f32[200,256]{1,0:T(8,128)S(1)}, u32[]{:S(2)}, u32[]{:S(2)}) collective-permute-start(f32[200,256]{1,0:T(8,128)S(1)} %get-tuple-element.39), channel_id=1, source_target_pairs={{0,2},{1,3},{2,0},{3,1},{4,5},{5,4},{6,7},{7,6},{8,10},{9,11},{10,... | collective-permute-start | bytes 614408 | tf_op jit(solution)/shard_map/ppermute | solution.py:485
  28.6 0.0 collective-permute-done.9.refs_1_
  28.6 1.4 %collective-permute-start.10 = (f32[72,256]{1,0:T(8,128)S(1)}, f32[72,256]{1,0:T(8,128)S(1)}, u32[]{:S(2)}, u32[]{:S(2)}) collective-permute-start(f32[72,256]{1,0:T(8,128)S(1)} %get-tuple-element.43), channel_id=1, source_target_pairs={{0,2},{1,3},{2,0},{3,1},{4,5},{5,4},{6,7},{7,6},{8,10},{9,11},{10,... | collective-permute-start | bytes 221192 | tf_op jit(solution)/shard_map/ppermute | solution.py:485
  30.0 3.6 %collective-permute-done.10.refs_3_ = f32[72,256]{1,0:T(8,128)S(1)} collective-permute-done((f32[72,256]{1,0:T(8,128)S(1)}, f32[72,256]{1,0:T(8,128)S(1)}, u32[]{:S(2)}, u32[]{:S(2)}) %collective-permute-start.10) | collective-permute-done | bytes 73760 | tf_op jit(solution)/shard_map/ppermute | solution.py:485
  33.6 0.0 collective-permute-done.8.refs_1_
  33.6 0.1 shard_map.79
  33.6 2.0 %collective-permute-start.11 = (f32[72,256]{1,0:T(8,128)S(1)}, f32[72,256]{1,0:T(8,128)S(1)}, u32[]{:S(2)}, u32[]{:S(2)}) collective-permute-start(f32[72,256]{1,0:T(8,128)S(1)} %get-tuple-element.45), channel_id=1, source_target_pairs={{0,16},{4,20},{8,24},{12,28},{16,0},{20,4},{24,8},{28,12},{1,17},{... | collective-permute-start | bytes 221192 | tf_op jit(solution)/shard_map/ppermute | solution.py:504
  35.7 2.2 %collective-permute-start.12 = (f32[64,256]{1,0:T(8,128)S(1)}, f32[64,256]{1,0:T(8,128)S(1)}, u32[]{:S(2)}, u32[]{:S(2)}) collective-permute-start(f32[64,256]{1,0:T(8,128)S(1)} %get-tuple-element.46), channel_id=1, source_target_pairs={{0,24},{4,28},{8,16},{12,20},{16,8},{20,12},{24,0},{28,4},{1,25},{... | collective-permute-start | bytes 196616 | tf_op jit(solution)/shard_map/ppermute | solution.py:504
  37.8 0.0 collective-permute-start.13
  37.9 4.0 %collective-permute-done.12.refs_2_ = f32[64,256]{1,0:T(8,128)S(1)} collective-permute-done((f32[64,256]{1,0:T(8,128)S(1)}, f32[64,256]{1,0:T(8,128)S(1)}, u32[]{:S(2)}, u32[]{:S(2)}) %collective-permute-start.12) | collective-permute-done | bytes 65568 | tf_op jit(solution)/shard_map/ppermute | solution.py:504
  41.8 0.7 %collective-permute-done.13.refs_3_ = f32[64,256]{1,0:T(8,128)S(1)} collective-permute-done((f32[64,256]{1,0:T(8,128)S(1)}, f32[64,256]{1,0:T(8,128)S(1)}, u32[]{:S(2)}, u32[]{:S(2)}) %collective-permute-start.13) | collective-permute-done | bytes 65568 | tf_op jit(solution)/shard_map/ppermute | solution.py:504
  42.5 0.0 collective-permute-done.11.refs_1_
  42.5 0.7 %shard_map.80 = (f32[64,256]{1,0:T(8,128)}, f32[1,256]{1,0:T(1,128)}, f32[1,256]{1,0:T(1,128)}) custom-call(f32[72,256]{1,0:T(8,128)S(1)} %get-tuple-element.44.refs_0_, f32[72,256]{1,0:T(8,128)S(1)} %collective-permute-done.11.refs_1_, f32[64,256]{1,0:T(8,128)S(1)} %collective-permute-done.12.refs_2_, f32[64,256]{1,0:T(8,128)S(1)} %collective-permute-done.13.refs_3_), custom_call_target="tpu_custom_call" | custom-call | tf_op jit(solution)/shard_map/pallas_call | solution.py:42
  (2 shorter events, 0.1 us)
Async XLA Ops:
  2.4 2.0 %collective-permute-start = (f32[4,64,256]{2,1,0:T(8,128)S(1)}, f32[4,64,256]{2,1,0:T(8,128)S(1)}, u32[]{:S(2)}, u32[]{:S(2)}) collective-permute-start(f32[4,64,256]{2,1,0:T(8,128)S(1)} %get-tuple-element.31), channel_id=1, source_target_pairs={{0,4},{4,0},{8,12},{12,8},{16,20},{20,16},{24,28},{28,24},{1,5},{5... | collective-permute-start | bytes 786440 | tf_op jit(solution)/shard_map/ppermute | solution.py:378
  4.7 8.9 %collective-permute-start.1 = (f32[2,128,1024]{2,1,0:T(8,128)S(1)}, f32[2,128,1024]{2,1,0:T(8,128)S(1)}, u32[]{:S(2)}, u32[]{:S(2)}) collective-permute-start(f32[2,128,1024]{2,1,0:T(8,128)S(1)} %shard_map.70), channel_id=1, source_target_pairs={{0,4},{4,0},{8,12},{12,8},{16,20},{20,16},{24,28},{28,24},{1,5},{5... | collective-permute-start | bytes 3145736 | tf_op jit(solution)/shard_map/ppermute | solution.py:406
  4.8 5.3 %collective-permute-start.4 = (f32[1,64,256]{2,1,0:T(8,128)S(1)}, f32[1,64,256]{2,1,0:T(8,128)S(1)}, u32[]{:S(2)}, u32[]{:S(2)}) collective-permute-start(f32[1,64,256]{2,1,0:T(8,128)S(1)} %get-tuple-element.32.refs_1_), channel_id=1, source_target_pairs={{0,8},{4,12},{8,0},{12,4},{16,24},{20,28},{24,16},{28,20},{1,9},{5... | collective-permute-start | bytes 196616 | tf_op jit(solution)/shard_map/ppermute | solution.py:409
  7.8 5.8 %collective-permute-start.2 = (f32[64,256]{1,0:T(8,128)S(1)}, f32[64,256]{1,0:T(8,128)S(1)}, u32[]{:S(2)}, u32[]{:S(2)}) collective-permute-start(f32[64,256]{1,0:T(8,128)S(1)} %get-tuple-element.33.refs_0_.refs_2_), channel_id=1, source_target_pairs={{0,8},{4,12},{8,0},{12,4},{16,24},{20,28},{24,16},{28,20},{1,9},{5... | collective-permute-start | bytes 196616 | tf_op jit(solution)/shard_map/ppermute | solution.py:410
  7.9 5.8 %collective-permute-start.3 = (f32[64,256]{1,0:T(8,128)S(1)}, f32[64,256]{1,0:T(8,128)S(1)}, u32[]{:S(2)}, u32[]{:S(2)}) collective-permute-start(f32[64,256]{1,0:T(8,128)S(1)} %get-tuple-element.33.refs_0_.refs_2_), channel_id=1, source_target_pairs={{8,16},{12,20},{16,8},{20,12},{9,17},{13,21},{17,9},{21,13},{10,18... | collective-permute-start | bytes 196616 | tf_op jit(solution)/shard_map/ppermute | solution.py:411
  10.2 6.6 %collective-permute-start.5 = (f32[1,64,256]{2,1,0:T(8,128)S(1)}, f32[1,64,256]{2,1,0:T(8,128)S(1)}, u32[]{:S(2)}, u32[]{:S(2)}) collective-permute-start(f32[1,64,256]{2,1,0:T(8,128)S(1)} %shard_map.72), channel_id=1, source_target_pairs={{0,16},{4,20},{8,24},{12,28},{16,0},{20,4},{24,8},{28,12},{1,17},{... | collective-permute-start | bytes 196616 | tf_op jit(solution)/shard_map/ppermute | solution.py:413
  17.0 1.6 %collective-permute-start.6 = (f32[264,256]{1,0:T(8,128)S(1)}, f32[264,256]{1,0:T(8,128)S(1)}, u32[]{:S(2)}, u32[]{:S(2)}) collective-permute-start(f32[264,256]{1,0:T(8,128)S(1)} %shard_map.73.refs_1_.refs_2_), channel_id=1, source_target_pairs={{0,4},{4,0},{8,12},{12,8},{16,20},{20,16},{24,28},{28,24},{1,5},{5... | collective-permute-start | bytes 811016 | tf_op jit(solution)/shard_map/ppermute | solution.py:456
  19.0 7.9 %collective-permute-start.7 = (f32[392,256]{1,0:T(8,128)S(1)}, f32[392,256]{1,0:T(8,128)S(1)}, u32[]{:S(2)}, u32[]{:S(2)}) collective-permute-start(f32[392,256]{1,0:T(8,128)S(1)} %get-tuple-element.37), channel_id=1, source_target_pairs={{0,1},{1,0},{2,3},{3,2},{4,6},{5,7},{6,4},{7,5},{8,9},{9,8},{10,11... | collective-permute-start | bytes 1204232 | tf_op jit(solution)/shard_map/ppermute | solution.py:485
  20.8 7.8 %collective-permute-start.9 = (f32[136,256]{1,0:T(8,128)S(1)}, f32[136,256]{1,0:T(8,128)S(1)}, u32[]{:S(2)}, u32[]{:S(2)}) collective-permute-start(f32[136,256]{1,0:T(8,128)S(1)} %get-tuple-element.41), channel_id=1, source_target_pairs={{0,1},{1,0},{2,3},{3,2},{4,6},{5,7},{6,4},{7,5},{8,9},{9,8},{10,11... | collective-permute-start | bytes 417800 | tf_op jit(solution)/shard_map/ppermute | solution.py:485
  27.0 6.6 %collective-permute-start.8 = (f32[200,256]{1,0:T(8,128)S(1)}, f32[200,256]{1,0:T(8,128)S(1)}, u32[]{:S(2)}, u32[]{:S(2)}) collective-permute-start(f32[200,256]{1,0:T(8,128)S(1)} %get-tuple-element.39), channel_id=1, source_target_pairs={{0,2},{1,3},{2,0},{3,1},{4,5},{5,4},{6,7},{7,6},{8,10},{9,11},{10,... | collective-permute-start | bytes 614408 | tf_op jit(solution)/shard_map/ppermute | solution.py:485
  28.6 5.0 %collective-permute-start.10 = (f32[72,256]{1,0:T(8,128)S(1)}, f32[72,256]{1,0:T(8,128)S(1)}, u32[]{:S(2)}, u32[]{:S(2)}) collective-permute-start(f32[72,256]{1,0:T(8,128)S(1)} %get-tuple-element.43), channel_id=1, source_target_pairs={{0,2},{1,3},{2,0},{3,1},{4,5},{5,4},{6,7},{7,6},{8,10},{9,11},{10,... | collective-permute-start | bytes 221192 | tf_op jit(solution)/shard_map/ppermute | solution.py:485
  33.6 8.9 %collective-permute-start.11 = (f32[72,256]{1,0:T(8,128)S(1)}, f32[72,256]{1,0:T(8,128)S(1)}, u32[]{:S(2)}, u32[]{:S(2)}) collective-permute-start(f32[72,256]{1,0:T(8,128)S(1)} %get-tuple-element.45), channel_id=1, source_target_pairs={{0,16},{4,20},{8,24},{12,28},{16,0},{20,4},{24,8},{28,12},{1,17},{... | collective-permute-start | bytes 221192 | tf_op jit(solution)/shard_map/ppermute | solution.py:504
  35.7 6.1 %collective-permute-start.12 = (f32[64,256]{1,0:T(8,128)S(1)}, f32[64,256]{1,0:T(8,128)S(1)}, u32[]{:S(2)}, u32[]{:S(2)}) collective-permute-start(f32[64,256]{1,0:T(8,128)S(1)} %get-tuple-element.46), channel_id=1, source_target_pairs={{0,24},{4,28},{8,16},{12,20},{16,8},{20,12},{24,0},{28,4},{1,25},{... | collective-permute-start | bytes 196616 | tf_op jit(solution)/shard_map/ppermute | solution.py:504
  37.8 4.6 %collective-permute-start.13 = (f32[64,256]{1,0:T(8,128)S(1)}, f32[64,256]{1,0:T(8,128)S(1)}, u32[]{:S(2)}, u32[]{:S(2)}) collective-permute-start(f32[64,256]{1,0:T(8,128)S(1)} %get-tuple-element.47), channel_id=1, source_target_pairs={{0,8},{4,12},{8,0},{12,4},{16,24},{20,28},{24,16},{28,20},{1,9},{5... | collective-permute-start | bytes 196616 | tf_op jit(solution)/shard_map/ppermute | solution.py:504

commit v5 on v4

--- a/solution.py
+++ b/solution.py
@@ -13,6 +13,7 @@
 STAT_ROWS = 8
 PIECES = 2
 FIRST = 4
+FIRST_ROWS = 5
 VMEM_LIMIT = 16 << 20
 f32 = jnp.float32
 bf16 = jnp.bfloat16
@@ -247,16 +248,20 @@
         out[rows, :] = scale * jnp.dot(side(columns, rows, core_of()), right, preferred_element_type=f32)
 
 
-def product_body(scale, first_chip, columns, begun, own, got, keep, message, product):
+def product_body(scale, cuts, columns, begun, own, got, *refs):
+    *outs, product = refs
     size = columns.shape[1] // 2
     right = got[:size, :].astype(bf16)
     chips, count, rows, contracts = product.shape
     width = count * rows
     for z in range(chips):
-        at = slice((first_chip + z) * width, (first_chip + z + 1) * width)
+        at = slice(z * width, (z + 1) * width)
         block = scale * jnp.dot(side(columns, at, 1 - core_of()), right, preferred_element_type=f32)
         product[z] = (begun[at, :] + block).reshape(count, rows, contracts)
-    halve(0, product, own[size:, :] + got[size:, :], keep, message)
+    stats = own[size:, :] + got[size:, :]
+    for part, cut in enumerate(cuts):
+        last = part + 1 == len(cuts)
+        halve(0, product, cut, stats if last else None, *outs[2 * part : 2 * part + 2])
 
 
 def path_bits(count):
@@ -264,8 +269,9 @@
     return bits, bits[len(bits) // 2 :] + bits[: len(bits) // 2]
 
 
-def halve(step, product, stats, keep, message):
-    chips, n, rows, _ = product.shape
+def halve(step, product, cut, stats, keep, message):
+    chips, n, _, _ = product.shape
+    rows = cut.stop - cut.start
     first, second = path_bits(lax.axis_size("path"))
     bit, place = (
         jnp.where(core_of() == 0, a, b)
@@ -281,8 +287,9 @@
                 low = i & ((1 << place) - 1)
                 at = ((i - low) << 1) + (value << place) + low
                 start = (z * (n // 2) + i) * rows
-                out[start : start + rows, :] = product[z, at]
-        out[chips * (n // 2) * rows :, :] = stats
+                out[start : start + rows, :] = product[z, at, cut, :]
+        if stats is not None:
+            out[chips * (n // 2) * rows :, :] = stats
 
 
 def path_pairs(chips, count, step):
@@ -296,10 +303,11 @@
 
 
 def path_sum_body(step, mine, got, keep, message, product):
-    chips, n, rows, contracts = product.shape
+    chips, n, rows, _ = product.shape
     size = chips * n * rows
     product[...] = (mine[:size, :] + got[:size, :]).reshape(product.shape)
-    halve(step, product, mine[size:, :] + got[size:, :], keep, message)
+    stats = mine[size:, :] + got[size:, :] if mine.shape[0] > size else None
+    halve(step, product, slice(0, rows), stats, keep, message)
 
 
 def partner(me, j, count):
@@ -318,16 +326,21 @@
     return [(2 * a + core, 2 * b + core) for a, b in pairs(chips, j) for core in range(2)]
 
 
-def chip_sum_body(chips, shares, *refs):
+def inner_pairs():
+    inner = [(2 * a + c, 6 - 2 * a + c) for a in (1, 2) for c in range(2)]
+    return inner + [(2 * a + c, 2 * a + 1 - c) for a in (0, 3) for c in range(2)]
+
+
+def chip_sum_body(chips, cuts, *refs):
     given, (keep, *messages), (total,) = refs[: -chips - 1], refs[-chips - 1 : -1], refs[-1:]
     rows = (total.shape[0] - STAT_ROWS) // chips
-    at = 0
-    for part, share in enumerate(shares):
+    for part, cut in enumerate(cuts):
         mine, got = given[2 * part : 2 * part + 2]
-        size = share * rows
-        total[at : at + size, :] = mine[:size, :] + got[:size, :]
-        at += size
-    total[at:, :] = mine[size:, :] + got[size:, :]
+        share = cut.stop - cut.start
+        for z in range(chips):
+            at = slice(z * share, (z + 1) * share)
+            total[z * rows + cut.start : z * rows + cut.stop, :] = mine[at, :] + got[at, :]
+    total[chips * rows :, :] = mine[chips * share :, :] + got[chips * share :, :]
     for j, out in enumerate((keep, *messages)):
         at = pl.multiple_of(partner(chip_of(), j, chips) * rows, rows)
         out[0:rows, :] = total[pl.ds(at, rows), :]
@@ -408,7 +421,7 @@
     if rounds == 2:
         near = lax.ppermute(message, "date", date_pairs(chips, 1))
         beside = lax.ppermute(total, "date", date_pairs(chips, 1))
-        across = lax.ppermute(total, "date", [(2 * a + c, 6 - 2 * a + c) for a in (1, 2) for c in range(2)])
+        across = lax.ppermute(total, "date", inner_pairs())
         (message,) = call(pair_body, [((1, *plane), f32)], total, message, near)
         far = lax.ppermute(message, "date", date_pairs(chips, 2))
         given, turn = [near, far, beside, across], [beside, across]
@@ -456,10 +469,12 @@
     tail_other = lax.ppermute(tail, "date", cores)
     steps = count.bit_length() - 1
     assert count == 1 << steps and steps > 0
-    shares = (chips - chips // 4, chips // 4) if chips >= 4 else (chips,)
-
-    def piece(n, chips):
-        return ((chips * n * rows + STAT_ROWS, contracts), f32)
+    first = rows * FIRST_ROWS // 8 // 8 * 8
+    cuts = [slice(0, first), slice(first, rows)] if first else [slice(0, rows)]
+
+    def piece(n, cut):
+        stats = STAT_ROWS if cut is cuts[-1] else 0
+        return ((chips * n * (cut.stop - cut.start) + stats, contracts), f32)
 
     (begun,) = call(
         functools.partial(first_body, -1.0 / paths_total),
@@ -468,19 +483,17 @@
         tail,
         flops=dates * paths * width * contracts,
     )
-    sent = [
-        call(
-            functools.partial(product_body, -1.0 / paths_total, sum(shares[:part])),
-            [piece(count // 2, share)] * 2,
-            columns,
-            begun,
-            tail,
-            tail_other,
-            scratch=[pltpu.VMEM((share, count, rows, contracts), f32)],
-            flops=dates * paths * width * contracts * share // chips,
-        )
-        for part, share in enumerate(shares)
-    ]
+    outs = call(
+        functools.partial(product_body, -1.0 / paths_total, cuts),
+        [piece(count // 2, cut) for cut in cuts for _ in range(2)],
+        columns,
+        begun,
+        tail,
+        tail_other,
+        scratch=[pltpu.VMEM((chips, count, rows, contracts), f32)],
+        flops=dates * paths * width * contracts,
+    )
+    sent = [outs[2 * part : 2 * part + 2] for part in range(len(cuts))]
     for step in range(steps):
         sent = [(keep, lax.ppermute(m, ("date", "path"), path_pairs(chips, count, step))) for keep, m in sent]
         if step + 1 == steps:
@@ -489,17 +502,17 @@
         sent = [
             call(
                 functools.partial(path_sum_body, step + 1),
-                [piece(n // 2, share)] * 2,
+                [piece(n // 2, cut)] * 2,
                 *pair,
-                scratch=[pltpu.VMEM((share, n, rows, contracts), f32)],
+                scratch=[pltpu.VMEM((chips, n, cut.stop - cut.start, contracts), f32)],
             )
-            for share, pair in zip(shares, sent)
+            for cut, pair in zip(cuts, sent)
         ]
     pieces = call(
-        functools.partial(chip_sum_body, chips, shares),
+        functools.partial(chip_sum_body, chips, cuts),
         [((rows + (STAT_ROWS if j in (0, chips // 2) else 0), contracts), f32) for j in range(chips)],
         *[x for pair in sent for x in pair],
-        scratch=[pltpu.VMEM(*piece(1, chips))],
+        scratch=[pltpu.VMEM((chips * rows + STAT_ROWS, contracts), f32)],
     )
     over = {j: lax.ppermute(pieces[j], "date", date_pairs(chips, j)) for j in chip_order(chips)}
     pieces = [pieces[0]] + list(over.values())

time: 43.3 us -> 42.8 us (0.988)
  waiting for transfers between devices: 19.5 us -> 18 us
  starting transfers between devices: 17.2 us -> 18.4 us
    ppermute x3, starting transfers between devices: 4.21 us -> 5.25 us  [shards(): lax.ppermute(pieces[j], 'date', date_pairs(chips, j))]
    ppermute x4, waiting for transfers between devices: 9.11 us -> 8.1 us  [shards(): lax.ppermute(m, ('date', 'path'), path_pairs(chips, count, step))]
    ppermute x1, waiting for transfers between devices: 2.88 us -> 1.9 us  [shards(): far = lax.ppermute(message, 'date', date_pairs(chips, 2))]
    ppermute x4, starting transfers between devices: 5.19 us -> 5.98 us  [shards(): lax.ppermute(m, ('date', 'path'), path_pairs(chips, count, step))]
    ppermute x1, waiting for transfers between devices: 1.64 us -> 2.3 us  [shards(): near = lax.ppermute(message, 'date', date_pairs(chips, 1))]
    ppermute x1, starting transfers between devices: 0.65 us -> 0.01 us  [shards(): across = lax.ppermute(total, 'date', inner_pairs())]
    pallas_call x14 -> x13, Pallas kernels: 5.67 us -> 5.52 us  [call(): pl.pallas_call(kernel, out_shape=[jax.ShapeDtypeStruct(*o) for o in outs]...]
  transfers between devices with their start and end apart: 14 -> 14, of which waited for: 7 -> 8; matrix products, arithmetic and copies ran while one was open for 0% -> 0% of each run, Pallas kernels for 6% -> 5%
where the time goes in v5:
time: 42.8 us; the launch traced here: 42.7 us
  starting transfers between devices  18.4 us (43%)
  waiting for transfers between devices  18 us (42%)
  Pallas kernels  5.52 us (13%)
  between operations  0.73 us (2%)
    ppermute x4, waiting for transfers between devices, shards(): lax.ppermute(m, ('date', 'path'), path_pairs(chips, count, step))  8.1 us
    ppermute x4, starting transfers between devices, shards(): lax.ppermute(m, ('date', 'path'), path_pairs(chips, count, step))  5.98 us
    pallas_call x13, Pallas kernels, call(): pl.pallas_call(kernel, out_shape=[jax.ShapeDtypeStruct(*o) for o in outs]...  5.52 us
    ppermute x3, starting transfers between devices, shards(): lax.ppermute(pieces[j], 'date', date_pairs(chips, j))  5.25 us
    ppermute x3, waiting for transfers between devices, shards(): lax.ppermute(pieces[j], 'date', date_pairs(chips, j))  4.48 us
    ppermute x1, starting transfers between devices, shards(): far = lax.ppermute(message, 'date', date_pairs(chips, 2))  3.4 us
    ppermute x1, starting transfers between devices, shards(): near = lax.ppermute(message, 'date', date_pairs(chips, 1))  3.01 us
    ppermute x1, waiting for transfers between devices, shards(): near = lax.ppermute(message, 'date', date_pairs(chips, 1))  2.3 us
  transfers between devices with their start and end apart: 14, of which 8 were waited for; matrix products, arithmetic and copies ran while one was open for 0% of the time, Pallas kernels for 5%

profile of v5, /device:TPU:0, one launch (start us, length us, event | category | flops | bytes accessed | tf_op | source)
XLA Modules:
  0.0 42.7 jit_solution(15734202294498959946)
XLA Ops:
  0.6 1.8 %shard_map.67 = (f32[4,64,256]{2,1,0:T(8,128)S(1)}, bf16[2,64,2048]{2,1,0:T(8,128)(2,1)S(1)}, bf16[2048,256]{1,0:T(8,128)(2,1)S(1)}) custom-call(bf16[2,128,2048]{2,1,0:T(8,128)(2,1)} %refs_0_.3, bf16[2048,256]{1,0:T(8,128)(2,1)} %refs_1_.2, f32[2,128,256]{2,1,0:T(8,128)} %refs_1_.3, s32[2,256]{1,0:T(2,128)} %refs_2_.3), custom_call_target="tpu_custom_call" | custom-call | tf_op jit(solution)/shard_map/pallas_call | solution.py:43
  2.4 0.5 %collective-permute-start = (f32[4,64,256]{2,1,0:T(8,128)S(1)}, f32[4,64,256]{2,1,0:T(8,128)S(1)}, u32[]{:S(2)}, u32[]{:S(2)}) collective-permute-start(f32[4,64,256]{2,1,0:T(8,128)S(1)} %get-tuple-element.31), channel_id=1, source_target_pairs={{0,4},{4,0},{8,12},{12,8},{16,20},{20,16},{24,28},{28,24},{1,5},{5... | collective-permute-start | bytes 786440 | tf_op jit(solution)/shard_map/ppermute | solution.py:391
  3.0 1.4 %shard_map.68 = (f32[4,64,256]{2,1,0:T(8,128)S(1)}, bf16[2,128,2048]{2,1,0:T(8,128)(2,1)S(1)}) custom-call(bf16[2,128,2048]{2,1,0:T(8,128)(2,1)} %refs_0_.3, f32[2,128,256]{2,1,0:T(8,128)} %refs_1_.3, s32[2,256]{1,0:T(2,128)} %refs_2_.3, bf16[2048,256]{1,0:T(8,128)(2,1)S(1)} %get-tuple-element.27.refs_3_, bf16[2,64,2048]{2,1,0:T(8,128)(2,1)S(1)} %get-tuple-element.28.refs_4_), custom_call_target="tpu_custom_call" | custom-call | tf_op jit(solution)/shard_map/pallas_call | solution.py:43
  4.4 0.0 collective-permute-done.refs_1_
  4.4 0.1 shard_map.69
  4.6 0.1 shard_map.70
  4.7 0.1 collective-permute-start.1
  4.8 3.0 %collective-permute-start.4 = (f32[1,64,256]{2,1,0:T(8,128)S(1)}, f32[1,64,256]{2,1,0:T(8,128)S(1)}, u32[]{:S(2)}, u32[]{:S(2)}) collective-permute-start(f32[1,64,256]{2,1,0:T(8,128)S(1)} %get-tuple-element.32.refs_1_), channel_id=1, source_target_pairs={{0,8},{4,12},{8,0},{12,4},{16,24},{20,28},{24,16},{28,20},{1,9},{5... | collective-permute-start | bytes 196616 | tf_op jit(solution)/shard_map/ppermute | solution.py:422
  7.8 0.0 collective-permute-start.2
  7.9 0.0 collective-permute-start.3
  7.9 2.3 %collective-permute-done.4.refs_2_.refs_3_ = f32[1,64,256]{2,1,0:T(8,128)S(1)} collective-permute-done((f32[1,64,256]{2,1,0:T(8,128)S(1)}, f32[1,64,256]{2,1,0:T(8,128)S(1)}, u32[]{:S(2)}, u32[]{:S(2)}) %collective-permute-start.4) | collective-permute-done | bytes 65568 | tf_op jit(solution)/shard_map/ppermute | solution.py:422
  10.2 3.4 %collective-permute-start.5 = (f32[1,64,256]{2,1,0:T(8,128)S(1)}, f32[1,64,256]{2,1,0:T(8,128)S(1)}, u32[]{:S(2)}, u32[]{:S(2)}) collective-permute-start(f32[1,64,256]{2,1,0:T(8,128)S(1)} %shard_map.72), channel_id=1, source_target_pairs={{0,16},{4,20},{8,24},{12,28},{16,0},{20,4},{24,8},{28,12},{1,17},{... | collective-permute-start | bytes 196616 | tf_op jit(solution)/shard_map/ppermute | solution.py:426
  13.6 0.0 collective-permute-done.2.refs_2_.refs_5_
  13.6 0.0 collective-permute-done.3.refs_3_.refs_6_
  13.6 0.0 collective-permute-done.1.refs_1_
  13.6 0.3 shard_map.71.refs_7_.refs_0_
  14.0 1.9 %collective-permute-done.5.refs_4_ = f32[1,64,256]{2,1,0:T(8,128)S(1)} collective-permute-done((f32[1,64,256]{2,1,0:T(8,128)S(1)}, f32[1,64,256]{2,1,0:T(8,128)S(1)}, u32[]{:S(2)}, u32[]{:S(2)}) %collective-permute-start.5) | collective-permute-done | bytes 65568 | tf_op jit(solution)/shard_map/ppermute | solution.py:426
  15.9 0.2 shard_map.73.refs_1_.refs_2_
  16.0 0.1 collective-permute-start.6
  16.1 0.3 shard_map.74.refs_1_
  16.4 1.2 %collective-permute-done.6.refs_3_ = f32[264,256]{1,0:T(8,128)S(1)} collective-permute-done((f32[264,256]{1,0:T(8,128)S(1)}, f32[264,256]{1,0:T(8,128)S(1)}, u32[]{:S(2)}, u32[]{:S(2)}) %collective-permute-start.6) | collective-permute-done | bytes 270368 | tf_op jit(solution)/shard_map/ppermute | solution.py:469
  17.6 0.4 shard_map.75
  18.0 1.9 %collective-permute-start.7 = (f32[320,256]{1,0:T(8,128)S(1)}, f32[320,256]{1,0:T(8,128)S(1)}, u32[]{:S(2)}, u32[]{:S(2)}) collective-permute-start(f32[320,256]{1,0:T(8,128)S(1)} %get-tuple-element.37), channel_id=1, source_target_pairs={{0,1},{1,0},{2,3},{3,2},{4,6},{5,7},{6,4},{7,5},{8,9},{9,8},{10,11... | collective-permute-start | bytes 983048 | tf_op jit(solution)/shard_map/ppermute | solution.py:498
  19.9 0.2 collective-permute-start.9
  20.1 5.0 %collective-permute-done.7.refs_1_ = f32[320,256]{1,0:T(8,128)S(1)} collective-permute-done((f32[320,256]{1,0:T(8,128)S(1)}, f32[320,256]{1,0:T(8,128)S(1)}, u32[]{:S(2)}, u32[]{:S(2)}) %collective-permute-start.7) | collective-permute-done | bytes 327712 | tf_op jit(solution)/shard_map/ppermute | solution.py:498
  25.2 0.1 shard_map.76
  25.2 1.9 %collective-permute-start.8 = (f32[160,256]{1,0:T(8,128)S(1)}, f32[160,256]{1,0:T(8,128)S(1)}, u32[]{:S(2)}, u32[]{:S(2)}) collective-permute-start(f32[160,256]{1,0:T(8,128)S(1)} %get-tuple-element.39), channel_id=1, source_target_pairs={{0,2},{1,3},{2,0},{3,1},{4,5},{5,4},{6,7},{7,6},{8,10},{9,11},{10,... | collective-permute-start | bytes 491528 | tf_op jit(solution)/shard_map/ppermute | solution.py:498
  27.1 0.3 collective-permute-done.9.refs_1_
  27.4 2.0 %collective-permute-start.10 = (f32[104,256]{1,0:T(8,128)S(1)}, f32[104,256]{1,0:T(8,128)S(1)}, u32[]{:S(2)}, u32[]{:S(2)}) collective-permute-start(f32[104,256]{1,0:T(8,128)S(1)} %get-tuple-element.43), channel_id=1, source_target_pairs={{0,2},{1,3},{2,0},{3,1},{4,5},{5,4},{6,7},{7,6},{8,10},{9,11},{10,... | collective-permute-start | bytes 319496 | tf_op jit(solution)/shard_map/ppermute | solution.py:498
  29.4 2.8 %collective-permute-done.10.refs_3_ = f32[104,256]{1,0:T(8,128)S(1)} collective-permute-done((f32[104,256]{1,0:T(8,128)S(1)}, f32[104,256]{1,0:T(8,128)S(1)}, u32[]{:S(2)}, u32[]{:S(2)}) %collective-permute-start.10) | collective-permute-done | bytes 106528 | tf_op jit(solution)/shard_map/ppermute | solution.py:498
  32.2 0.0 collective-permute-done.8.refs_1_
  32.2 0.1 shard_map.78
  32.3 3.1 %collective-permute-start.11 = (f32[72,256]{1,0:T(8,128)S(1)}, f32[72,256]{1,0:T(8,128)S(1)}, u32[]{:S(2)}, u32[]{:S(2)}) collective-permute-start(f32[72,256]{1,0:T(8,128)S(1)} %get-tuple-element.45), channel_id=1, source_target_pairs={{0,16},{4,20},{8,24},{12,28},{16,0},{20,4},{24,8},{28,12},{1,17},{... | collective-permute-start | bytes 221192 | tf_op jit(solution)/shard_map/ppermute | solution.py:517
  35.4 1.6 %collective-permute-start.12 = (f32[64,256]{1,0:T(8,128)S(1)}, f32[64,256]{1,0:T(8,128)S(1)}, u32[]{:S(2)}, u32[]{:S(2)}) collective-permute-start(f32[64,256]{1,0:T(8,128)S(1)} %get-tuple-element.46), channel_id=1, source_target_pairs={{0,24},{4,28},{8,16},{12,20},{16,8},{20,12},{24,0},{28,4},{1,25},{... | collective-permute-start | bytes 196616 | tf_op jit(solution)/shard_map/ppermute | solution.py:517
  37.0 0.5 %collective-permute-start.13 = (f32[64,256]{1,0:T(8,128)S(1)}, f32[64,256]{1,0:T(8,128)S(1)}, u32[]{:S(2)}, u32[]{:S(2)}) collective-permute-start(f32[64,256]{1,0:T(8,128)S(1)} %get-tuple-element.47), channel_id=1, source_target_pairs={{0,8},{4,12},{8,0},{12,4},{16,24},{20,28},{24,16},{28,20},{1,9},{5... | collective-permute-start | bytes 196616 | tf_op jit(solution)/shard_map/ppermute | solution.py:517
  37.5 4.1 %collective-permute-done.12.refs_2_ = f32[64,256]{1,0:T(8,128)S(1)} collective-permute-done((f32[64,256]{1,0:T(8,128)S(1)}, f32[64,256]{1,0:T(8,128)S(1)}, u32[]{:S(2)}, u32[]{:S(2)}) %collective-permute-start.12) | collective-permute-done | bytes 65568 | tf_op jit(solution)/shard_map/ppermute | solution.py:517
  41.6 0.4 collective-permute-done.13.refs_3_
  42.0 0.0 collective-permute-done.11.refs_1_
  42.0 0.7 %shard_map.79 = (f32[64,256]{1,0:T(8,128)}, f32[1,256]{1,0:T(1,128)}, f32[1,256]{1,0:T(1,128)}) custom-call(f32[72,256]{1,0:T(8,128)S(1)} %get-tuple-element.44.refs_0_, f32[72,256]{1,0:T(8,128)S(1)} %collective-permute-done.11.refs_1_, f32[64,256]{1,0:T(8,128)S(1)} %collective-permute-done.12.refs_2_, f32[64,256]{1,0:T(8,128)S(1)} %collective-permute-done.13.refs_3_), custom_call_target="tpu_custom_call" | custom-call | tf_op jit(solution)/shard_map/pallas_call | solution.py:43
  (2 shorter events, 0.1 us)
Async XLA Ops:
  2.4 2.0 %collective-permute-start = (f32[4,64,256]{2,1,0:T(8,128)S(1)}, f32[4,64,256]{2,1,0:T(8,128)S(1)}, u32[]{:S(2)}, u32[]{:S(2)}) collective-permute-start(f32[4,64,256]{2,1,0:T(8,128)S(1)} %get-tuple-element.31), channel_id=1, source_target_pairs={{0,4},{4,0},{8,12},{12,8},{16,20},{20,16},{24,28},{28,24},{1,5},{5... | collective-permute-start | bytes 786440 | tf_op jit(solution)/shard_map/ppermute | solution.py:391
  4.7 8.9 %collective-permute-start.1 = (f32[2,128,1024]{2,1,0:T(8,128)S(1)}, f32[2,128,1024]{2,1,0:T(8,128)S(1)}, u32[]{:S(2)}, u32[]{:S(2)}) collective-permute-start(f32[2,128,1024]{2,1,0:T(8,128)S(1)} %shard_map.70), channel_id=1, source_target_pairs={{0,4},{4,0},{8,12},{12,8},{16,20},{20,16},{24,28},{28,24},{1,5},{5... | collective-permute-start | bytes 3145736 | tf_op jit(solution)/shard_map/ppermute | solution.py:419
  4.8 5.3 %collective-permute-start.4 = (f32[1,64,256]{2,1,0:T(8,128)S(1)}, f32[1,64,256]{2,1,0:T(8,128)S(1)}, u32[]{:S(2)}, u32[]{:S(2)}) collective-permute-start(f32[1,64,256]{2,1,0:T(8,128)S(1)} %get-tuple-element.32.refs_1_), channel_id=1, source_target_pairs={{0,8},{4,12},{8,0},{12,4},{16,24},{20,28},{24,16},{28,20},{1,9},{5... | collective-permute-start | bytes 196616 | tf_op jit(solution)/shard_map/ppermute | solution.py:422
  7.8 5.8 %collective-permute-start.2 = (f32[64,256]{1,0:T(8,128)S(1)}, f32[64,256]{1,0:T(8,128)S(1)}, u32[]{:S(2)}, u32[]{:S(2)}) collective-permute-start(f32[64,256]{1,0:T(8,128)S(1)} %get-tuple-element.33.refs_0_.refs_2_), channel_id=1, source_target_pairs={{0,8},{4,12},{8,0},{12,4},{16,24},{20,28},{24,16},{28,20},{1,9},{5... | collective-permute-start | bytes 196616 | tf_op jit(solution)/shard_map/ppermute | solution.py:423
  7.9 5.8 %collective-permute-start.3 = (f32[64,256]{1,0:T(8,128)S(1)}, f32[64,256]{1,0:T(8,128)S(1)}, u32[]{:S(2)}, u32[]{:S(2)}) collective-permute-start(f32[64,256]{1,0:T(8,128)S(1)} %get-tuple-element.33.refs_0_.refs_2_), channel_id=1, source_target_pairs={{8,16},{12,20},{16,8},{20,12},{0,4},{4,0},{24,28},{28,24},{9,17},{... | collective-permute-start | bytes 196616 | tf_op jit(solution)/shard_map/ppermute | solution.py:424
  10.2 5.6 %collective-permute-start.5 = (f32[1,64,256]{2,1,0:T(8,128)S(1)}, f32[1,64,256]{2,1,0:T(8,128)S(1)}, u32[]{:S(2)}, u32[]{:S(2)}) collective-permute-start(f32[1,64,256]{2,1,0:T(8,128)S(1)} %shard_map.72), channel_id=1, source_target_pairs={{0,16},{4,20},{8,24},{12,28},{16,0},{20,4},{24,8},{28,12},{1,17},{... | collective-permute-start | bytes 196616 | tf_op jit(solution)/shard_map/ppermute | solution.py:426
  16.0 1.6 %collective-permute-start.6 = (f32[264,256]{1,0:T(8,128)S(1)}, f32[264,256]{1,0:T(8,128)S(1)}, u32[]{:S(2)}, u32[]{:S(2)}) collective-permute-start(f32[264,256]{1,0:T(8,128)S(1)} %shard_map.73.refs_1_.refs_2_), channel_id=1, source_target_pairs={{0,4},{4,0},{8,12},{12,8},{16,20},{20,16},{24,28},{28,24},{1,5},{5... | collective-permute-start | bytes 811016 | tf_op jit(solution)/shard_map/ppermute | solution.py:469
  18.0 7.1 %collective-permute-start.7 = (f32[320,256]{1,0:T(8,128)S(1)}, f32[320,256]{1,0:T(8,128)S(1)}, u32[]{:S(2)}, u32[]{:S(2)}) collective-permute-start(f32[320,256]{1,0:T(8,128)S(1)} %get-tuple-element.37), channel_id=1, source_target_pairs={{0,1},{1,0},{2,3},{3,2},{4,6},{5,7},{6,4},{7,5},{8,9},{9,8},{10,11... | collective-permute-start | bytes 983048 | tf_op jit(solution)/shard_map/ppermute | solution.py:498
  19.9 7.5 %collective-permute-start.9 = (f32[200,256]{1,0:T(8,128)S(1)}, f32[200,256]{1,0:T(8,128)S(1)}, u32[]{:S(2)}, u32[]{:S(2)}) collective-permute-start(f32[200,256]{1,0:T(8,128)S(1)} %get-tuple-element.41), channel_id=1, source_target_pairs={{0,1},{1,0},{2,3},{3,2},{4,6},{5,7},{6,4},{7,5},{8,9},{9,8},{10,11... | collective-permute-start | bytes 614408 | tf_op jit(solution)/shard_map/ppermute | solution.py:498
  25.2 7.0 %collective-permute-start.8 = (f32[160,256]{1,0:T(8,128)S(1)}, f32[160,256]{1,0:T(8,128)S(1)}, u32[]{:S(2)}, u32[]{:S(2)}) collective-permute-start(f32[160,256]{1,0:T(8,128)S(1)} %get-tuple-element.39), channel_id=1, source_target_pairs={{0,2},{1,3},{2,0},{3,1},{4,5},{5,4},{6,7},{7,6},{8,10},{9,11},{10,... | collective-permute-start | bytes 491528 | tf_op jit(solution)/shard_map/ppermute | solution.py:498
  27.4 4.8 %collective-permute-start.10 = (f32[104,256]{1,0:T(8,128)S(1)}, f32[104,256]{1,0:T(8,128)S(1)}, u32[]{:S(2)}, u32[]{:S(2)}) collective-permute-start(f32[104,256]{1,0:T(8,128)S(1)} %get-tuple-element.43), channel_id=1, source_target_pairs={{0,2},{1,3},{2,0},{3,1},{4,5},{5,4},{6,7},{7,6},{8,10},{9,11},{10,... | collective-permute-start | bytes 319496 | tf_op jit(solution)/shard_map/ppermute | solution.py:498
  32.3 9.7 %collective-permute-start.11 = (f32[72,256]{1,0:T(8,128)S(1)}, f32[72,256]{1,0:T(8,128)S(1)}, u32[]{:S(2)}, u32[]{:S(2)}) collective-permute-start(f32[72,256]{1,0:T(8,128)S(1)} %get-tuple-element.45), channel_id=1, source_target_pairs={{0,16},{4,20},{8,24},{12,28},{16,0},{20,4},{24,8},{28,12},{1,17},{... | collective-permute-start | bytes 221192 | tf_op jit(solution)/shard_map/ppermute | solution.py:517
  35.4 6.2 %collective-permute-start.12 = (f32[64,256]{1,0:T(8,128)S(1)}, f32[64,256]{1,0:T(8,128)S(1)}, u32[]{:S(2)}, u32[]{:S(2)}) collective-permute-start(f32[64,256]{1,0:T(8,128)S(1)} %get-tuple-element.46), channel_id=1, source_target_pairs={{0,24},{4,28},{8,16},{12,20},{16,8},{20,12},{24,0},{28,4},{1,25},{... | collective-permute-start | bytes 196616 | tf_op jit(solution)/shard_map/ppermute | solution.py:517
  37.0 5.0 %collective-permute-start.13 = (f32[64,256]{1,0:T(8,128)S(1)}, f32[64,256]{1,0:T(8,128)S(1)}, u32[]{:S(2)}, u32[]{:S(2)}) collective-permute-start(f32[64,256]{1,0:T(8,128)S(1)} %get-tuple-element.47), channel_id=1, source_target_pairs={{0,8},{4,12},{8,0},{12,4},{16,24},{20,28},{24,16},{28,20},{1,9},{5... | collective-permute-start | bytes 196616 | tf_op jit(solution)/shard_map/ppermute | solution.py:517

commit v6 on v5

--- a/solution.py
+++ b/solution.py
@@ -13,7 +13,6 @@
 STAT_ROWS = 8
 PIECES = 2
 FIRST = 4
-FIRST_ROWS = 5
 VMEM_LIMIT = 16 << 20
 f32 = jnp.float32
 bf16 = jnp.bfloat16
@@ -248,8 +247,8 @@
         out[rows, :] = scale * jnp.dot(side(columns, rows, core_of()), right, preferred_element_type=f32)
 
 
-def product_body(scale, cuts, columns, begun, own, got, *refs):
-    *outs, product = refs
+def product_body(scale, far, near, columns, begun, own, got, *refs):
+    keep, message, *outs, product = refs
     size = columns.shape[1] // 2
     right = got[:size, :].astype(bf16)
     chips, count, rows, contracts = product.shape
@@ -259,9 +258,9 @@
         block = scale * jnp.dot(side(columns, at, 1 - core_of()), right, preferred_element_type=f32)
         product[z] = (begun[at, :] + block).reshape(count, rows, contracts)
     stats = own[size:, :] + got[size:, :]
-    for part, cut in enumerate(cuts):
-        last = part + 1 == len(cuts)
-        halve(0, product, cut, stats if last else None, *outs[2 * part : 2 * part + 2])
+    halve(0, product, [partner(chip_of(), j, chips) for j in far], stats, keep, message)
+    for j, out in zip(near, outs):
+        out[...] = product[partner(chip_of(), j, chips)].reshape(out.shape)
 
 
 def path_bits(count):
@@ -269,9 +268,8 @@
     return bits, bits[len(bits) // 2 :] + bits[: len(bits) // 2]
 
 
-def halve(step, product, cut, stats, keep, message):
-    chips, n, _, _ = product.shape
-    rows = cut.stop - cut.start
+def halve(step, product, chosen, stats, keep, message):
+    _, n, rows, _ = product.shape
     first, second = path_bits(lax.axis_size("path"))
     bit, place = (
         jnp.where(core_of() == 0, a, b)
@@ -282,14 +280,14 @@
     )
     mine = (lax.axis_index("path") >> bit) & 1
     for out, value in ((keep, mine), (message, 1 - mine)):
-        for z in range(chips):
+        for k, z in enumerate(chosen):
             for i in range(n // 2):
                 low = i & ((1 << place) - 1)
                 at = ((i - low) << 1) + (value << place) + low
-                start = (z * (n // 2) + i) * rows
-                out[start : start + rows, :] = product[z, at, cut, :]
+                start = (k * (n // 2) + i) * rows
+                out[start : start + rows, :] = product[z, at]
         if stats is not None:
-            out[chips * (n // 2) * rows :, :] = stats
+            out[len(chosen) * (n // 2) * rows :, :] = stats
 
 
 def path_pairs(chips, count, step):
@@ -302,12 +300,13 @@
     ]
 
 
-def path_sum_body(step, mine, got, keep, message, product):
+def path_sum_body(step, *refs):
+    *given, keep, message, product = refs
     chips, n, rows, _ = product.shape
     size = chips * n * rows
-    product[...] = (mine[:size, :] + got[:size, :]).reshape(product.shape)
-    stats = mine[size:, :] + got[size:, :] if mine.shape[0] > size else None
-    halve(step, product, slice(0, rows), stats, keep, message)
+    total = functools.reduce(lambda a, b: a + b, (p[...] for p in given))
+    product[...] = total[:size, :].reshape(product.shape)
+    halve(step, product, range(chips), total[size:, :] if total.shape[0] > size else None, keep, message)
 
 
 def partner(me, j, count):
@@ -331,33 +330,24 @@
     return inner + [(2 * a + c, 2 * a + 1 - c) for a in (0, 3) for c in range(2)]
 
 
-def chip_sum_body(chips, cuts, *refs):
-    given, (keep, *messages), (total,) = refs[: -chips - 1], refs[-chips - 1 : -1], refs[-1:]
-    rows = (total.shape[0] - STAT_ROWS) // chips
-    for part, cut in enumerate(cuts):
-        mine, got = given[2 * part : 2 * part + 2]
-        share = cut.stop - cut.start
-        for z in range(chips):
-            at = slice(z * share, (z + 1) * share)
-            total[z * rows + cut.start : z * rows + cut.stop, :] = mine[at, :] + got[at, :]
-    total[chips * rows :, :] = mine[chips * share :, :] + got[chips * share :, :]
-    for j, out in enumerate((keep, *messages)):
-        at = pl.multiple_of(partner(chip_of(), j, chips) * rows, rows)
-        out[0:rows, :] = total[pl.ds(at, rows), :]
+def part_sum_body(chips, rows, mine, got, *outs):
+    total = mine[...] + got[...]
+    for k, out in enumerate(outs[:chips]):
+        out[0:rows, :] = total[k * rows : (k + 1) * rows, :]
         if out.shape[0] > rows:
             out[rows:, :] = total[chips * rows :, :]
-
-
-def date_sum_body(chips, paths_total, *refs):
-    parts, (gradient, bound, spread) = refs[:chips], refs[chips:]
+    for out in outs[chips:]:
+        out[...] = total[chips * rows :, :]
+
+
+def date_sum_body(chips, paths_total, stats, across, *refs):
+    parts, (gradient, bound, spread) = refs[:-3], refs[-3:]
     rows = gradient.shape[0]
-    gradient[...] = functools.reduce(lambda a, b: a + b, (p[:rows, :] for p in parts))
-    first = chip_of() < max(chips // 2, 1)
-    across = parts[([0] + chip_order(chips)).index(chips // 2)]
-    stats = jnp.where(first, parts[0][rows:, :], across[rows:, :])
-    mean = stats[0:1, :] * (1.0 / paths_total)
+    gradient[...] = functools.reduce(lambda a, b: a + b, (p[:rows, :] for p in parts), across[:rows, :])
+    sums = jnp.where(chip_of() < chips // 2, stats[...], across[rows:, :])
+    mean = sums[0:1, :] * (1.0 / paths_total)
     bound[...] = mean
-    spread[...] = stats[1:2, :] * (1.0 / paths_total) - mean * mean
+    spread[...] = sums[1:2, :] * (1.0 / paths_total) - mean * mean
 
 
 def chip_order(chips):
@@ -469,12 +459,27 @@
     tail_other = lax.ppermute(tail, "date", cores)
     steps = count.bit_length() - 1
     assert count == 1 << steps and steps > 0
-    first = rows * FIRST_ROWS // 8 // 8 * 8
-    cuts = [slice(0, first), slice(first, rows)] if first else [slice(0, rows)]
-
-    def piece(n, cut):
-        stats = STAT_ROWS if cut is cuts[-1] else 0
-        return ((chips * n * (cut.stop - cut.start) + stats, contracts), f32)
+    near, far = list(range(chips // 2)), list(range(chips // 2, chips))
+
+    def piece(n, chips, stats=False):
+        return ((chips * n * rows + (STAT_ROWS if stats else 0), contracts), f32)
+
+    def over_path(step, message):
+        return lax.ppermute(message, ("date", "path"), path_pairs(chips, count, step))
+
+    def over_date(j, message):
+        return lax.ppermute(message, "date", date_pairs(chips, j))
+
+    def next_round(step, given, after, chips, stats):
+        n = count >> step
+        return call(
+            functools.partial(path_sum_body, step),
+            [piece(n // 2, chips, stats)] * 2,
+            *given,
+            *after,
+            unread=len(after),
+            scratch=[pltpu.VMEM((chips, n, rows, contracts), f32)],
+        )
 
     (begun,) = call(
         functools.partial(first_body, -1.0 / paths_total),
@@ -483,9 +488,9 @@
         tail,
         flops=dates * paths * width * contracts,
     )
-    outs = call(
-        functools.partial(product_body, -1.0 / paths_total, cuts),
-        [piece(count // 2, cut) for cut in cuts for _ in range(2)],
+    keep, message, *firsts = call(
+        functools.partial(product_body, -1.0 / paths_total, far, near),
+        [piece(count // 2, len(far), True)] * 2 + [piece(count, 1)] * len(near),
         columns,
         begun,
         tail,
@@ -493,33 +498,30 @@
         scratch=[pltpu.VMEM((chips, count, rows, contracts), f32)],
         flops=dates * paths * width * contracts,
     )
-    sent = [outs[2 * part : 2 * part + 2] for part in range(len(cuts))]
-    for step in range(steps):
-        sent = [(keep, lax.ppermute(m, ("date", "path"), path_pairs(chips, count, step))) for keep, m in sent]
-        if step + 1 == steps:
-            break
-        n = count >> (step + 1)
-        sent = [
-            call(
-                functools.partial(path_sum_body, step + 1),
-                [piece(n // 2, cut)] * 2,
-                *pair,
-                scratch=[pltpu.VMEM((chips, n, cut.stop - cut.start, contracts), f32)],
-            )
-            for cut, pair in zip(cuts, sent)
-        ]
-    pieces = call(
-        functools.partial(chip_sum_body, chips, cuts),
-        [((rows + (STAT_ROWS if j in (0, chips // 2) else 0), contracts), f32) for j in range(chips)],
-        *[x for pair in sent for x in pair],
-        scratch=[pltpu.VMEM((chips * rows + STAT_ROWS, contracts), f32)],
-    )
-    over = {j: lax.ppermute(pieces[j], "date", date_pairs(chips, j)) for j in chip_order(chips)}
-    pieces = [pieces[0]] + list(over.values())
+    got = over_path(0, message)
+    near_parts = [firsts[0]] + [over_date(j, firsts[j]) for j in chip_order(chips) if j in near]
+    for step in range(1, steps):
+        keep, message = next_round(step, [keep, got], [], len(far), True)
+        got = over_path(step, message)
+        near_keep, near_message = next_round(step - 1, near_parts, [message], 1, False)
+        near_parts = [near_keep, over_path(step - 1, near_message)]
+    row = ((rows, contracts), f32)
+    *sums, stats = call(
+        functools.partial(part_sum_body, len(far), rows),
+        [piece(1, 1, True)] * len(far) + [((STAT_ROWS, contracts), f32)],
+        keep,
+        got,
+        *([near_message] if steps > 1 else []),
+        unread=min(1, steps - 1),
+    )
+    over = [over_date(j, sums[far.index(j)]) for j in chip_order(chips) if j in far]
+    near_keep, near_message = next_round(steps - 1, near_parts, sums[:1], 1, False)
+    over += [near_keep, over_path(steps - 1, near_message)]
     gradient, bound, spread = call(
         functools.partial(date_sum_body, chips, paths_total),
-        [((rows, contracts), f32), ((1, contracts), f32), ((1, contracts), f32)],
-        *pieces,
+        [row, ((1, contracts), f32), ((1, contracts), f32)],
+        stats,
+        *over,
     )
     return gradient, bound.reshape(contracts), spread.reshape(contracts)
 

time: 42.8 us -> 40.4 us (0.944)
  waiting for transfers between devices: 18 us -> 13.3 us
  starting transfers between devices: 18.4 us -> 20.7 us
    ppermute x7, waiting for transfers between devices: 12.6 us -> 7.85 us  [the longest x4 6.36 us: over_path(): lax.ppermute(message, ('date', 'path'), path_pairs(chips, count, step))]
    ppermute x7, starting transfers between devices: 11.2 us -> 13.6 us  [the longest x4 7.51 us: over_path(): lax.ppermute(message, ('date', 'path'), path_pairs(chips, count, step))]
    pallas_call x13 -> x14, Pallas kernels: 5.52 us -> 5.51 us  [call(): pl.pallas_call(kernel, out_shape=[jax.ShapeDtypeStruct(*o) for o in outs]...]
  transfers between devices with their start and end apart: 14 -> 14, of which waited for: 8 -> 7; matrix products, arithmetic and copies ran while one was open for 0% -> 0% of each run, Pallas kernels for 5% -> 6%
where the time goes in v6:
time: 40.4 us; the launch traced here: 40.3 us
  starting transfers between devices  20.7 us (51%)
  waiting for transfers between devices  13.3 us (33%)
  Pallas kernels  5.51 us (14%)
  between operations  0.73 us (2%)
    ppermute x4, starting transfers between devices, over_path(): lax.ppermute(message, ('date', 'path'), path_pairs(chips, count, step))  7.51 us
    ppermute x4, waiting for transfers between devices, over_path(): lax.ppermute(message, ('date', 'path'), path_pairs(chips, count, step))  6.36 us
    ppermute x3, starting transfers between devices, over_date(): return lax.ppermute(message, 'date', date_pairs(chips, j))  6.06 us
    pallas_call x14, Pallas kernels, call(): pl.pallas_call(kernel, out_shape=[jax.ShapeDtypeStruct(*o) for o in outs]...  5.51 us
    ppermute x1, starting transfers between devices, shards(): far = lax.ppermute(message, 'date', date_pairs(chips, 2))  3.4 us
    ppermute x1, starting transfers between devices, shards(): near = lax.ppermute(message, 'date', date_pairs(chips, 1))  3.01 us
    ppermute x1, waiting for transfers between devices, shards(): near = lax.ppermute(message, 'date', date_pairs(chips, 1))  2.3 us
    ppermute x1, waiting for transfers between devices, shards(): far = lax.ppermute(message, 'date', date_pairs(chips, 2))  1.9 us
  transfers between devices with their start and end apart: 14, of which 7 were waited for; matrix products, arithmetic and copies ran while one was open for 0% of the time, Pallas kernels for 6%

profile of v6, /device:TPU:0, one launch (start us, length us, event | category | flops | bytes accessed | tf_op | source)
XLA Modules:
  0.0 40.3 jit_solution(14472560778942560191)
XLA Ops:
  0.6 1.8 %shard_map.67 = (f32[4,64,256]{2,1,0:T(8,128)S(1)}, bf16[2,64,2048]{2,1,0:T(8,128)(2,1)S(1)}, bf16[2048,256]{1,0:T(8,128)(2,1)S(1)}) custom-call(bf16[2,128,2048]{2,1,0:T(8,128)(2,1)} %refs_0_.3, bf16[2048,256]{1,0:T(8,128)(2,1)} %refs_1_.2, f32[2,128,256]{2,1,0:T(8,128)} %refs_1_.3, s32[2,256]{1,0:T(2,128)} %refs_2_.3), custom_call_target="tpu_custom_call" | custom-call | tf_op jit(solution)/shard_map/pallas_call | solution.py:42
  2.4 0.5 %collective-permute-start = (f32[4,64,256]{2,1,0:T(8,128)S(1)}, f32[4,64,256]{2,1,0:T(8,128)S(1)}, u32[]{:S(2)}, u32[]{:S(2)}) collective-permute-start(f32[4,64,256]{2,1,0:T(8,128)S(1)} %get-tuple-element.32), channel_id=1, source_target_pairs={{0,4},{4,0},{8,12},{12,8},{16,20},{20,16},{24,28},{28,24},{1,5},{5... | collective-permute-start | bytes 786440 | tf_op jit(solution)/shard_map/ppermute | solution.py:381
  3.0 1.4 %shard_map.68 = (f32[4,64,256]{2,1,0:T(8,128)S(1)}, bf16[2,128,2048]{2,1,0:T(8,128)(2,1)S(1)}) custom-call(bf16[2,128,2048]{2,1,0:T(8,128)(2,1)} %refs_0_.3, f32[2,128,256]{2,1,0:T(8,128)} %refs_1_.3, s32[2,256]{1,0:T(2,128)} %refs_2_.3, bf16[2048,256]{1,0:T(8,128)(2,1)S(1)} %get-tuple-element.28.refs_3_, bf16[2,64,2048]{2,1,0:T(8,128)(2,1)S(1)} %get-tuple-element.29.refs_4_), custom_call_target="tpu_custom_call" | custom-call | tf_op jit(solution)/shard_map/pallas_call | solution.py:42
  4.4 0.0 collective-permute-done.refs_1_
  4.4 0.1 shard_map.69
  4.6 0.1 shard_map.70
  4.7 0.1 collective-permute-start.1
  4.8 3.0 %collective-permute-start.4 = (f32[1,64,256]{2,1,0:T(8,128)S(1)}, f32[1,64,256]{2,1,0:T(8,128)S(1)}, u32[]{:S(2)}, u32[]{:S(2)}) collective-permute-start(f32[1,64,256]{2,1,0:T(8,128)S(1)} %get-tuple-element.33.refs_1_), channel_id=1, source_target_pairs={{0,8},{4,12},{8,0},{12,4},{16,24},{20,28},{24,16},{28,20},{1,9},{5... | collective-permute-start | bytes 196616 | tf_op jit(solution)/shard_map/ppermute | solution.py:412
  7.8 0.0 collective-permute-start.2
  7.9 0.0 collective-permute-start.3
  7.9 2.3 %collective-permute-done.4.refs_2_.refs_3_ = f32[1,64,256]{2,1,0:T(8,128)S(1)} collective-permute-done((f32[1,64,256]{2,1,0:T(8,128)S(1)}, f32[1,64,256]{2,1,0:T(8,128)S(1)}, u32[]{:S(2)}, u32[]{:S(2)}) %collective-permute-start.4) | collective-permute-done | bytes 65568 | tf_op jit(solution)/shard_map/ppermute | solution.py:412
  10.2 3.4 %collective-permute-start.5 = (f32[1,64,256]{2,1,0:T(8,128)S(1)}, f32[1,64,256]{2,1,0:T(8,128)S(1)}, u32[]{:S(2)}, u32[]{:S(2)}) collective-permute-start(f32[1,64,256]{2,1,0:T(8,128)S(1)} %shard_map.72), channel_id=1, source_target_pairs={{0,16},{4,20},{8,24},{12,28},{16,0},{20,4},{24,8},{28,12},{1,17},{... | collective-permute-start | bytes 196616 | tf_op jit(solution)/shard_map/ppermute | solution.py:416
  13.6 0.0 collective-permute-done.2.refs_2_.refs_5_
  13.6 0.0 collective-permute-done.3.refs_3_.refs_6_
  13.6 0.0 collective-permute-done.1.refs_1_
  13.6 0.3 shard_map.71.refs_7_.refs_0_
  14.0 1.9 %collective-permute-done.5.refs_4_ = f32[1,64,256]{2,1,0:T(8,128)S(1)} collective-permute-done((f32[1,64,256]{2,1,0:T(8,128)S(1)}, f32[1,64,256]{2,1,0:T(8,128)S(1)}, u32[]{:S(2)}, u32[]{:S(2)}) %collective-permute-start.5) | collective-permute-done | bytes 65568 | tf_op jit(solution)/shard_map/ppermute | solution.py:416
  15.9 0.2 shard_map.73.refs_1_.refs_2_
  16.0 0.1 collective-permute-start.6
  16.1 0.3 shard_map.74.refs_1_
  16.4 1.2 %collective-permute-done.6.refs_3_ = f32[264,256]{1,0:T(8,128)S(1)} collective-permute-done((f32[264,256]{1,0:T(8,128)S(1)}, f32[264,256]{1,0:T(8,128)S(1)}, u32[]{:S(2)}, u32[]{:S(2)}) %collective-permute-start.6) | collective-permute-done | bytes 270368 | tf_op jit(solution)/shard_map/ppermute | solution.py:459
  17.6 0.4 shard_map.75
  18.0 1.9 %collective-permute-start.7 = (f32[264,256]{1,0:T(8,128)S(1)}, f32[264,256]{1,0:T(8,128)S(1)}, u32[]{:S(2)}, u32[]{:S(2)}) collective-permute-start(f32[264,256]{1,0:T(8,128)S(1)} %get-tuple-element.38), channel_id=1, source_target_pairs={{0,1},{1,0},{2,3},{3,2},{4,6},{5,7},{6,4},{7,5},{8,9},{9,8},{10,11... | collective-permute-start | bytes 811016 | tf_op jit(solution)/shard_map/ppermute | solution.py:468
  19.9 1.7 %collective-permute-start.9 = (f32[256,256]{1,0:T(8,128)S(1)}, f32[256,256]{1,0:T(8,128)S(1)}, u32[]{:S(2)}, u32[]{:S(2)}) collective-permute-start(f32[256,256]{1,0:T(8,128)S(1)} %get-tuple-element.42), channel_id=1, source_target_pairs={{0,8},{4,12},{8,0},{12,4},{16,24},{20,28},{24,16},{28,20},{1,9},{5... | collective-permute-start | bytes 786440 | tf_op jit(solution)/shard_map/ppermute | solution.py:471
  21.6 2.9 %collective-permute-done.7.refs_1_ = f32[264,256]{1,0:T(8,128)S(1)} collective-permute-done((f32[264,256]{1,0:T(8,128)S(1)}, f32[264,256]{1,0:T(8,128)S(1)}, u32[]{:S(2)}, u32[]{:S(2)}) %collective-permute-start.7) | collective-permute-done | bytes 270368 | tf_op jit(solution)/shard_map/ppermute | solution.py:468
  24.6 1.9 %collective-permute-start.8 = (f32[136,256]{1,0:T(8,128)S(1)}, f32[136,256]{1,0:T(8,128)S(1)}, u32[]{:S(2)}, u32[]{:S(2)}) collective-permute-start(f32[136,256]{1,0:T(8,128)S(1)} %get-tuple-element.40.refs_2_), channel_id=1, source_target_pairs={{0,2},{1,3},{2,0},{3,1},{4,5},{5,4},{6,7},{7,6},{8,10},{9,11},{10,... | collective-permute-start | bytes 417800 | tf_op jit(solution)/shard_map/ppermute | solution.py:468
  26.5 1.5 %collective-permute-done.9.refs_1_ = f32[256,256]{1,0:T(8,128)S(1)} collective-permute-done((f32[256,256]{1,0:T(8,128)S(1)}, f32[256,256]{1,0:T(8,128)S(1)}, u32[]{:S(2)}, u32[]{:S(2)}) %collective-permute-start.9) | collective-permute-done | bytes 262176 | tf_op jit(solution)/shard_map/ppermute | solution.py:471
  28.0 0.1 shard_map.77
  28.1 1.2 %collective-permute-start.12 = (f32[128,256]{1,0:T(8,128)S(1)}, f32[128,256]{1,0:T(8,128)S(1)}, u32[]{:S(2)}, u32[]{:S(2)}) collective-permute-start(f32[128,256]{1,0:T(8,128)S(1)} %get-tuple-element.43.refs_2_), channel_id=1, source_target_pairs={{0,1},{1,0},{2,3},{3,2},{4,6},{5,7},{6,4},{7,5},{8,9},{9,8},{10,11... | collective-permute-start | bytes 393224 | tf_op jit(solution)/shard_map/ppermute | solution.py:468
  29.3 1.2 %collective-permute-done.8.refs_1_ = f32[136,256]{1,0:T(8,128)S(1)} collective-permute-done((f32[136,256]{1,0:T(8,128)S(1)}, f32[136,256]{1,0:T(8,128)S(1)}, u32[]{:S(2)}, u32[]{:S(2)}) %collective-permute-start.8) | collective-permute-done | bytes 139296 | tf_op jit(solution)/shard_map/ppermute | solution.py:468
  30.4 2.3 %collective-permute-start.10 = (f32[72,256]{1,0:T(8,128)S(1)}, f32[72,256]{1,0:T(8,128)S(1)}, u32[]{:S(2)}, u32[]{:S(2)}) collective-permute-start(f32[72,256]{1,0:T(8,128)S(1)} %get-tuple-element.45.refs_2_), channel_id=1, source_target_pairs={{0,16},{4,20},{8,24},{12,28},{16,0},{20,4},{24,8},{28,12},{1,17},{... | collective-permute-start | bytes 221192 | tf_op jit(solution)/shard_map/ppermute | solution.py:471
  32.8 2.0 %collective-permute-start.11 = (f32[72,256]{1,0:T(8,128)S(1)}, f32[72,256]{1,0:T(8,128)S(1)}, u32[]{:S(2)}, u32[]{:S(2)}) collective-permute-start(f32[72,256]{1,0:T(8,128)S(1)} %get-tuple-element.46), channel_id=1, source_target_pairs={{0,24},{4,28},{8,16},{12,20},{16,8},{20,12},{24,0},{28,4},{1,25},{... | collective-permute-start | bytes 221192 | tf_op jit(solution)/shard_map/ppermute | solution.py:471
  34.8 0.0 collective-permute-done.12.refs_1_
  34.8 2.5 %collective-permute-start.13 = (f32[64,256]{1,0:T(8,128)S(1)}, f32[64,256]{1,0:T(8,128)S(1)}, u32[]{:S(2)}, u32[]{:S(2)}) collective-permute-start(f32[64,256]{1,0:T(8,128)S(1)} %get-tuple-element.49), channel_id=1, source_target_pairs={{0,2},{1,3},{2,0},{3,1},{4,5},{5,4},{6,7},{7,6},{8,10},{9,11},{10,... | collective-permute-start | bytes 196616 | tf_op jit(solution)/shard_map/ppermute | solution.py:468
  37.4 2.2 %collective-permute-done.13.refs_4_ = f32[64,256]{1,0:T(8,128)S(1)} collective-permute-done((f32[64,256]{1,0:T(8,128)S(1)}, f32[64,256]{1,0:T(8,128)S(1)}, u32[]{:S(2)}, u32[]{:S(2)}) %collective-permute-start.13) | collective-permute-done | bytes 65568 | tf_op jit(solution)/shard_map/ppermute | solution.py:468
  39.6 0.0 collective-permute-done.10.refs_1_
  39.6 0.0 collective-permute-done.11.refs_2_
  39.6 0.6 %shard_map.80 = (f32[64,256]{1,0:T(8,128)}, f32[1,256]{1,0:T(1,128)}, f32[1,256]{1,0:T(1,128)}) custom-call(f32[8,256]{1,0:T(8,128)S(1)} %get-tuple-element.44.refs_0_, f32[72,256]{1,0:T(8,128)S(1)} %collective-permute-done.10.refs_1_, f32[72,256]{1,0:T(8,128)S(1)} %collective-permute-done.11.refs_2_, f32[64,256]{1,0:T(8,128)S(1)} %get-tuple-element.48.refs_3_, ...), custom_call_target="tpu_custom_call" | custom-call | tf_op jit(solution)/shard_map/pallas_call | solution.py:42
  (4 shorter events, 0.1 us)
Async XLA Ops:
  2.4 2.0 %collective-permute-start = (f32[4,64,256]{2,1,0:T(8,128)S(1)}, f32[4,64,256]{2,1,0:T(8,128)S(1)}, u32[]{:S(2)}, u32[]{:S(2)}) collective-permute-start(f32[4,64,256]{2,1,0:T(8,128)S(1)} %get-tuple-element.32), channel_id=1, source_target_pairs={{0,4},{4,0},{8,12},{12,8},{16,20},{20,16},{24,28},{28,24},{1,5},{5... | collective-permute-start | bytes 786440 | tf_op jit(solution)/shard_map/ppermute | solution.py:381
  4.7 8.9 %collective-permute-start.1 = (f32[2,128,1024]{2,1,0:T(8,128)S(1)}, f32[2,128,1024]{2,1,0:T(8,128)S(1)}, u32[]{:S(2)}, u32[]{:S(2)}) collective-permute-start(f32[2,128,1024]{2,1,0:T(8,128)S(1)} %shard_map.70), channel_id=1, source_target_pairs={{0,4},{4,0},{8,12},{12,8},{16,20},{20,16},{24,28},{28,24},{1,5},{5... | collective-permute-start | bytes 3145736 | tf_op jit(solution)/shard_map/ppermute | solution.py:409
  4.8 5.3 %collective-permute-start.4 = (f32[1,64,256]{2,1,0:T(8,128)S(1)}, f32[1,64,256]{2,1,0:T(8,128)S(1)}, u32[]{:S(2)}, u32[]{:S(2)}) collective-permute-start(f32[1,64,256]{2,1,0:T(8,128)S(1)} %get-tuple-element.33.refs_1_), channel_id=1, source_target_pairs={{0,8},{4,12},{8,0},{12,4},{16,24},{20,28},{24,16},{28,20},{1,9},{5... | collective-permute-start | bytes 196616 | tf_op jit(solution)/shard_map/ppermute | solution.py:412
  7.8 5.8 %collective-permute-start.2 = (f32[64,256]{1,0:T(8,128)S(1)}, f32[64,256]{1,0:T(8,128)S(1)}, u32[]{:S(2)}, u32[]{:S(2)}) collective-permute-start(f32[64,256]{1,0:T(8,128)S(1)} %get-tuple-element.34.refs_0_.refs_2_), channel_id=1, source_target_pairs={{0,8},{4,12},{8,0},{12,4},{16,24},{20,28},{24,16},{28,20},{1,9},{5... | collective-permute-start | bytes 196616 | tf_op jit(solution)/shard_map/ppermute | solution.py:413
  7.9 5.8 %collective-permute-start.3 = (f32[64,256]{1,0:T(8,128)S(1)}, f32[64,256]{1,0:T(8,128)S(1)}, u32[]{:S(2)}, u32[]{:S(2)}) collective-permute-start(f32[64,256]{1,0:T(8,128)S(1)} %get-tuple-element.34.refs_0_.refs_2_), channel_id=1, source_target_pairs={{8,16},{12,20},{16,8},{20,12},{0,4},{4,0},{24,28},{28,24},{9,17},{... | collective-permute-start | bytes 196616 | tf_op jit(solution)/shard_map/ppermute | solution.py:414
  10.2 5.6 %collective-permute-start.5 = (f32[1,64,256]{2,1,0:T(8,128)S(1)}, f32[1,64,256]{2,1,0:T(8,128)S(1)}, u32[]{:S(2)}, u32[]{:S(2)}) collective-permute-start(f32[1,64,256]{2,1,0:T(8,128)S(1)} %shard_map.72), channel_id=1, source_target_pairs={{0,16},{4,20},{8,24},{12,28},{16,0},{20,4},{24,8},{28,12},{1,17},{... | collective-permute-start | bytes 196616 | tf_op jit(solution)/shard_map/ppermute | solution.py:416
  16.0 1.6 %collective-permute-start.6 = (f32[264,256]{1,0:T(8,128)S(1)}, f32[264,256]{1,0:T(8,128)S(1)}, u32[]{:S(2)}, u32[]{:S(2)}) collective-permute-start(f32[264,256]{1,0:T(8,128)S(1)} %shard_map.73.refs_1_.refs_2_), channel_id=1, source_target_pairs={{0,4},{4,0},{8,12},{12,8},{16,20},{20,16},{24,28},{28,24},{1,5},{5... | collective-permute-start | bytes 811016 | tf_op jit(solution)/shard_map/ppermute | solution.py:459
  18.0 6.5 %collective-permute-start.7 = (f32[264,256]{1,0:T(8,128)S(1)}, f32[264,256]{1,0:T(8,128)S(1)}, u32[]{:S(2)}, u32[]{:S(2)}) collective-permute-start(f32[264,256]{1,0:T(8,128)S(1)} %get-tuple-element.38), channel_id=1, source_target_pairs={{0,1},{1,0},{2,3},{3,2},{4,6},{5,7},{6,4},{7,5},{8,9},{9,8},{10,11... | collective-permute-start | bytes 811016 | tf_op jit(solution)/shard_map/ppermute | solution.py:468
  19.9 8.1 %collective-permute-start.9 = (f32[256,256]{1,0:T(8,128)S(1)}, f32[256,256]{1,0:T(8,128)S(1)}, u32[]{:S(2)}, u32[]{:S(2)}) collective-permute-start(f32[256,256]{1,0:T(8,128)S(1)} %get-tuple-element.42), channel_id=1, source_target_pairs={{0,8},{4,12},{8,0},{12,4},{16,24},{20,28},{24,16},{28,20},{1,9},{5... | collective-permute-start | bytes 786440 | tf_op jit(solution)/shard_map/ppermute | solution.py:471
  24.6 5.8 %collective-permute-start.8 = (f32[136,256]{1,0:T(8,128)S(1)}, f32[136,256]{1,0:T(8,128)S(1)}, u32[]{:S(2)}, u32[]{:S(2)}) collective-permute-start(f32[136,256]{1,0:T(8,128)S(1)} %get-tuple-element.40.refs_2_), channel_id=1, source_target_pairs={{0,2},{1,3},{2,0},{3,1},{4,5},{5,4},{6,7},{7,6},{8,10},{9,11},{10,... | collective-permute-start | bytes 417800 | tf_op jit(solution)/shard_map/ppermute | solution.py:468
  28.1 6.7 %collective-permute-start.12 = (f32[128,256]{1,0:T(8,128)S(1)}, f32[128,256]{1,0:T(8,128)S(1)}, u32[]{:S(2)}, u32[]{:S(2)}) collective-permute-start(f32[128,256]{1,0:T(8,128)S(1)} %get-tuple-element.43.refs_2_), channel_id=1, source_target_pairs={{0,1},{1,0},{2,3},{3,2},{4,6},{5,7},{6,4},{7,5},{8,9},{9,8},{10,11... | collective-permute-start | bytes 393224 | tf_op jit(solution)/shard_map/ppermute | solution.py:468
  30.4 9.2 %collective-permute-start.10 = (f32[72,256]{1,0:T(8,128)S(1)}, f32[72,256]{1,0:T(8,128)S(1)}, u32[]{:S(2)}, u32[]{:S(2)}) collective-permute-start(f32[72,256]{1,0:T(8,128)S(1)} %get-tuple-element.45.refs_2_), channel_id=1, source_target_pairs={{0,16},{4,20},{8,24},{12,28},{16,0},{20,4},{24,8},{28,12},{1,17},{... | collective-permute-start | bytes 221192 | tf_op jit(solution)/shard_map/ppermute | solution.py:471
  32.8 6.8 %collective-permute-start.11 = (f32[72,256]{1,0:T(8,128)S(1)}, f32[72,256]{1,0:T(8,128)S(1)}, u32[]{:S(2)}, u32[]{:S(2)}) collective-permute-start(f32[72,256]{1,0:T(8,128)S(1)} %get-tuple-element.46), channel_id=1, source_target_pairs={{0,24},{4,28},{8,16},{12,20},{16,8},{20,12},{24,0},{28,4},{1,25},{... | collective-permute-start | bytes 221192 | tf_op jit(solution)/shard_map/ppermute | solution.py:471
  34.8 4.8 %collective-permute-start.13 = (f32[64,256]{1,0:T(8,128)S(1)}, f32[64,256]{1,0:T(8,128)S(1)}, u32[]{:S(2)}, u32[]{:S(2)}) collective-permute-start(f32[64,256]{1,0:T(8,128)S(1)} %get-tuple-element.49), channel_id=1, source_target_pairs={{0,2},{1,3},{2,0},{3,1},{4,5},{5,4},{6,7},{7,6},{8,10},{9,11},{10,... | collective-permute-start | bytes 196616 | tf_op jit(solution)/shard_map/ppermute | solution.py:468

commit v7 on v6

--- a/solution.py
+++ b/solution.py
@@ -247,20 +247,25 @@
         out[rows, :] = scale * jnp.dot(side(columns, rows, core_of()), right, preferred_element_type=f32)
 
 
-def product_body(scale, far, near, columns, begun, own, got, *refs):
-    keep, message, *outs, product = refs
+def rows_of(scale, j, width, columns, begun, right):
+    chip = partner(chip_of(), j, begun.shape[0] // width)
+    at = pl.ds(pl.multiple_of(chip * width, width), width)
+    return begun[at, :] + scale * jnp.dot(side(columns, at, 1 - core_of()), right, preferred_element_type=f32)
+
+
+def far_body(scale, far, columns, begun, own, got, keep, message, product):
     size = columns.shape[1] // 2
     right = got[:size, :].astype(bf16)
-    chips, count, rows, contracts = product.shape
-    width = count * rows
-    for z in range(chips):
-        at = slice(z * width, (z + 1) * width)
-        block = scale * jnp.dot(side(columns, at, 1 - core_of()), right, preferred_element_type=f32)
-        product[z] = (begun[at, :] + block).reshape(count, rows, contracts)
-    stats = own[size:, :] + got[size:, :]
-    halve(0, product, [partner(chip_of(), j, chips) for j in far], stats, keep, message)
+    _, count, rows, _ = product.shape
+    for k, j in enumerate(far):
+        product[k] = rows_of(scale, j, count * rows, columns, begun, right).reshape(product.shape[1:])
+    halve(0, product, own[size:, :] + got[size:, :], keep, message)
+
+
+def near_body(scale, near, columns, begun, got, *outs):
+    right = got[: columns.shape[1] // 2, :].astype(bf16)
     for j, out in zip(near, outs):
-        out[...] = product[partner(chip_of(), j, chips)].reshape(out.shape)
+        out[...] = rows_of(scale, j, out.shape[0], columns, begun, right)
 
 
 def path_bits(count):
@@ -268,8 +273,8 @@
     return bits, bits[len(bits) // 2 :] + bits[: len(bits) // 2]
 
 
-def halve(step, product, chosen, stats, keep, message):
-    _, n, rows, _ = product.shape
+def halve(step, product, stats, keep, message):
+    chips, n, rows, _ = product.shape
     first, second = path_bits(lax.axis_size("path"))
     bit, place = (
         jnp.where(core_of() == 0, a, b)
@@ -280,14 +285,14 @@
     )
     mine = (lax.axis_index("path") >> bit) & 1
     for out, value in ((keep, mine), (message, 1 - mine)):
-        for k, z in enumerate(chosen):
+        start = 0
+        for k in range(chips):
             for i in range(n // 2):
                 low = i & ((1 << place) - 1)
-                at = ((i - low) << 1) + (value << place) + low
-                start = (k * (n // 2) + i) * rows
-                out[start : start + rows, :] = product[z, at]
+                out[start : start + rows, :] = product[k, ((i - low) << 1) + (value << place) + low]
+                start += rows
         if stats is not None:
-            out[len(chosen) * (n // 2) * rows :, :] = stats
+            out[start:, :] = stats
 
 
 def path_pairs(chips, count, step):
@@ -302,11 +307,10 @@
 
 def path_sum_body(step, *refs):
     *given, keep, message, product = refs
-    chips, n, rows, _ = product.shape
-    size = chips * n * rows
+    size = product.shape[0] * product.shape[1] * product.shape[2]
     total = functools.reduce(lambda a, b: a + b, (p[...] for p in given))
     product[...] = total[:size, :].reshape(product.shape)
-    halve(step, product, range(chips), total[size:, :] if total.shape[0] > size else None, keep, message)
+    halve(step, product, total[size:, :] if total.shape[0] > size else None, keep, message)
 
 
 def partner(me, j, count):
@@ -330,14 +334,14 @@
     return inner + [(2 * a + c, 2 * a + 1 - c) for a in (0, 3) for c in range(2)]
 
 
-def part_sum_body(chips, rows, mine, got, *outs):
+def part_sum_body(rows, mine, got, *outs):
     total = mine[...] + got[...]
-    for k, out in enumerate(outs[:chips]):
-        out[0:rows, :] = total[k * rows : (k + 1) * rows, :]
-        if out.shape[0] > rows:
-            out[rows:, :] = total[chips * rows :, :]
-    for out in outs[chips:]:
-        out[...] = total[chips * rows :, :]
+    chips = len(outs) - 1
+    blocks = [total[k * rows : (k + 1) * rows, :] for k in range(chips)]
+    for first, second, out in zip(blocks, blocks[::-1], outs):
+        out[0:rows, :] = jnp.where(core_of() == 0, first, second)
+        out[rows:, :] = total[chips * rows :, :]
+    outs[-1][...] = total[chips * rows :, :]
 
 
 def date_sum_body(chips, paths_total, stats, across, *refs):
@@ -350,8 +354,8 @@
     spread[...] = sums[1:2, :] * (1.0 / paths_total) - mean * mean
 
 
-def chip_order(chips):
-    return sorted(range(1, chips), key=lambda j: (-j.bit_length(), j))
+def far_pairs(chips, far, k):
+    return [(2 * z + c, 2 * (z ^ (far, far[::-1])[c][k]) + c) for z in range(chips) for c in range(2)]
 
 
 def shards(features, payoff, coefficients, exercise):
@@ -461,24 +465,21 @@
     assert count == 1 << steps and steps > 0
     near, far = list(range(chips // 2)), list(range(chips // 2, chips))
 
-    def piece(n, chips, stats=False):
-        return ((chips * n * rows + (STAT_ROWS if stats else 0), contracts), f32)
+    def piece(n, part, stats=False):
+        return ((n * part * rows + (STAT_ROWS if stats else 0), contracts), f32)
 
     def over_path(step, message):
         return lax.ppermute(message, ("date", "path"), path_pairs(chips, count, step))
 
-    def over_date(j, message):
-        return lax.ppermute(message, "date", date_pairs(chips, j))
-
-    def next_round(step, given, after, chips, stats):
+    def next_round(step, given, after, part, stats):
         n = count >> step
         return call(
             functools.partial(path_sum_body, step),
-            [piece(n // 2, chips, stats)] * 2,
+            [piece(n // 2, part, stats)] * 2,
             *given,
             *after,
             unread=len(after),
-            scratch=[pltpu.VMEM((chips, n, rows, contracts), f32)],
+            scratch=[pltpu.VMEM((part, n, rows, contracts), f32)],
         )
 
     (begun,) = call(
@@ -488,38 +489,48 @@
         tail,
         flops=dates * paths * width * contracts,
     )
-    keep, message, *firsts = call(
-        functools.partial(product_body, -1.0 / paths_total, far, near),
-        [piece(count // 2, len(far), True)] * 2 + [piece(count, 1)] * len(near),
+    keep, message = call(
+        functools.partial(far_body, -1.0 / paths_total, far),
+        [piece(count // 2, len(far), True)] * 2,
         columns,
         begun,
         tail,
         tail_other,
-        scratch=[pltpu.VMEM((chips, count, rows, contracts), f32)],
-        flops=dates * paths * width * contracts,
+        scratch=[pltpu.VMEM((len(far), count, rows, contracts), f32)],
+        flops=dates * paths * width * contracts // 2,
     )
     got = over_path(0, message)
-    near_parts = [firsts[0]] + [over_date(j, firsts[j]) for j in chip_order(chips) if j in near]
+    firsts = call(
+        functools.partial(near_body, -1.0 / paths_total, near),
+        [piece(count, 1)] * len(near),
+        columns,
+        begun,
+        tail_other,
+        message,
+        unread=1,
+        flops=dates * paths * width * contracts // 2,
+    )
+    near_parts = [lax.ppermute(x, "date", date_pairs(chips, j)) if j else x for j, x in zip(near, firsts)]
+    assert steps > 1
     for step in range(1, steps):
         keep, message = next_round(step, [keep, got], [], len(far), True)
         got = over_path(step, message)
         near_keep, near_message = next_round(step - 1, near_parts, [message], 1, False)
         near_parts = [near_keep, over_path(step - 1, near_message)]
-    row = ((rows, contracts), f32)
     *sums, stats = call(
-        functools.partial(part_sum_body, len(far), rows),
+        functools.partial(part_sum_body, rows),
         [piece(1, 1, True)] * len(far) + [((STAT_ROWS, contracts), f32)],
         keep,
         got,
-        *([near_message] if steps > 1 else []),
-        unread=min(1, steps - 1),
-    )
-    over = [over_date(j, sums[far.index(j)]) for j in chip_order(chips) if j in far]
+        near_message,
+        unread=1,
+    )
+    over = [lax.ppermute(x, "date", far_pairs(chips, far, k)) for k, x in enumerate(sums)]
     near_keep, near_message = next_round(steps - 1, near_parts, sums[:1], 1, False)
     over += [near_keep, over_path(steps - 1, near_message)]
     gradient, bound, spread = call(
         functools.partial(date_sum_body, chips, paths_total),
-        [row, ((1, contracts), f32), ((1, contracts), f32)],
+        [((rows, contracts), f32), ((1, contracts), f32), ((1, contracts), f32)],
         stats,
         *over,
     )

time: 40.4 us -> 40.2 us (level)
    ppermute x4, waiting for transfers between devices: 6.36 us -> 5.68 us  [over_path(): lax.ppermute(message, ('date', 'path'), path_pairs(chips, count, step))]
    pallas_call x14 -> x15, Pallas kernels: 5.51 us -> 5.65 us  [call(): pl.pallas_call(kernel, out_shape=[jax.ShapeDtypeStruct(*o) for o in outs]...]
where the time goes in v7:
time: 40.2 us; the launch traced here: 40.1 us
  starting transfers between devices  20.8 us (52%)
  waiting for transfers between devices  12.9 us (32%)
  Pallas kernels  5.65 us (14%)
  between operations  0.74 us (2%)
    ppermute x4, starting transfers between devices, over_path(): lax.ppermute(message, ('date', 'path'), path_pairs(chips, count, step))  7.53 us
    ppermute x4, waiting for transfers between devices, over_path(): lax.ppermute(message, ('date', 'path'), path_pairs(chips, count, step))  5.68 us
    pallas_call x15, Pallas kernels, call(): pl.pallas_call(kernel, out_shape=[jax.ShapeDtypeStruct(*o) for o in outs]...  5.65 us
    ppermute x2, starting transfers between devices, shards(): lax.ppermute(x, 'date', far_pairs(chips, far, k))  4.32 us
    ppermute x1, starting transfers between devices, shards(): far = lax.ppermute(message, 'date', date_pairs(chips, 2))  3.4 us
    ppermute x1, starting transfers between devices, shards(): near = lax.ppermute(message, 'date', date_pairs(chips, 1))  3.01 us
    ppermute x1, waiting for transfers between devices, shards(): near = lax.ppermute(message, 'date', date_pairs(chips, 1))  2.3 us
    ppermute x1, waiting for transfers between devices, shards(): far = lax.ppermute(message, 'date', date_pairs(chips, 2))  1.9 us
  transfers between devices with their start and end apart: 14, of which 7 were waited for; matrix products, arithmetic and copies ran while one was open for 0% of the time, Pallas kernels for 6%

profile of v7, /device:TPU:0, one launch (start us, length us, event | category | flops | bytes accessed | tf_op | source)
XLA Modules:
  0.0 40.1 jit_solution(18011946463051540561)
XLA Ops:
  0.6 1.8 %shard_map.67 = (f32[4,64,256]{2,1,0:T(8,128)S(1)}, bf16[2,64,2048]{2,1,0:T(8,128)(2,1)S(1)}, bf16[2048,256]{1,0:T(8,128)(2,1)S(1)}) custom-call(bf16[2,128,2048]{2,1,0:T(8,128)(2,1)} %refs_0_.3, bf16[2048,256]{1,0:T(8,128)(2,1)} %refs_1_.2, f32[2,128,256]{2,1,0:T(8,128)} %refs_1_.3, s32[2,256]{1,0:T(2,128)} %refs_2_.3), custom_call_target="tpu_custom_call" | custom-call | tf_op jit(solution)/shard_map/pallas_call | solution.py:42
  2.4 0.5 %collective-permute-start = (f32[4,64,256]{2,1,0:T(8,128)S(1)}, f32[4,64,256]{2,1,0:T(8,128)S(1)}, u32[]{:S(2)}, u32[]{:S(2)}) collective-permute-start(f32[4,64,256]{2,1,0:T(8,128)S(1)} %get-tuple-element.32), channel_id=1, source_target_pairs={{0,4},{4,0},{8,12},{12,8},{16,20},{20,16},{24,28},{28,24},{1,5},{5... | collective-permute-start | bytes 786440 | tf_op jit(solution)/shard_map/ppermute | solution.py:385
  3.0 1.4 %shard_map.68 = (f32[4,64,256]{2,1,0:T(8,128)S(1)}, bf16[2,128,2048]{2,1,0:T(8,128)(2,1)S(1)}) custom-call(bf16[2,128,2048]{2,1,0:T(8,128)(2,1)} %refs_0_.3, f32[2,128,256]{2,1,0:T(8,128)} %refs_1_.3, s32[2,256]{1,0:T(2,128)} %refs_2_.3, bf16[2048,256]{1,0:T(8,128)(2,1)S(1)} %get-tuple-element.28.refs_3_, bf16[2,64,2048]{2,1,0:T(8,128)(2,1)S(1)} %get-tuple-element.29.refs_4_), custom_call_target="tpu_custom_call" | custom-call | tf_op jit(solution)/shard_map/pallas_call | solution.py:42
  4.4 0.0 collective-permute-done.refs_1_
  4.4 0.1 shard_map.69
  4.6 0.1 shard_map.70
  4.7 0.1 collective-permute-start.1
  4.8 3.0 %collective-permute-start.4 = (f32[1,64,256]{2,1,0:T(8,128)S(1)}, f32[1,64,256]{2,1,0:T(8,128)S(1)}, u32[]{:S(2)}, u32[]{:S(2)}) collective-permute-start(f32[1,64,256]{2,1,0:T(8,128)S(1)} %get-tuple-element.33.refs_1_), channel_id=1, source_target_pairs={{0,8},{4,12},{8,0},{12,4},{16,24},{20,28},{24,16},{28,20},{1,9},{5... | collective-permute-start | bytes 196616 | tf_op jit(solution)/shard_map/ppermute | solution.py:416
  7.8 0.0 collective-permute-start.2
  7.9 0.0 collective-permute-start.3
  7.9 2.3 %collective-permute-done.4.refs_2_.refs_3_ = f32[1,64,256]{2,1,0:T(8,128)S(1)} collective-permute-done((f32[1,64,256]{2,1,0:T(8,128)S(1)}, f32[1,64,256]{2,1,0:T(8,128)S(1)}, u32[]{:S(2)}, u32[]{:S(2)}) %collective-permute-start.4) | collective-permute-done | bytes 65568 | tf_op jit(solution)/shard_map/ppermute | solution.py:416
  10.2 3.4 %collective-permute-start.5 = (f32[1,64,256]{2,1,0:T(8,128)S(1)}, f32[1,64,256]{2,1,0:T(8,128)S(1)}, u32[]{:S(2)}, u32[]{:S(2)}) collective-permute-start(f32[1,64,256]{2,1,0:T(8,128)S(1)} %shard_map.72), channel_id=1, source_target_pairs={{0,16},{4,20},{8,24},{12,28},{16,0},{20,4},{24,8},{28,12},{1,17},{... | collective-permute-start | bytes 196616 | tf_op jit(solution)/shard_map/ppermute | solution.py:420
  13.6 0.0 collective-permute-done.2.refs_2_.refs_5_
  13.6 0.0 collective-permute-done.3.refs_3_.refs_6_
  13.6 0.0 collective-permute-done.1.refs_1_
  13.6 0.3 shard_map.71.refs_7_.refs_0_
  14.0 1.9 %collective-permute-done.5.refs_4_ = f32[1,64,256]{2,1,0:T(8,128)S(1)} collective-permute-done((f32[1,64,256]{2,1,0:T(8,128)S(1)}, f32[1,64,256]{2,1,0:T(8,128)S(1)}, u32[]{:S(2)}, u32[]{:S(2)}) %collective-permute-start.5) | collective-permute-done | bytes 65568 | tf_op jit(solution)/shard_map/ppermute | solution.py:420
  15.9 0.2 shard_map.73.refs_1_.refs_2_
  16.0 0.1 collective-permute-start.6
  16.1 0.3 shard_map.74.refs_1_
  16.4 1.2 %collective-permute-done.6.refs_3_.refs_2_ = f32[264,256]{1,0:T(8,128)S(1)} collective-permute-done((f32[264,256]{1,0:T(8,128)S(1)}, f32[264,256]{1,0:T(8,128)S(1)}, u32[]{:S(2)}, u32[]{:S(2)}) %collective-permute-start.6) | collective-permute-done | bytes 270368 | tf_op jit(solution)/shard_map/ppermute | solution.py:463
  17.6 0.3 shard_map.75
  17.9 1.9 %collective-permute-start.7 = (f32[264,256]{1,0:T(8,128)S(1)}, f32[264,256]{1,0:T(8,128)S(1)}, u32[]{:S(2)}, u32[]{:S(2)}) collective-permute-start(f32[264,256]{1,0:T(8,128)S(1)} %get-tuple-element.38.refs_3_), channel_id=1, source_target_pairs={{0,1},{1,0},{2,3},{3,2},{4,6},{5,7},{6,4},{7,5},{8,9},{9,8},{10,11... | collective-permute-start | bytes 811016 | tf_op jit(solution)/shard_map/ppermute | solution.py:472
  19.8 0.2 shard_map.77
  20.0 1.8 %collective-permute-start.9 = (f32[256,256]{1,0:T(8,128)S(1)}, f32[256,256]{1,0:T(8,128)S(1)}, u32[]{:S(2)}, u32[]{:S(2)}) collective-permute-start(f32[256,256]{1,0:T(8,128)S(1)} %get-tuple-element.42), channel_id=1, source_target_pairs={{0,8},{4,12},{8,0},{12,4},{16,24},{20,28},{24,16},{28,20},{1,9},{5... | collective-permute-start | bytes 786440 | tf_op jit(solution)/shard_map/ppermute | solution.py:513
  21.8 2.7 %collective-permute-done.7.refs_1_ = f32[264,256]{1,0:T(8,128)S(1)} collective-permute-done((f32[264,256]{1,0:T(8,128)S(1)}, f32[264,256]{1,0:T(8,128)S(1)}, u32[]{:S(2)}, u32[]{:S(2)}) %collective-permute-start.7) | collective-permute-done | bytes 270368 | tf_op jit(solution)/shard_map/ppermute | solution.py:472
  24.4 0.1 shard_map.76
  24.5 1.9 %collective-permute-start.8 = (f32[136,256]{1,0:T(8,128)S(1)}, f32[136,256]{1,0:T(8,128)S(1)}, u32[]{:S(2)}, u32[]{:S(2)}) collective-permute-start(f32[136,256]{1,0:T(8,128)S(1)} %get-tuple-element.40.refs_2_), channel_id=1, source_target_pairs={{0,2},{1,3},{2,0},{3,1},{4,5},{5,4},{6,7},{7,6},{8,10},{9,11},{10,... | collective-permute-start | bytes 417800 | tf_op jit(solution)/shard_map/ppermute | solution.py:472
  26.4 1.8 %collective-permute-done.9.refs_1_ = f32[256,256]{1,0:T(8,128)S(1)} collective-permute-done((f32[256,256]{1,0:T(8,128)S(1)}, f32[256,256]{1,0:T(8,128)S(1)}, u32[]{:S(2)}, u32[]{:S(2)}) %collective-permute-start.9) | collective-permute-done | bytes 262176 | tf_op jit(solution)/shard_map/ppermute | solution.py:513
  28.2 0.1 shard_map.78
  28.2 1.2 %collective-permute-start.12 = (f32[128,256]{1,0:T(8,128)S(1)}, f32[128,256]{1,0:T(8,128)S(1)}, u32[]{:S(2)}, u32[]{:S(2)}) collective-permute-start(f32[128,256]{1,0:T(8,128)S(1)} %get-tuple-element.43.refs_2_), channel_id=1, source_target_pairs={{0,1},{1,0},{2,3},{3,2},{4,6},{5,7},{6,4},{7,5},{8,9},{9,8},{10,11... | collective-permute-start | bytes 393224 | tf_op jit(solution)/shard_map/ppermute | solution.py:472
  29.5 0.8 %collective-permute-done.8.refs_1_ = f32[136,256]{1,0:T(8,128)S(1)} collective-permute-done((f32[136,256]{1,0:T(8,128)S(1)}, f32[136,256]{1,0:T(8,128)S(1)}, u32[]{:S(2)}, u32[]{:S(2)}) %collective-permute-start.8) | collective-permute-done | bytes 139296 | tf_op jit(solution)/shard_map/ppermute | solution.py:472
  30.3 2.4 %collective-permute-start.10 = (f32[72,256]{1,0:T(8,128)S(1)}, f32[72,256]{1,0:T(8,128)S(1)}, u32[]{:S(2)}, u32[]{:S(2)}) collective-permute-start(f32[72,256]{1,0:T(8,128)S(1)} %get-tuple-element.45.refs_2_), channel_id=1, source_target_pairs={{0,16},{4,28},{8,24},{12,20},{16,0},{20,12},{24,8},{28,4},{1,17},{... | collective-permute-start | bytes 221192 | tf_op jit(solution)/shard_map/ppermute | solution.py:528
  32.7 1.9 %collective-permute-start.11 = (f32[72,256]{1,0:T(8,128)S(1)}, f32[72,256]{1,0:T(8,128)S(1)}, u32[]{:S(2)}, u32[]{:S(2)}) collective-permute-start(f32[72,256]{1,0:T(8,128)S(1)} %get-tuple-element.46), channel_id=1, source_target_pairs={{0,24},{4,20},{8,16},{12,28},{16,8},{20,4},{24,0},{28,12},{1,25},{... | collective-permute-start | bytes 221192 | tf_op jit(solution)/shard_map/ppermute | solution.py:528
  34.6 0.0 collective-permute-done.12.refs_1_
  34.6 2.5 %collective-permute-start.13 = (f32[64,256]{1,0:T(8,128)S(1)}, f32[64,256]{1,0:T(8,128)S(1)}, u32[]{:S(2)}, u32[]{:S(2)}) collective-permute-start(f32[64,256]{1,0:T(8,128)S(1)} %get-tuple-element.49), channel_id=1, source_target_pairs={{0,2},{1,3},{2,0},{3,1},{4,5},{5,4},{6,7},{7,6},{8,10},{9,11},{10,... | collective-permute-start | bytes 196616 | tf_op jit(solution)/shard_map/ppermute | solution.py:472
  37.2 2.2 %collective-permute-done.13.refs_4_ = f32[64,256]{1,0:T(8,128)S(1)} collective-permute-done((f32[64,256]{1,0:T(8,128)S(1)}, f32[64,256]{1,0:T(8,128)S(1)}, u32[]{:S(2)}, u32[]{:S(2)}) %collective-permute-start.13) | collective-permute-done | bytes 65568 | tf_op jit(solution)/shard_map/ppermute | solution.py:472
  39.4 0.0 collective-permute-done.10.refs_1_
  39.4 0.0 collective-permute-done.11.refs_2_
  39.4 0.7 %shard_map.81 = (f32[64,256]{1,0:T(8,128)}, f32[1,256]{1,0:T(1,128)}, f32[1,256]{1,0:T(1,128)}) custom-call(f32[8,256]{1,0:T(8,128)S(1)} %get-tuple-element.44.refs_0_, f32[72,256]{1,0:T(8,128)S(1)} %collective-permute-done.10.refs_1_, f32[72,256]{1,0:T(8,128)S(1)} %collective-permute-done.11.refs_2_, f32[64,256]{1,0:T(8,128)S(1)} %get-tuple-element.48.refs_3_, ...), custom_call_target="tpu_custom_call" | custom-call | tf_op jit(solution)/shard_map/pallas_call | solution.py:42
  (3 shorter events, 0.1 us)
Async XLA Ops:
  2.4 2.0 %collective-permute-start = (f32[4,64,256]{2,1,0:T(8,128)S(1)}, f32[4,64,256]{2,1,0:T(8,128)S(1)}, u32[]{:S(2)}, u32[]{:S(2)}) collective-permute-start(f32[4,64,256]{2,1,0:T(8,128)S(1)} %get-tuple-element.32), channel_id=1, source_target_pairs={{0,4},{4,0},{8,12},{12,8},{16,20},{20,16},{24,28},{28,24},{1,5},{5... | collective-permute-start | bytes 786440 | tf_op jit(solution)/shard_map/ppermute | solution.py:385
  4.7 8.9 %collective-permute-start.1 = (f32[2,128,1024]{2,1,0:T(8,128)S(1)}, f32[2,128,1024]{2,1,0:T(8,128)S(1)}, u32[]{:S(2)}, u32[]{:S(2)}) collective-permute-start(f32[2,128,1024]{2,1,0:T(8,128)S(1)} %shard_map.70), channel_id=1, source_target_pairs={{0,4},{4,0},{8,12},{12,8},{16,20},{20,16},{24,28},{28,24},{1,5},{5... | collective-permute-start | bytes 3145736 | tf_op jit(solution)/shard_map/ppermute | solution.py:413
  4.8 5.3 %collective-permute-start.4 = (f32[1,64,256]{2,1,0:T(8,128)S(1)}, f32[1,64,256]{2,1,0:T(8,128)S(1)}, u32[]{:S(2)}, u32[]{:S(2)}) collective-permute-start(f32[1,64,256]{2,1,0:T(8,128)S(1)} %get-tuple-element.33.refs_1_), channel_id=1, source_target_pairs={{0,8},{4,12},{8,0},{12,4},{16,24},{20,28},{24,16},{28,20},{1,9},{5... | collective-permute-start | bytes 196616 | tf_op jit(solution)/shard_map/ppermute | solution.py:416
  7.8 5.8 %collective-permute-start.2 = (f32[64,256]{1,0:T(8,128)S(1)}, f32[64,256]{1,0:T(8,128)S(1)}, u32[]{:S(2)}, u32[]{:S(2)}) collective-permute-start(f32[64,256]{1,0:T(8,128)S(1)} %get-tuple-element.34.refs_0_.refs_2_), channel_id=1, source_target_pairs={{0,8},{4,12},{8,0},{12,4},{16,24},{20,28},{24,16},{28,20},{1,9},{5... | collective-permute-start | bytes 196616 | tf_op jit(solution)/shard_map/ppermute | solution.py:417
  7.9 5.8 %collective-permute-start.3 = (f32[64,256]{1,0:T(8,128)S(1)}, f32[64,256]{1,0:T(8,128)S(1)}, u32[]{:S(2)}, u32[]{:S(2)}) collective-permute-start(f32[64,256]{1,0:T(8,128)S(1)} %get-tuple-element.34.refs_0_.refs_2_), channel_id=1, source_target_pairs={{8,16},{12,20},{16,8},{20,12},{0,4},{4,0},{24,28},{28,24},{9,17},{... | collective-permute-start | bytes 196616 | tf_op jit(solution)/shard_map/ppermute | solution.py:418
  10.2 5.6 %collective-permute-start.5 = (f32[1,64,256]{2,1,0:T(8,128)S(1)}, f32[1,64,256]{2,1,0:T(8,128)S(1)}, u32[]{:S(2)}, u32[]{:S(2)}) collective-permute-start(f32[1,64,256]{2,1,0:T(8,128)S(1)} %shard_map.72), channel_id=1, source_target_pairs={{0,16},{4,20},{8,24},{12,28},{16,0},{20,4},{24,8},{28,12},{1,17},{... | collective-permute-start | bytes 196616 | tf_op jit(solution)/shard_map/ppermute | solution.py:420
  16.0 1.6 %collective-permute-start.6 = (f32[264,256]{1,0:T(8,128)S(1)}, f32[264,256]{1,0:T(8,128)S(1)}, u32[]{:S(2)}, u32[]{:S(2)}) collective-permute-start(f32[264,256]{1,0:T(8,128)S(1)} %shard_map.73.refs_1_.refs_2_), channel_id=1, source_target_pairs={{0,4},{4,0},{8,12},{12,8},{16,20},{20,16},{24,28},{28,24},{1,5},{5... | collective-permute-start | bytes 811016 | tf_op jit(solution)/shard_map/ppermute | solution.py:463
  17.9 6.5 %collective-permute-start.7 = (f32[264,256]{1,0:T(8,128)S(1)}, f32[264,256]{1,0:T(8,128)S(1)}, u32[]{:S(2)}, u32[]{:S(2)}) collective-permute-start(f32[264,256]{1,0:T(8,128)S(1)} %get-tuple-element.38.refs_3_), channel_id=1, source_target_pairs={{0,1},{1,0},{2,3},{3,2},{4,6},{5,7},{6,4},{7,5},{8,9},{9,8},{10,11... | collective-permute-start | bytes 811016 | tf_op jit(solution)/shard_map/ppermute | solution.py:472
  20.0 8.2 %collective-permute-start.9 = (f32[256,256]{1,0:T(8,128)S(1)}, f32[256,256]{1,0:T(8,128)S(1)}, u32[]{:S(2)}, u32[]{:S(2)}) collective-permute-start(f32[256,256]{1,0:T(8,128)S(1)} %get-tuple-element.42), channel_id=1, source_target_pairs={{0,8},{4,12},{8,0},{12,4},{16,24},{20,28},{24,16},{28,20},{1,9},{5... | collective-permute-start | bytes 786440 | tf_op jit(solution)/shard_map/ppermute | solution.py:513
  24.5 5.7 %collective-permute-start.8 = (f32[136,256]{1,0:T(8,128)S(1)}, f32[136,256]{1,0:T(8,128)S(1)}, u32[]{:S(2)}, u32[]{:S(2)}) collective-permute-start(f32[136,256]{1,0:T(8,128)S(1)} %get-tuple-element.40.refs_2_), channel_id=1, source_target_pairs={{0,2},{1,3},{2,0},{3,1},{4,5},{5,4},{6,7},{7,6},{8,10},{9,11},{10,... | collective-permute-start | bytes 417800 | tf_op jit(solution)/shard_map/ppermute | solution.py:472
  28.2 6.4 %collective-permute-start.12 = (f32[128,256]{1,0:T(8,128)S(1)}, f32[128,256]{1,0:T(8,128)S(1)}, u32[]{:S(2)}, u32[]{:S(2)}) collective-permute-start(f32[128,256]{1,0:T(8,128)S(1)} %get-tuple-element.43.refs_2_), channel_id=1, source_target_pairs={{0,1},{1,0},{2,3},{3,2},{4,6},{5,7},{6,4},{7,5},{8,9},{9,8},{10,11... | collective-permute-start | bytes 393224 | tf_op jit(solution)/shard_map/ppermute | solution.py:472
  30.3 9.2 %collective-permute-start.10 = (f32[72,256]{1,0:T(8,128)S(1)}, f32[72,256]{1,0:T(8,128)S(1)}, u32[]{:S(2)}, u32[]{:S(2)}) collective-permute-start(f32[72,256]{1,0:T(8,128)S(1)} %get-tuple-element.45.refs_2_), channel_id=1, source_target_pairs={{0,16},{4,28},{8,24},{12,20},{16,0},{20,12},{24,8},{28,4},{1,17},{... | collective-permute-start | bytes 221192 | tf_op jit(solution)/shard_map/ppermute | solution.py:528
  32.7 6.7 %collective-permute-start.11 = (f32[72,256]{1,0:T(8,128)S(1)}, f32[72,256]{1,0:T(8,128)S(1)}, u32[]{:S(2)}, u32[]{:S(2)}) collective-permute-start(f32[72,256]{1,0:T(8,128)S(1)} %get-tuple-element.46), channel_id=1, source_target_pairs={{0,24},{4,20},{8,16},{12,28},{16,8},{20,4},{24,0},{28,12},{1,25},{... | collective-permute-start | bytes 221192 | tf_op jit(solution)/shard_map/ppermute | solution.py:528
  34.6 4.8 %collective-permute-start.13 = (f32[64,256]{1,0:T(8,128)S(1)}, f32[64,256]{1,0:T(8,128)S(1)}, u32[]{:S(2)}, u32[]{:S(2)}) collective-permute-start(f32[64,256]{1,0:T(8,128)S(1)} %get-tuple-element.49), channel_id=1, source_target_pairs={{0,2},{1,3},{2,0},{3,1},{4,5},{5,4},{6,7},{7,6},{8,10},{9,11},{10,... | collective-permute-start | bytes 196616 | tf_op jit(solution)/shard_map/ppermute | solution.py:472

commit v8 on v7

--- a/solution.py
+++ b/solution.py
@@ -259,7 +259,7 @@
     _, count, rows, _ = product.shape
     for k, j in enumerate(far):
         product[k] = rows_of(scale, j, count * rows, columns, begun, right).reshape(product.shape[1:])
-    halve(0, product, own[size:, :] + got[size:, :], keep, message)
+    halve(0, False, product, own[size:, :] + got[size:, :], keep, message)
 
 
 def near_body(scale, near, columns, begun, got, *outs):
@@ -268,14 +268,15 @@
         out[...] = rows_of(scale, j, out.shape[0], columns, begun, right)
 
 
-def path_bits(count):
+def path_bits(count, near):
     bits = list(range(count.bit_length() - 1))
-    return bits, bits[len(bits) // 2 :] + bits[: len(bits) // 2]
-
-
-def halve(step, product, stats, keep, message):
+    orders = bits, bits[len(bits) // 2 :] + bits[: len(bits) // 2]
+    return orders[::-1] if near else orders
+
+
+def halve(step, near, product, stats, keep, message):
     chips, n, rows, _ = product.shape
-    first, second = path_bits(lax.axis_size("path"))
+    first, second = path_bits(lax.axis_size("path"), near)
     bit, place = (
         jnp.where(core_of() == 0, a, b)
         for a, b in (
@@ -295,8 +296,8 @@
             out[start:, :] = stats
 
 
-def path_pairs(chips, count, step):
-    first, second = path_bits(count)
+def path_pairs(chips, count, step, near):
+    first, second = path_bits(count, near)
     return [
         ((2 * z + core) * count + p, (2 * z + core) * count + (p ^ (1 << order[step])))
         for z in range(chips)
@@ -305,12 +306,12 @@
     ]
 
 
-def path_sum_body(step, *refs):
+def path_sum_body(step, near, *refs):
     *given, keep, message, product = refs
     size = product.shape[0] * product.shape[1] * product.shape[2]
     total = functools.reduce(lambda a, b: a + b, (p[...] for p in given))
     product[...] = total[:size, :].reshape(product.shape)
-    halve(step, product, total[size:, :] if total.shape[0] > size else None, keep, message)
+    halve(step, near, product, total[size:, :] if total.shape[0] > size else None, keep, message)
 
 
 def partner(me, j, count):
@@ -337,9 +338,8 @@
 def part_sum_body(rows, mine, got, *outs):
     total = mine[...] + got[...]
     chips = len(outs) - 1
-    blocks = [total[k * rows : (k + 1) * rows, :] for k in range(chips)]
-    for first, second, out in zip(blocks, blocks[::-1], outs):
-        out[0:rows, :] = jnp.where(core_of() == 0, first, second)
+    for k, out in enumerate(outs[:chips]):
+        out[0:rows, :] = total[k * rows : (k + 1) * rows, :]
         out[rows:, :] = total[chips * rows :, :]
     outs[-1][...] = total[chips * rows :, :]
 
@@ -352,10 +352,6 @@
     mean = sums[0:1, :] * (1.0 / paths_total)
     bound[...] = mean
     spread[...] = sums[1:2, :] * (1.0 / paths_total) - mean * mean
-
-
-def far_pairs(chips, far, k):
-    return [(2 * z + c, 2 * (z ^ (far, far[::-1])[c][k]) + c) for z in range(chips) for c in range(2)]
 
 
 def shards(features, payoff, coefficients, exercise):
@@ -468,13 +464,13 @@
     def piece(n, part, stats=False):
         return ((n * part * rows + (STAT_ROWS if stats else 0), contracts), f32)
 
-    def over_path(step, message):
-        return lax.ppermute(message, ("date", "path"), path_pairs(chips, count, step))
+    def over_path(step, message, near=False):
+        return lax.ppermute(message, ("date", "path"), path_pairs(chips, count, step, near))
 
     def next_round(step, given, after, part, stats):
         n = count >> step
         return call(
-            functools.partial(path_sum_body, step),
+            functools.partial(path_sum_body, step, not stats),
             [piece(n // 2, part, stats)] * 2,
             *given,
             *after,
@@ -516,7 +512,7 @@
         keep, message = next_round(step, [keep, got], [], len(far), True)
         got = over_path(step, message)
         near_keep, near_message = next_round(step - 1, near_parts, [message], 1, False)
-        near_parts = [near_keep, over_path(step - 1, near_message)]
+        near_parts = [near_keep, over_path(step - 1, near_message, True)]
     *sums, stats = call(
         functools.partial(part_sum_body, rows),
         [piece(1, 1, True)] * len(far) + [((STAT_ROWS, contracts), f32)],
@@ -525,9 +521,9 @@
         near_message,
         unread=1,
     )
-    over = [lax.ppermute(x, "date", far_pairs(chips, far, k)) for k, x in enumerate(sums)]
+    over = [lax.ppermute(x, "date", date_pairs(chips, j)) for j, x in zip(far, sums)]
     near_keep, near_message = next_round(steps - 1, near_parts, sums[:1], 1, False)
-    over += [near_keep, over_path(steps - 1, near_message)]
+    over += [near_keep, over_path(steps - 1, near_message, True)]
     gradient, bound, spread = call(
         functools.partial(date_sum_body, chips, paths_total),
         [((rows, contracts), f32), ((1, contracts), f32), ((1, contracts), f32)],

time: 40.2 us -> 39.7 us (0.988)
  starting transfers between devices: 20.8 us -> 19.4 us
  waiting for transfers between devices: 12.9 us -> 13.8 us
    ppermute x6 -> x4, starting transfers between devices: 11.9 us -> 5.85 us  [over_path(): lax.ppermute(message, ('date', 'path'), path_pairs(chips, count, step, ne...]
    ppermute x1 -> x3, starting transfers between devices: 1.77 us -> 6.43 us  [shards(): lax.ppermute(x, 'date', date_pairs(chips, j))]
    ppermute x6 -> x4, waiting for transfers between devices: 5.68 us -> 6.29 us  [over_path(): lax.ppermute(message, ('date', 'path'), path_pairs(chips, count, step, ne...]
    ppermute x1 -> x3, waiting for transfers between devices: 1.78 us -> 2.04 us  [shards(): lax.ppermute(x, 'date', date_pairs(chips, j))]
  transfers between devices with their start and end apart: 14 -> 14, of which waited for: 7 -> 8; matrix products, arithmetic and copies ran while one was open for 0% -> 0% of each run, Pallas kernels for 6% -> 6%
where the time goes in v8:
time: 39.7 us; the launch traced here: 39.6 us
  starting transfers between devices  19.4 us (49%)
  waiting for transfers between devices  13.8 us (35%)
  Pallas kernels  5.64 us (14%)
  between operations  0.74 us (2%)
    ppermute x3, starting transfers between devices, shards(): lax.ppermute(x, 'date', date_pairs(chips, j))  6.43 us
    ppermute x4, waiting for transfers between devices, over_path(): lax.ppermute(message, ('date', 'path'), path_pairs(chips, count, step, ne...  6.29 us
    ppermute x4, starting transfers between devices, over_path(): lax.ppermute(message, ('date', 'path'), path_pairs(chips, count, step, ne...  5.85 us
    pallas_call x15, Pallas kernels, call(): pl.pallas_call(kernel, out_shape=[jax.ShapeDtypeStruct(*o) for o in outs]...  5.64 us
    ppermute x1, starting transfers between devices, shards(): far = lax.ppermute(message, 'date', date_pairs(chips, 2))  3.4 us
    ppermute x1, starting transfers between devices, shards(): near = lax.ppermute(message, 'date', date_pairs(chips, 1))  3.01 us
    ppermute x1, waiting for transfers between devices, shards(): near = lax.ppermute(message, 'date', date_pairs(chips, 1))  2.3 us
    ppermute x3, waiting for transfers between devices, shards(): lax.ppermute(x, 'date', date_pairs(chips, j))  2.04 us
  transfers between devices with their start and end apart: 14, of which 8 were waited for; matrix products, arithmetic and copies ran while one was open for 0% of the time, Pallas kernels for 6%

profile of v8, /device:TPU:0, one launch (start us, length us, event | category | flops | bytes accessed | tf_op | source)
XLA Modules:
  0.0 39.6 jit_solution(17743705266838583957)
XLA Ops:
  0.6 1.8 %shard_map.67 = (f32[4,64,256]{2,1,0:T(8,128)S(1)}, bf16[2,64,2048]{2,1,0:T(8,128)(2,1)S(1)}, bf16[2048,256]{1,0:T(8,128)(2,1)S(1)}) custom-call(bf16[2,128,2048]{2,1,0:T(8,128)(2,1)} %refs_0_.3, bf16[2048,256]{1,0:T(8,128)(2,1)} %refs_1_.2, f32[2,128,256]{2,1,0:T(8,128)} %refs_1_.3, s32[2,256]{1,0:T(2,128)} %refs_2_.3), custom_call_target="tpu_custom_call" | custom-call | tf_op jit(solution)/shard_map/pallas_call | solution.py:42
  2.4 0.5 %collective-permute-start = (f32[4,64,256]{2,1,0:T(8,128)S(1)}, f32[4,64,256]{2,1,0:T(8,128)S(1)}, u32[]{:S(2)}, u32[]{:S(2)}) collective-permute-start(f32[4,64,256]{2,1,0:T(8,128)S(1)} %get-tuple-element.32), channel_id=1, source_target_pairs={{0,4},{4,0},{8,12},{12,8},{16,20},{20,16},{24,28},{28,24},{1,5},{5... | collective-permute-start | bytes 786440 | tf_op jit(solution)/shard_map/ppermute | solution.py:381
  3.0 1.4 %shard_map.68 = (f32[4,64,256]{2,1,0:T(8,128)S(1)}, bf16[2,128,2048]{2,1,0:T(8,128)(2,1)S(1)}) custom-call(bf16[2,128,2048]{2,1,0:T(8,128)(2,1)} %refs_0_.3, f32[2,128,256]{2,1,0:T(8,128)} %refs_1_.3, s32[2,256]{1,0:T(2,128)} %refs_2_.3, bf16[2048,256]{1,0:T(8,128)(2,1)S(1)} %get-tuple-element.28.refs_3_, bf16[2,64,2048]{2,1,0:T(8,128)(2,1)S(1)} %get-tuple-element.29.refs_4_), custom_call_target="tpu_custom_call" | custom-call | tf_op jit(solution)/shard_map/pallas_call | solution.py:42
  4.4 0.0 collective-permute-done.refs_1_
  4.4 0.1 shard_map.69
  4.6 0.1 shard_map.70
  4.7 0.1 collective-permute-start.1
  4.8 3.0 %collective-permute-start.4 = (f32[1,64,256]{2,1,0:T(8,128)S(1)}, f32[1,64,256]{2,1,0:T(8,128)S(1)}, u32[]{:S(2)}, u32[]{:S(2)}) collective-permute-start(f32[1,64,256]{2,1,0:T(8,128)S(1)} %get-tuple-element.33.refs_1_), channel_id=1, source_target_pairs={{0,8},{4,12},{8,0},{12,4},{16,24},{20,28},{24,16},{28,20},{1,9},{5... | collective-permute-start | bytes 196616 | tf_op jit(solution)/shard_map/ppermute | solution.py:412
  7.8 0.0 collective-permute-start.2
  7.9 0.0 collective-permute-start.3
  7.9 2.3 %collective-permute-done.4.refs_2_.refs_3_ = f32[1,64,256]{2,1,0:T(8,128)S(1)} collective-permute-done((f32[1,64,256]{2,1,0:T(8,128)S(1)}, f32[1,64,256]{2,1,0:T(8,128)S(1)}, u32[]{:S(2)}, u32[]{:S(2)}) %collective-permute-start.4) | collective-permute-done | bytes 65568 | tf_op jit(solution)/shard_map/ppermute | solution.py:412
  10.2 3.4 %collective-permute-start.5 = (f32[1,64,256]{2,1,0:T(8,128)S(1)}, f32[1,64,256]{2,1,0:T(8,128)S(1)}, u32[]{:S(2)}, u32[]{:S(2)}) collective-permute-start(f32[1,64,256]{2,1,0:T(8,128)S(1)} %shard_map.72), channel_id=1, source_target_pairs={{0,16},{4,20},{8,24},{12,28},{16,0},{20,4},{24,8},{28,12},{1,17},{... | collective-permute-start | bytes 196616 | tf_op jit(solution)/shard_map/ppermute | solution.py:416
  13.6 0.0 collective-permute-done.2.refs_2_.refs_5_
  13.6 0.0 collective-permute-done.3.refs_3_.refs_6_
  13.6 0.0 collective-permute-done.1.refs_1_
  13.6 0.3 shard_map.71.refs_7_.refs_0_
  14.0 1.9 %collective-permute-done.5.refs_4_ = f32[1,64,256]{2,1,0:T(8,128)S(1)} collective-permute-done((f32[1,64,256]{2,1,0:T(8,128)S(1)}, f32[1,64,256]{2,1,0:T(8,128)S(1)}, u32[]{:S(2)}, u32[]{:S(2)}) %collective-permute-start.5) | collective-permute-done | bytes 65568 | tf_op jit(solution)/shard_map/ppermute | solution.py:416
  15.9 0.2 shard_map.73.refs_1_.refs_2_
  16.0 0.1 collective-permute-start.6
  16.1 0.3 shard_map.74.refs_1_
  16.4 1.2 %collective-permute-done.6.refs_3_.refs_2_ = f32[264,256]{1,0:T(8,128)S(1)} collective-permute-done((f32[264,256]{1,0:T(8,128)S(1)}, f32[264,256]{1,0:T(8,128)S(1)}, u32[]{:S(2)}, u32[]{:S(2)}) %collective-permute-start.6) | collective-permute-done | bytes 270368 | tf_op jit(solution)/shard_map/ppermute | solution.py:459
  17.6 0.3 shard_map.75
  17.9 1.9 %collective-permute-start.7 = (f32[264,256]{1,0:T(8,128)S(1)}, f32[264,256]{1,0:T(8,128)S(1)}, u32[]{:S(2)}, u32[]{:S(2)}) collective-permute-start(f32[264,256]{1,0:T(8,128)S(1)} %get-tuple-element.38.refs_3_), channel_id=1, source_target_pairs={{0,1},{1,0},{2,3},{3,2},{4,6},{5,7},{6,4},{7,5},{8,9},{9,8},{10,11... | collective-permute-start | bytes 811016 | tf_op jit(solution)/shard_map/ppermute | solution.py:468
  19.8 0.2 shard_map.77
  20.0 1.8 %collective-permute-start.9 = (f32[256,256]{1,0:T(8,128)S(1)}, f32[256,256]{1,0:T(8,128)S(1)}, u32[]{:S(2)}, u32[]{:S(2)}) collective-permute-start(f32[256,256]{1,0:T(8,128)S(1)} %get-tuple-element.42), channel_id=1, source_target_pairs={{0,8},{4,12},{8,0},{12,4},{16,24},{20,28},{24,16},{28,20},{1,9},{5... | collective-permute-start | bytes 786440 | tf_op jit(solution)/shard_map/ppermute | solution.py:509
  21.8 2.7 %collective-permute-done.7.refs_1_ = f32[264,256]{1,0:T(8,128)S(1)} collective-permute-done((f32[264,256]{1,0:T(8,128)S(1)}, f32[264,256]{1,0:T(8,128)S(1)}, u32[]{:S(2)}, u32[]{:S(2)}) %collective-permute-start.7) | collective-permute-done | bytes 270368 | tf_op jit(solution)/shard_map/ppermute | solution.py:468
  24.4 0.1 shard_map.76
  24.5 1.9 %collective-permute-start.8 = (f32[136,256]{1,0:T(8,128)S(1)}, f32[136,256]{1,0:T(8,128)S(1)}, u32[]{:S(2)}, u32[]{:S(2)}) collective-permute-start(f32[136,256]{1,0:T(8,128)S(1)} %get-tuple-element.40.refs_2_), channel_id=1, source_target_pairs={{0,2},{1,3},{2,0},{3,1},{4,5},{5,4},{6,7},{7,6},{8,10},{9,11},{10,... | collective-permute-start | bytes 417800 | tf_op jit(solution)/shard_map/ppermute | solution.py:468
  26.4 1.8 %collective-permute-done.9.refs_1_ = f32[256,256]{1,0:T(8,128)S(1)} collective-permute-done((f32[256,256]{1,0:T(8,128)S(1)}, f32[256,256]{1,0:T(8,128)S(1)}, u32[]{:S(2)}, u32[]{:S(2)}) %collective-permute-start.9) | collective-permute-done | bytes 262176 | tf_op jit(solution)/shard_map/ppermute | solution.py:509
  28.2 0.1 shard_map.78
  28.2 0.5 %collective-permute-start.12 = (f32[128,256]{1,0:T(8,128)S(1)}, f32[128,256]{1,0:T(8,128)S(1)}, u32[]{:S(2)}, u32[]{:S(2)}) collective-permute-start(f32[128,256]{1,0:T(8,128)S(1)} %get-tuple-element.43.refs_2_), channel_id=1, source_target_pairs={{0,2},{1,3},{2,0},{3,1},{4,5},{5,4},{6,7},{7,6},{8,10},{9,11},{10,... | collective-permute-start | bytes 393224 | tf_op jit(solution)/shard_map/ppermute | solution.py:468
  28.8 0.8 %collective-permute-done.8.refs_1_ = f32[136,256]{1,0:T(8,128)S(1)} collective-permute-done((f32[136,256]{1,0:T(8,128)S(1)}, f32[136,256]{1,0:T(8,128)S(1)}, u32[]{:S(2)}, u32[]{:S(2)}) %collective-permute-start.8) | collective-permute-done | bytes 139296 | tf_op jit(solution)/shard_map/ppermute | solution.py:468
  29.6 3.0 %collective-permute-start.10 = (f32[72,256]{1,0:T(8,128)S(1)}, f32[72,256]{1,0:T(8,128)S(1)}, u32[]{:S(2)}, u32[]{:S(2)}) collective-permute-start(f32[72,256]{1,0:T(8,128)S(1)} %get-tuple-element.45.refs_2_), channel_id=1, source_target_pairs={{0,16},{4,20},{8,24},{12,28},{16,0},{20,4},{24,8},{28,12},{1,17},{... | collective-permute-start | bytes 221192 | tf_op jit(solution)/shard_map/ppermute | solution.py:524
  32.7 1.6 %collective-permute-start.11 = (f32[72,256]{1,0:T(8,128)S(1)}, f32[72,256]{1,0:T(8,128)S(1)}, u32[]{:S(2)}, u32[]{:S(2)}) collective-permute-start(f32[72,256]{1,0:T(8,128)S(1)} %get-tuple-element.46), channel_id=1, source_target_pairs={{0,24},{4,28},{8,16},{12,20},{16,8},{20,12},{24,0},{28,4},{1,25},{... | collective-permute-start | bytes 221192 | tf_op jit(solution)/shard_map/ppermute | solution.py:524
  34.3 0.0 collective-permute-done.12.refs_1_
  34.3 1.5 %collective-permute-start.13 = (f32[64,256]{1,0:T(8,128)S(1)}, f32[64,256]{1,0:T(8,128)S(1)}, u32[]{:S(2)}, u32[]{:S(2)}) collective-permute-start(f32[64,256]{1,0:T(8,128)S(1)} %get-tuple-element.49), channel_id=1, source_target_pairs={{0,1},{1,0},{2,3},{3,2},{4,6},{5,7},{6,4},{7,5},{8,9},{9,8},{10,11... | collective-permute-start | bytes 196616 | tf_op jit(solution)/shard_map/ppermute | solution.py:468
  35.9 2.8 %collective-permute-done.13.refs_4_ = f32[64,256]{1,0:T(8,128)S(1)} collective-permute-done((f32[64,256]{1,0:T(8,128)S(1)}, f32[64,256]{1,0:T(8,128)S(1)}, u32[]{:S(2)}, u32[]{:S(2)}) %collective-permute-start.13) | collective-permute-done | bytes 65568 | tf_op jit(solution)/shard_map/ppermute | solution.py:468
  38.7 0.0 collective-permute-done.10.refs_1_
  38.7 0.3 collective-permute-done.11.refs_2_
  38.9 0.6 %shard_map.81 = (f32[64,256]{1,0:T(8,128)}, f32[1,256]{1,0:T(1,128)}, f32[1,256]{1,0:T(1,128)}) custom-call(f32[8,256]{1,0:T(8,128)S(1)} %get-tuple-element.44.refs_0_, f32[72,256]{1,0:T(8,128)S(1)} %collective-permute-done.10.refs_1_, f32[72,256]{1,0:T(8,128)S(1)} %collective-permute-done.11.refs_2_, f32[64,256]{1,0:T(8,128)S(1)} %get-tuple-element.48.refs_3_, ...), custom_call_target="tpu_custom_call" | custom-call | tf_op jit(solution)/shard_map/pallas_call | solution.py:42
  (3 shorter events, 0.1 us)
Async XLA Ops:
  2.4 2.0 %collective-permute-start = (f32[4,64,256]{2,1,0:T(8,128)S(1)}, f32[4,64,256]{2,1,0:T(8,128)S(1)}, u32[]{:S(2)}, u32[]{:S(2)}) collective-permute-start(f32[4,64,256]{2,1,0:T(8,128)S(1)} %get-tuple-element.32), channel_id=1, source_target_pairs={{0,4},{4,0},{8,12},{12,8},{16,20},{20,16},{24,28},{28,24},{1,5},{5... | collective-permute-start | bytes 786440 | tf_op jit(solution)/shard_map/ppermute | solution.py:381
  4.7 8.9 %collective-permute-start.1 = (f32[2,128,1024]{2,1,0:T(8,128)S(1)}, f32[2,128,1024]{2,1,0:T(8,128)S(1)}, u32[]{:S(2)}, u32[]{:S(2)}) collective-permute-start(f32[2,128,1024]{2,1,0:T(8,128)S(1)} %shard_map.70), channel_id=1, source_target_pairs={{0,4},{4,0},{8,12},{12,8},{16,20},{20,16},{24,28},{28,24},{1,5},{5... | collective-permute-start | bytes 3145736 | tf_op jit(solution)/shard_map/ppermute | solution.py:409
  4.8 5.3 %collective-permute-start.4 = (f32[1,64,256]{2,1,0:T(8,128)S(1)}, f32[1,64,256]{2,1,0:T(8,128)S(1)}, u32[]{:S(2)}, u32[]{:S(2)}) collective-permute-start(f32[1,64,256]{2,1,0:T(8,128)S(1)} %get-tuple-element.33.refs_1_), channel_id=1, source_target_pairs={{0,8},{4,12},{8,0},{12,4},{16,24},{20,28},{24,16},{28,20},{1,9},{5... | collective-permute-start | bytes 196616 | tf_op jit(solution)/shard_map/ppermute | solution.py:412
  7.8 5.8 %collective-permute-start.2 = (f32[64,256]{1,0:T(8,128)S(1)}, f32[64,256]{1,0:T(8,128)S(1)}, u32[]{:S(2)}, u32[]{:S(2)}) collective-permute-start(f32[64,256]{1,0:T(8,128)S(1)} %get-tuple-element.34.refs_0_.refs_2_), channel_id=1, source_target_pairs={{0,8},{4,12},{8,0},{12,4},{16,24},{20,28},{24,16},{28,20},{1,9},{5... | collective-permute-start | bytes 196616 | tf_op jit(solution)/shard_map/ppermute | solution.py:413
  7.9 5.8 %collective-permute-start.3 = (f32[64,256]{1,0:T(8,128)S(1)}, f32[64,256]{1,0:T(8,128)S(1)}, u32[]{:S(2)}, u32[]{:S(2)}) collective-permute-start(f32[64,256]{1,0:T(8,128)S(1)} %get-tuple-element.34.refs_0_.refs_2_), channel_id=1, source_target_pairs={{8,16},{12,20},{16,8},{20,12},{0,4},{4,0},{24,28},{28,24},{9,17},{... | collective-permute-start | bytes 196616 | tf_op jit(solution)/shard_map/ppermute | solution.py:414
  10.2 5.6 %collective-permute-start.5 = (f32[1,64,256]{2,1,0:T(8,128)S(1)}, f32[1,64,256]{2,1,0:T(8,128)S(1)}, u32[]{:S(2)}, u32[]{:S(2)}) collective-permute-start(f32[1,64,256]{2,1,0:T(8,128)S(1)} %shard_map.72), channel_id=1, source_target_pairs={{0,16},{4,20},{8,24},{12,28},{16,0},{20,4},{24,8},{28,12},{1,17},{... | collective-permute-start | bytes 196616 | tf_op jit(solution)/shard_map/ppermute | solution.py:416
  16.0 1.6 %collective-permute-start.6 = (f32[264,256]{1,0:T(8,128)S(1)}, f32[264,256]{1,0:T(8,128)S(1)}, u32[]{:S(2)}, u32[]{:S(2)}) collective-permute-start(f32[264,256]{1,0:T(8,128)S(1)} %shard_map.73.refs_1_.refs_2_), channel_id=1, source_target_pairs={{0,4},{4,0},{8,12},{12,8},{16,20},{20,16},{24,28},{28,24},{1,5},{5... | collective-permute-start | bytes 811016 | tf_op jit(solution)/shard_map/ppermute | solution.py:459
  17.9 6.5 %collective-permute-start.7 = (f32[264,256]{1,0:T(8,128)S(1)}, f32[264,256]{1,0:T(8,128)S(1)}, u32[]{:S(2)}, u32[]{:S(2)}) collective-permute-start(f32[264,256]{1,0:T(8,128)S(1)} %get-tuple-element.38.refs_3_), channel_id=1, source_target_pairs={{0,1},{1,0},{2,3},{3,2},{4,6},{5,7},{6,4},{7,5},{8,9},{9,8},{10,11... | collective-permute-start | bytes 811016 | tf_op jit(solution)/shard_map/ppermute | solution.py:468
  20.0 8.2 %collective-permute-start.9 = (f32[256,256]{1,0:T(8,128)S(1)}, f32[256,256]{1,0:T(8,128)S(1)}, u32[]{:S(2)}, u32[]{:S(2)}) collective-permute-start(f32[256,256]{1,0:T(8,128)S(1)} %get-tuple-element.42), channel_id=1, source_target_pairs={{0,8},{4,12},{8,0},{12,4},{16,24},{20,28},{24,16},{28,20},{1,9},{5... | collective-permute-start | bytes 786440 | tf_op jit(solution)/shard_map/ppermute | solution.py:509
  24.5 5.1 %collective-permute-start.8 = (f32[136,256]{1,0:T(8,128)S(1)}, f32[136,256]{1,0:T(8,128)S(1)}, u32[]{:S(2)}, u32[]{:S(2)}) collective-permute-start(f32[136,256]{1,0:T(8,128)S(1)} %get-tuple-element.40.refs_2_), channel_id=1, source_target_pairs={{0,2},{1,3},{2,0},{3,1},{4,5},{5,4},{6,7},{7,6},{8,10},{9,11},{10,... | collective-permute-start | bytes 417800 | tf_op jit(solution)/shard_map/ppermute | solution.py:468
  28.2 6.1 %collective-permute-start.12 = (f32[128,256]{1,0:T(8,128)S(1)}, f32[128,256]{1,0:T(8,128)S(1)}, u32[]{:S(2)}, u32[]{:S(2)}) collective-permute-start(f32[128,256]{1,0:T(8,128)S(1)} %get-tuple-element.43.refs_2_), channel_id=1, source_target_pairs={{0,2},{1,3},{2,0},{3,1},{4,5},{5,4},{6,7},{7,6},{8,10},{9,11},{10,... | collective-permute-start | bytes 393224 | tf_op jit(solution)/shard_map/ppermute | solution.py:468
  29.6 9.0 %collective-permute-start.10 = (f32[72,256]{1,0:T(8,128)S(1)}, f32[72,256]{1,0:T(8,128)S(1)}, u32[]{:S(2)}, u32[]{:S(2)}) collective-permute-start(f32[72,256]{1,0:T(8,128)S(1)} %get-tuple-element.45.refs_2_), channel_id=1, source_target_pairs={{0,16},{4,20},{8,24},{12,28},{16,0},{20,4},{24,8},{28,12},{1,17},{... | collective-permute-start | bytes 221192 | tf_op jit(solution)/shard_map/ppermute | solution.py:524
  32.7 6.3 %collective-permute-start.11 = (f32[72,256]{1,0:T(8,128)S(1)}, f32[72,256]{1,0:T(8,128)S(1)}, u32[]{:S(2)}, u32[]{:S(2)}) collective-permute-start(f32[72,256]{1,0:T(8,128)S(1)} %get-tuple-element.46), channel_id=1, source_target_pairs={{0,24},{4,28},{8,16},{12,20},{16,8},{20,12},{24,0},{28,4},{1,25},{... | collective-permute-start | bytes 221192 | tf_op jit(solution)/shard_map/ppermute | solution.py:524
  34.3 4.3 %collective-permute-start.13 = (f32[64,256]{1,0:T(8,128)S(1)}, f32[64,256]{1,0:T(8,128)S(1)}, u32[]{:S(2)}, u32[]{:S(2)}) collective-permute-start(f32[64,256]{1,0:T(8,128)S(1)} %get-tuple-element.49), channel_id=1, source_target_pairs={{0,1},{1,0},{2,3},{3,2},{4,6},{5,7},{6,4},{7,5},{8,9},{9,8},{10,11... | collective-permute-start | bytes 196616 | tf_op jit(solution)/shard_map/ppermute | solution.py:468

commit v9 on v8

--- a/solution.py
+++ b/solution.py
@@ -115,7 +115,7 @@
     return [level, total]
 
 
-def local_body(rounds, keep, other, score, level, total, message):
+def local_body(rounds, keep, other, since, peak_out, level, total, message):
     dates = keep.shape[0] // 2
     first = core_of() == 0
     run = jnp.zeros(keep.shape[1:], f32)
@@ -128,9 +128,12 @@
             run = run + inc
             scores.append(base - run)
     peak = functools.reduce(jnp.maximum, scores)
-    lev = peak + jnp.log(sum(jnp.exp(s - peak) for s in scores))
-    for i, s in enumerate(scores):
-        score[i] = s
+    run_since = jnp.zeros_like(peak)
+    for i in reversed(range(len(scores))):
+        run_since = run_since + jnp.exp(scores[i] - peak)
+        since[i] = run_since
+    lev = peak + jnp.log(run_since)
+    peak_out[...] = peak
     level[...] = lev
     total[...] = run
     left = chip_of() % 2 == 0
@@ -193,19 +196,19 @@
     return before, after, jnp.where(first, 0.0, beside[...])
 
 
-def tail_body(join, score, level, total, *refs):
+def tail_body(join, since, peak, level, total, *refs):
     *given, out = refs
     lev, tot = level[...], total[...]
     before, after, sum_before = join(*given, jnp.zeros_like(lev))
     later = after - tot
     norm = log_add(log_add(before, lev), later)
-    run = jnp.exp(later - norm)
-    half = score.shape[1]
-    for i in reversed(range(score.shape[0])):
-        run = run + jnp.exp(score[i] - norm)
+    rest, factor = jnp.exp(later - norm), jnp.exp(peak[...] - norm)
+    half = since.shape[1]
+    for i in range(since.shape[0]):
+        run = rest + factor * since[i]
         out[i * half : (i + 1) * half, :] = run.astype(bf16).astype(f32)
     smoothed = TEMP * (norm - sum_before)
-    at = score.shape[0] * half
+    at = since.shape[0] * half
     out[at : at + STAT_ROWS, :] = jnp.zeros((STAT_ROWS, smoothed.shape[1]), f32)
     out[at : at + 1, :] = jnp.sum(smoothed, axis=0, keepdims=True)
     out[at + 1 : at + 2, :] = jnp.sum(smoothed * smoothed, axis=0, keepdims=True)
@@ -337,21 +340,31 @@
 
 def part_sum_body(rows, mine, got, *outs):
     total = mine[...] + got[...]
-    chips = len(outs) - 1
-    for k, out in enumerate(outs[:chips]):
-        out[0:rows, :] = total[k * rows : (k + 1) * rows, :]
-        out[rows:, :] = total[chips * rows :, :]
-    outs[-1][...] = total[chips * rows :, :]
-
-
-def date_sum_body(chips, paths_total, stats, across, *refs):
+    *messages, stats = outs
+    half = total.shape[1] // 2
+    sums = total[len(messages) * rows :, :]
+    for k, out in enumerate(messages):
+        block = total[k * rows : (k + 1) * rows, :]
+        out[2 * rows :, :] = jnp.zeros((STAT_ROWS, half), f32)
+        for side_, columns in enumerate((slice(0, half), slice(half, None))):
+            out[side_ * rows : (side_ + 1) * rows, :] = block[:, columns]
+            out[2 * rows + 2 * side_ : 2 * rows + 2 * side_ + 2, :] = sums[0:2, columns]
+    stats[...] = sums
+
+
+def date_sum_body(chips, far, paths_total, stats, *refs):
     parts, (gradient, bound, spread) = refs[:-3], refs[-3:]
-    rows = gradient.shape[0]
-    gradient[...] = functools.reduce(lambda a, b: a + b, (p[:rows, :] for p in parts), across[:rows, :])
-    sums = jnp.where(chip_of() < chips // 2, stats[...], across[rows:, :])
-    mean = sums[0:1, :] * (1.0 / paths_total)
-    bound[...] = mean
-    spread[...] = sums[1:2, :] * (1.0 / paths_total) - mean * mean
+    rows, contracts = gradient.shape
+    half = contracts // 2
+    first = chip_of() < chips // 2
+    for side_, columns in enumerate((slice(0, half), slice(half, contracts))):
+        at, behind = side_ * rows, 2 * rows + 2 * side_
+        total = functools.reduce(lambda a, b: a + b, (p[:, columns] for p in parts[far:]))
+        gradient[:, columns] = functools.reduce(lambda a, b: a + b, (p[at : at + rows, :] for p in parts[:far]), total)
+        sums = jnp.where(first, stats[0:2, columns], parts[0][behind : behind + 2, :])
+        mean = sums[0:1, :] * (1.0 / paths_total)
+        bound[:, columns] = mean
+        spread[:, columns] = sums[1:2, :] * (1.0 / paths_total) - mean * mean
 
 
 def shards(features, payoff, coefficients, exercise):
@@ -393,9 +406,9 @@
         place=[pltpu.HBM] * 3,
     )
     sizes = [1 if step + 1 == rounds or rounds == 2 else 2 for step in range(rounds)] or [2]
-    score, level, total, message = call(
+    since, peak, level, total, message = call(
         functools.partial(local_body, rounds),
-        [((2 * dates, *plane), f32), (plane, f32), (plane, f32), ((sizes[0], *plane), f32)],
+        [((2 * dates, *plane), f32)] + [(plane, f32)] * 3 + [((sizes[0], *plane), f32)],
         keep,
         other,
     )
@@ -449,7 +462,8 @@
     (tail,) = call(
         functools.partial(tail_body, join),
         [((2 * dates * half + STAT_ROWS, contracts), f32)],
-        score,
+        since,
+        peak,
         own_level,
         own_total,
         *given,
@@ -515,7 +529,7 @@
         near_parts = [near_keep, over_path(step - 1, near_message, True)]
     *sums, stats = call(
         functools.partial(part_sum_body, rows),
-        [piece(1, 1, True)] * len(far) + [((STAT_ROWS, contracts), f32)],
+        [((2 * rows + STAT_ROWS, contracts // 2), f32)] * len(far) + [((STAT_ROWS, contracts), f32)],
         keep,
         got,
         near_message,
@@ -525,7 +539,7 @@
     near_keep, near_message = next_round(steps - 1, near_parts, sums[:1], 1, False)
     over += [near_keep, over_path(steps - 1, near_message, True)]
     gradient, bound, spread = call(
-        functools.partial(date_sum_body, chips, paths_total),
+        functools.partial(date_sum_body, chips, len(far), paths_total),
         [((rows, contracts), f32), ((1, contracts), f32), ((1, contracts), f32)],
         stats,
         *over,

time: 39.7 us -> 39.7 us (level)
  no operation moved by 1% of the time
where the time goes in v9:
time: 39.7 us; the launch traced here: 39.5 us
  starting transfers between devices  19.5 us (49%)
  waiting for transfers between devices  13.7 us (35%)
  Pallas kernels  5.6 us (14%)
  between operations  0.74 us (2%)
    ppermute x3, starting transfers between devices, shards(): lax.ppermute(x, 'date', date_pairs(chips, j))  6.43 us
    ppermute x4, waiting for transfers between devices, over_path(): lax.ppermute(message, ('date', 'path'), path_pairs(chips, count, step, ne...  6.28 us
    ppermute x4, starting transfers between devices, over_path(): lax.ppermute(message, ('date', 'path'), path_pairs(chips, count, step, ne...  5.85 us
    pallas_call x15, Pallas kernels, call(): pl.pallas_call(kernel, out_shape=[jax.ShapeDtypeStruct(*o) for o in outs]...  5.6 us
    ppermute x1, starting transfers between devices, shards(): far = lax.ppermute(message, 'date', date_pairs(chips, 2))  3.4 us
    ppermute x1, starting transfers between devices, shards(): near = lax.ppermute(message, 'date', date_pairs(chips, 1))  3.02 us
    ppermute x1, waiting for transfers between devices, shards(): near = lax.ppermute(message, 'date', date_pairs(chips, 1))  2.3 us
    ppermute x3, waiting for transfers between devices, shards(): lax.ppermute(x, 'date', date_pairs(chips, j))  2 us
  transfers between devices with their start and end apart: 14, of which 8 were waited for; matrix products, arithmetic and copies ran while one was open for 0% of the time, Pallas kernels for 6%

profile of v9, /device:TPU:0, one launch (start us, length us, event | category | flops | bytes accessed | tf_op | source)
XLA Modules:
  0.0 39.5 jit_solution(5412448074458209432)
XLA Ops:
  0.6 1.8 %shard_map.67 = (f32[4,64,256]{2,1,0:T(8,128)S(1)}, bf16[2,64,2048]{2,1,0:T(8,128)(2,1)S(1)}, bf16[2048,256]{1,0:T(8,128)(2,1)S(1)}) custom-call(bf16[2,128,2048]{2,1,0:T(8,128)(2,1)} %refs_0_.3, bf16[2048,256]{1,0:T(8,128)(2,1)} %refs_1_.2, f32[2,128,256]{2,1,0:T(8,128)} %refs_1_.3, s32[2,256]{1,0:T(2,128)} %refs_2_.3), custom_call_target="tpu_custom_call" | custom-call | tf_op jit(solution)/shard_map/pallas_call | solution.py:42
  2.4 0.5 %collective-permute-start = (f32[4,64,256]{2,1,0:T(8,128)S(1)}, f32[4,64,256]{2,1,0:T(8,128)S(1)}, u32[]{:S(2)}, u32[]{:S(2)}) collective-permute-start(f32[4,64,256]{2,1,0:T(8,128)S(1)} %get-tuple-element.33), channel_id=1, source_target_pairs={{0,4},{4,0},{8,12},{12,8},{16,20},{20,16},{24,28},{28,24},{1,5},{5... | collective-permute-start | bytes 786440 | tf_op jit(solution)/shard_map/ppermute | solution.py:394
  3.0 1.4 %shard_map.68 = (f32[4,64,256]{2,1,0:T(8,128)S(1)}, bf16[2,128,2048]{2,1,0:T(8,128)(2,1)S(1)}) custom-call(bf16[2,128,2048]{2,1,0:T(8,128)(2,1)} %refs_0_.3, f32[2,128,256]{2,1,0:T(8,128)} %refs_1_.3, s32[2,256]{1,0:T(2,128)} %refs_2_.3, bf16[2048,256]{1,0:T(8,128)(2,1)S(1)} %get-tuple-element.29.refs_3_, bf16[2,64,2048]{2,1,0:T(8,128)(2,1)S(1)} %get-tuple-element.30.refs_4_), custom_call_target="tpu_custom_call" | custom-call | tf_op jit(solution)/shard_map/pallas_call | solution.py:42
  4.4 0.0 collective-permute-done.refs_1_
  4.4 0.1 shard_map.69
  4.5 0.1 shard_map.70
  4.7 0.1 collective-permute-start.1
  4.8 3.0 %collective-permute-start.4 = (f32[1,64,256]{2,1,0:T(8,128)S(1)}, f32[1,64,256]{2,1,0:T(8,128)S(1)}, u32[]{:S(2)}, u32[]{:S(2)}) collective-permute-start(f32[1,64,256]{2,1,0:T(8,128)S(1)} %get-tuple-element.34.refs_1_), channel_id=1, source_target_pairs={{0,8},{4,12},{8,0},{12,4},{16,24},{20,28},{24,16},{28,20},{1,9},{5... | collective-permute-start | bytes 196616 | tf_op jit(solution)/shard_map/ppermute | solution.py:425
  7.8 0.0 collective-permute-start.2
  7.8 0.0 collective-permute-start.3
  7.8 2.3 %collective-permute-done.4.refs_2_.refs_4_ = f32[1,64,256]{2,1,0:T(8,128)S(1)} collective-permute-done((f32[1,64,256]{2,1,0:T(8,128)S(1)}, f32[1,64,256]{2,1,0:T(8,128)S(1)}, u32[]{:S(2)}, u32[]{:S(2)}) %collective-permute-start.4) | collective-permute-done | bytes 65568 | tf_op jit(solution)/shard_map/ppermute | solution.py:425
  10.2 3.4 %collective-permute-start.5 = (f32[1,64,256]{2,1,0:T(8,128)S(1)}, f32[1,64,256]{2,1,0:T(8,128)S(1)}, u32[]{:S(2)}, u32[]{:S(2)}) collective-permute-start(f32[1,64,256]{2,1,0:T(8,128)S(1)} %shard_map.72), channel_id=1, source_target_pairs={{0,16},{4,20},{8,24},{12,28},{16,0},{20,4},{24,8},{28,12},{1,17},{... | collective-permute-start | bytes 196616 | tf_op jit(solution)/shard_map/ppermute | solution.py:429
  13.6 0.0 collective-permute-done.2.refs_2_.refs_6_
  13.6 0.0 collective-permute-done.3.refs_3_.refs_7_
  13.6 0.0 collective-permute-done.1.refs_1_
  13.6 0.3 shard_map.71.refs_8_.refs_0_
  13.9 1.9 %collective-permute-done.5.refs_5_ = f32[1,64,256]{2,1,0:T(8,128)S(1)} collective-permute-done((f32[1,64,256]{2,1,0:T(8,128)S(1)}, f32[1,64,256]{2,1,0:T(8,128)S(1)}, u32[]{:S(2)}, u32[]{:S(2)}) %collective-permute-start.5) | collective-permute-done | bytes 65568 | tf_op jit(solution)/shard_map/ppermute | solution.py:429
  15.8 0.2 shard_map.73.refs_1_.refs_2_
  16.0 0.1 collective-permute-start.6
  16.1 0.3 shard_map.74.refs_1_
  16.4 1.2 %collective-permute-done.6.refs_3_.refs_2_ = f32[264,256]{1,0:T(8,128)S(1)} collective-permute-done((f32[264,256]{1,0:T(8,128)S(1)}, f32[264,256]{1,0:T(8,128)S(1)}, u32[]{:S(2)}, u32[]{:S(2)}) %collective-permute-start.6) | collective-permute-done | bytes 270368 | tf_op jit(solution)/shard_map/ppermute | solution.py:473
  17.6 0.3 shard_map.75
  17.9 1.9 %collective-permute-start.7 = (f32[264,256]{1,0:T(8,128)S(1)}, f32[264,256]{1,0:T(8,128)S(1)}, u32[]{:S(2)}, u32[]{:S(2)}) collective-permute-start(f32[264,256]{1,0:T(8,128)S(1)} %get-tuple-element.40.refs_3_), channel_id=1, source_target_pairs={{0,1},{1,0},{2,3},{3,2},{4,6},{5,7},{6,4},{7,5},{8,9},{9,8},{10,11... | collective-permute-start | bytes 811016 | tf_op jit(solution)/shard_map/ppermute | solution.py:482
  19.8 0.2 shard_map.77
  20.0 1.8 %collective-permute-start.9 = (f32[256,256]{1,0:T(8,128)S(1)}, f32[256,256]{1,0:T(8,128)S(1)}, u32[]{:S(2)}, u32[]{:S(2)}) collective-permute-start(f32[256,256]{1,0:T(8,128)S(1)} %get-tuple-element.44), channel_id=1, source_target_pairs={{0,8},{4,12},{8,0},{12,4},{16,24},{20,28},{24,16},{28,20},{1,9},{5... | collective-permute-start | bytes 786440 | tf_op jit(solution)/shard_map/ppermute | solution.py:523
  21.8 2.7 %collective-permute-done.7.refs_1_ = f32[264,256]{1,0:T(8,128)S(1)} collective-permute-done((f32[264,256]{1,0:T(8,128)S(1)}, f32[264,256]{1,0:T(8,128)S(1)}, u32[]{:S(2)}, u32[]{:S(2)}) %collective-permute-start.7) | collective-permute-done | bytes 270368 | tf_op jit(solution)/shard_map/ppermute | solution.py:482
  24.5 1.9 %collective-permute-start.8 = (f32[136,256]{1,0:T(8,128)S(1)}, f32[136,256]{1,0:T(8,128)S(1)}, u32[]{:S(2)}, u32[]{:S(2)}) collective-permute-start(f32[136,256]{1,0:T(8,128)S(1)} %get-tuple-element.42.refs_2_), channel_id=1, source_target_pairs={{0,2},{1,3},{2,0},{3,1},{4,5},{5,4},{6,7},{7,6},{8,10},{9,11},{10,... | collective-permute-start | bytes 417800 | tf_op jit(solution)/shard_map/ppermute | solution.py:482
  26.4 1.8 %collective-permute-done.9.refs_1_ = f32[256,256]{1,0:T(8,128)S(1)} collective-permute-done((f32[256,256]{1,0:T(8,128)S(1)}, f32[256,256]{1,0:T(8,128)S(1)}, u32[]{:S(2)}, u32[]{:S(2)}) %collective-permute-start.9) | collective-permute-done | bytes 262176 | tf_op jit(solution)/shard_map/ppermute | solution.py:523
  28.1 0.1 shard_map.78
  28.2 0.5 %collective-permute-start.12 = (f32[128,256]{1,0:T(8,128)S(1)}, f32[128,256]{1,0:T(8,128)S(1)}, u32[]{:S(2)}, u32[]{:S(2)}) collective-permute-start(f32[128,256]{1,0:T(8,128)S(1)} %get-tuple-element.45.refs_2_), channel_id=1, source_target_pairs={{0,2},{1,3},{2,0},{3,1},{4,5},{5,4},{6,7},{7,6},{8,10},{9,11},{10,... | collective-permute-start | bytes 393224 | tf_op jit(solution)/shard_map/ppermute | solution.py:482
  28.8 0.8 %collective-permute-done.8.refs_1_ = f32[136,256]{1,0:T(8,128)S(1)} collective-permute-done((f32[136,256]{1,0:T(8,128)S(1)}, f32[136,256]{1,0:T(8,128)S(1)}, u32[]{:S(2)}, u32[]{:S(2)}) %collective-permute-start.8) | collective-permute-done | bytes 139296 | tf_op jit(solution)/shard_map/ppermute | solution.py:482
  29.6 3.0 %collective-permute-start.10 = (f32[136,128]{1,0:T(8,128)S(1)}, f32[136,128]{1,0:T(8,128)S(1)}, u32[]{:S(2)}, u32[]{:S(2)}) collective-permute-start(f32[136,128]{1,0:T(8,128)S(1)} %get-tuple-element.47.refs_2_), channel_id=1, source_target_pairs={{0,16},{4,20},{8,24},{12,28},{16,0},{20,4},{24,8},{28,12},{1,17},{... | collective-permute-start | bytes 208904 | tf_op jit(solution)/shard_map/ppermute | solution.py:538
  32.6 1.6 %collective-permute-start.11 = (f32[136,128]{1,0:T(8,128)S(1)}, f32[136,128]{1,0:T(8,128)S(1)}, u32[]{:S(2)}, u32[]{:S(2)}) collective-permute-start(f32[136,128]{1,0:T(8,128)S(1)} %get-tuple-element.48), channel_id=1, source_target_pairs={{0,24},{4,28},{8,16},{12,20},{16,8},{20,12},{24,0},{28,4},{1,25},{... | collective-permute-start | bytes 208904 | tf_op jit(solution)/shard_map/ppermute | solution.py:538
  34.3 0.0 collective-permute-done.12.refs_1_
  34.3 1.5 %collective-permute-start.13 = (f32[64,256]{1,0:T(8,128)S(1)}, f32[64,256]{1,0:T(8,128)S(1)}, u32[]{:S(2)}, u32[]{:S(2)}) collective-permute-start(f32[64,256]{1,0:T(8,128)S(1)} %get-tuple-element.51), channel_id=1, source_target_pairs={{0,1},{1,0},{2,3},{3,2},{4,6},{5,7},{6,4},{7,5},{8,9},{9,8},{10,11... | collective-permute-start | bytes 196616 | tf_op jit(solution)/shard_map/ppermute | solution.py:482
  35.9 2.8 %collective-permute-done.13.refs_4_ = f32[64,256]{1,0:T(8,128)S(1)} collective-permute-done((f32[64,256]{1,0:T(8,128)S(1)}, f32[64,256]{1,0:T(8,128)S(1)}, u32[]{:S(2)}, u32[]{:S(2)}) %collective-permute-start.13) | collective-permute-done | bytes 65568 | tf_op jit(solution)/shard_map/ppermute | solution.py:482
  38.6 0.0 collective-permute-done.10.refs_1_
  38.6 0.2 collective-permute-done.11.refs_2_
  38.9 0.6 %shard_map.81 = (f32[64,256]{1,0:T(8,128)}, f32[1,256]{1,0:T(1,128)}, f32[1,256]{1,0:T(1,128)}) custom-call(f32[8,256]{1,0:T(8,128)S(1)} %get-tuple-element.46.refs_0_, f32[136,128]{1,0:T(8,128)S(1)} %collective-permute-done.10.refs_1_, f32[136,128]{1,0:T(8,128)S(1)} %collective-permute-done.11.refs_2_, f32[64,256]{1,0:T(8,128)S(1)} %get-tuple-element.50.refs_3_, ...), custom_call_target="tpu_custom_call" | custom-call | tf_op jit(solution)/shard_map/pallas_call | solution.py:42
  (4 shorter events, 0.1 us)
Async XLA Ops:
  2.4 2.0 %collective-permute-start = (f32[4,64,256]{2,1,0:T(8,128)S(1)}, f32[4,64,256]{2,1,0:T(8,128)S(1)}, u32[]{:S(2)}, u32[]{:S(2)}) collective-permute-start(f32[4,64,256]{2,1,0:T(8,128)S(1)} %get-tuple-element.33), channel_id=1, source_target_pairs={{0,4},{4,0},{8,12},{12,8},{16,20},{20,16},{24,28},{28,24},{1,5},{5... | collective-permute-start | bytes 786440 | tf_op jit(solution)/shard_map/ppermute | solution.py:394
  4.7 8.9 %collective-permute-start.1 = (f32[2,128,1024]{2,1,0:T(8,128)S(1)}, f32[2,128,1024]{2,1,0:T(8,128)S(1)}, u32[]{:S(2)}, u32[]{:S(2)}) collective-permute-start(f32[2,128,1024]{2,1,0:T(8,128)S(1)} %shard_map.70), channel_id=1, source_target_pairs={{0,4},{4,0},{8,12},{12,8},{16,20},{20,16},{24,28},{28,24},{1,5},{5... | collective-permute-start | bytes 3145736 | tf_op jit(solution)/shard_map/ppermute | solution.py:422
  4.8 5.4 %collective-permute-start.4 = (f32[1,64,256]{2,1,0:T(8,128)S(1)}, f32[1,64,256]{2,1,0:T(8,128)S(1)}, u32[]{:S(2)}, u32[]{:S(2)}) collective-permute-start(f32[1,64,256]{2,1,0:T(8,128)S(1)} %get-tuple-element.34.refs_1_), channel_id=1, source_target_pairs={{0,8},{4,12},{8,0},{12,4},{16,24},{20,28},{24,16},{28,20},{1,9},{5... | collective-permute-start | bytes 196616 | tf_op jit(solution)/shard_map/ppermute | solution.py:425
  7.8 5.8 %collective-permute-start.2 = (f32[64,256]{1,0:T(8,128)S(1)}, f32[64,256]{1,0:T(8,128)S(1)}, u32[]{:S(2)}, u32[]{:S(2)}) collective-permute-start(f32[64,256]{1,0:T(8,128)S(1)} %get-tuple-element.35.refs_0_.refs_3_), channel_id=1, source_target_pairs={{0,8},{4,12},{8,0},{12,4},{16,24},{20,28},{24,16},{28,20},{1,9},{5... | collective-permute-start | bytes 196616 | tf_op jit(solution)/shard_map/ppermute | solution.py:426
  7.8 5.8 %collective-permute-start.3 = (f32[64,256]{1,0:T(8,128)S(1)}, f32[64,256]{1,0:T(8,128)S(1)}, u32[]{:S(2)}, u32[]{:S(2)}) collective-permute-start(f32[64,256]{1,0:T(8,128)S(1)} %get-tuple-element.35.refs_0_.refs_3_), channel_id=1, source_target_pairs={{8,16},{12,20},{16,8},{20,12},{0,4},{4,0},{24,28},{28,24},{9,17},{... | collective-permute-start | bytes 196616 | tf_op jit(solution)/shard_map/ppermute | solution.py:427
  10.2 5.6 %collective-permute-start.5 = (f32[1,64,256]{2,1,0:T(8,128)S(1)}, f32[1,64,256]{2,1,0:T(8,128)S(1)}, u32[]{:S(2)}, u32[]{:S(2)}) collective-permute-start(f32[1,64,256]{2,1,0:T(8,128)S(1)} %shard_map.72), channel_id=1, source_target_pairs={{0,16},{4,20},{8,24},{12,28},{16,0},{20,4},{24,8},{28,12},{1,17},{... | collective-permute-start | bytes 196616 | tf_op jit(solution)/shard_map/ppermute | solution.py:429
  16.0 1.6 %collective-permute-start.6 = (f32[264,256]{1,0:T(8,128)S(1)}, f32[264,256]{1,0:T(8,128)S(1)}, u32[]{:S(2)}, u32[]{:S(2)}) collective-permute-start(f32[264,256]{1,0:T(8,128)S(1)} %shard_map.73.refs_1_.refs_2_), channel_id=1, source_target_pairs={{0,4},{4,0},{8,12},{12,8},{16,20},{20,16},{24,28},{28,24},{1,5},{5... | collective-permute-start | bytes 811016 | tf_op jit(solution)/shard_map/ppermute | solution.py:473
  17.9 6.5 %collective-permute-start.7 = (f32[264,256]{1,0:T(8,128)S(1)}, f32[264,256]{1,0:T(8,128)S(1)}, u32[]{:S(2)}, u32[]{:S(2)}) collective-permute-start(f32[264,256]{1,0:T(8,128)S(1)} %get-tuple-element.40.refs_3_), channel_id=1, source_target_pairs={{0,1},{1,0},{2,3},{3,2},{4,6},{5,7},{6,4},{7,5},{8,9},{9,8},{10,11... | collective-permute-start | bytes 811016 | tf_op jit(solution)/shard_map/ppermute | solution.py:482
  20.0 8.2 %collective-permute-start.9 = (f32[256,256]{1,0:T(8,128)S(1)}, f32[256,256]{1,0:T(8,128)S(1)}, u32[]{:S(2)}, u32[]{:S(2)}) collective-permute-start(f32[256,256]{1,0:T(8,128)S(1)} %get-tuple-element.44), channel_id=1, source_target_pairs={{0,8},{4,12},{8,0},{12,4},{16,24},{20,28},{24,16},{28,20},{1,9},{5... | collective-permute-start | bytes 786440 | tf_op jit(solution)/shard_map/ppermute | solution.py:523
  24.5 5.1 %collective-permute-start.8 = (f32[136,256]{1,0:T(8,128)S(1)}, f32[136,256]{1,0:T(8,128)S(1)}, u32[]{:S(2)}, u32[]{:S(2)}) collective-permute-start(f32[136,256]{1,0:T(8,128)S(1)} %get-tuple-element.42.refs_2_), channel_id=1, source_target_pairs={{0,2},{1,3},{2,0},{3,1},{4,5},{5,4},{6,7},{7,6},{8,10},{9,11},{10,... | collective-permute-start | bytes 417800 | tf_op jit(solution)/shard_map/ppermute | solution.py:482
  28.2 6.1 %collective-permute-start.12 = (f32[128,256]{1,0:T(8,128)S(1)}, f32[128,256]{1,0:T(8,128)S(1)}, u32[]{:S(2)}, u32[]{:S(2)}) collective-permute-start(f32[128,256]{1,0:T(8,128)S(1)} %get-tuple-element.45.refs_2_), channel_id=1, source_target_pairs={{0,2},{1,3},{2,0},{3,1},{4,5},{5,4},{6,7},{7,6},{8,10},{9,11},{10,... | collective-permute-start | bytes 393224 | tf_op jit(solution)/shard_map/ppermute | solution.py:482
  29.6 9.0 %collective-permute-start.10 = (f32[136,128]{1,0:T(8,128)S(1)}, f32[136,128]{1,0:T(8,128)S(1)}, u32[]{:S(2)}, u32[]{:S(2)}) collective-permute-start(f32[136,128]{1,0:T(8,128)S(1)} %get-tuple-element.47.refs_2_), channel_id=1, source_target_pairs={{0,16},{4,20},{8,24},{12,28},{16,0},{20,4},{24,8},{28,12},{1,17},{... | collective-permute-start | bytes 208904 | tf_op jit(solution)/shard_map/ppermute | solution.py:538
  32.6 6.2 %collective-permute-start.11 = (f32[136,128]{1,0:T(8,128)S(1)}, f32[136,128]{1,0:T(8,128)S(1)}, u32[]{:S(2)}, u32[]{:S(2)}) collective-permute-start(f32[136,128]{1,0:T(8,128)S(1)} %get-tuple-element.48), channel_id=1, source_target_pairs={{0,24},{4,28},{8,16},{12,20},{16,8},{20,12},{24,0},{28,4},{1,25},{... | collective-permute-start | bytes 208904 | tf_op jit(solution)/shard_map/ppermute | solution.py:538
  34.3 4.3 %collective-permute-start.13 = (f32[64,256]{1,0:T(8,128)S(1)}, f32[64,256]{1,0:T(8,128)S(1)}, u32[]{:S(2)}, u32[]{:S(2)}) collective-permute-start(f32[64,256]{1,0:T(8,128)S(1)} %get-tuple-element.51), channel_id=1, source_target_pairs={{0,1},{1,0},{2,3},{3,2},{4,6},{5,7},{6,4},{7,5},{8,9},{9,8},{10,11... | collective-permute-start | bytes 196616 | tf_op jit(solution)/shard_map/ppermute | solution.py:482

commit v10 on v9

--- a/solution.py
+++ b/solution.py
@@ -256,44 +256,70 @@
     return begun[at, :] + scale * jnp.dot(side(columns, at, 1 - core_of()), right, preferred_element_type=f32)
 
 
-def far_body(scale, far, columns, begun, own, got, keep, message, product):
+def far_half(scale, far, mine, columns, begun, own, got, out, product):
     size = columns.shape[1] // 2
     right = got[:size, :].astype(bf16)
-    _, count, rows, _ = product.shape
-    for k, j in enumerate(far):
-        product[k] = rows_of(scale, j, count * rows, columns, begun, right).reshape(product.shape[1:])
-    halve(0, False, product, own[size:, :] + got[size:, :], keep, message)
-
-
-def near_body(scale, near, columns, begun, got, *outs):
+    count, rows, _ = product.shape
+    bit, place = round_of(0, False)
+    value = (lax.axis_index("path") >> bit) & 1
+    value = value if mine else 1 - value
+    start = 0
+    for j in far:
+        chip = partner(chip_of(), j, begun.shape[0] // (count * rows))
+        if rows % 16:
+            product[...] = rows_of(scale, j, count * rows, columns, begun, right).reshape(product.shape)
+        for i in range(count // 2):
+            path = place_of(i, value, place)
+            if rows % 16:
+                block = product[path]
+            else:
+                at = pl.ds(pl.multiple_of((chip * count + path) * rows, rows), rows)
+                block = jnp.dot(side(columns, at, 1 - core_of()), right, preferred_element_type=f32)
+                block = begun[at, :] + scale * block
+            out[start : start + rows, :] = block
+            start += rows
+    out[start:, :] = own[size:, :] + got[size:, :]
+
+
+def near_body(scale, far, near, columns, begun, own, got, keep, *refs):
+    *outs, product = refs
     right = got[: columns.shape[1] // 2, :].astype(bf16)
     for j, out in zip(near, outs):
         out[...] = rows_of(scale, j, out.shape[0], columns, begun, right)
-
-
-def path_bits(count, near):
-    bits = list(range(count.bit_length() - 1))
-    orders = bits, bits[len(bits) // 2 :] + bits[: len(bits) // 2]
-    return orders[::-1] if near else orders
-
-
-def halve(step, near, product, stats, keep, message):
-    chips, n, rows, _ = product.shape
+    far_half(scale, far, True, columns, begun, own, got, keep, product)
+
+
+def round_of(step, near):
     first, second = path_bits(lax.axis_size("path"), near)
-    bit, place = (
+    return tuple(
         jnp.where(core_of() == 0, a, b)
         for a, b in (
             (first[step], second[step]),
             tuple(sum(x < order[step] for x in order[step + 1 :]) for order in (first, second)),
         )
     )
+
+
+def place_of(i, value, place):
+    low = i & ((1 << place) - 1)
+    return ((i - low) << 1) + (value << place) + low
+
+
+def path_bits(count, near):
+    bits = list(range(count.bit_length() - 1))
+    orders = bits, bits[len(bits) // 2 :] + bits[: len(bits) // 2]
+    return orders[::-1] if near else orders
+
+
+def halve(step, near, product, stats, keep, message):
+    chips, n, rows, _ = product.shape
+    bit, place = round_of(step, near)
     mine = (lax.axis_index("path") >> bit) & 1
     for out, value in ((keep, mine), (message, 1 - mine)):
         start = 0
         for k in range(chips):
             for i in range(n // 2):
-                low = i & ((1 << place) - 1)
-                out[start : start + rows, :] = product[k, ((i - low) << 1) + (value << place) + low]
+                out[start : start + rows, :] = product[k, place_of(i, value, place)]
                 start += rows
         if stats is not None:
             out[start:, :] = stats
@@ -499,26 +525,28 @@
         tail,
         flops=dates * paths * width * contracts,
     )
-    keep, message = call(
-        functools.partial(far_body, -1.0 / paths_total, far),
-        [piece(count // 2, len(far), True)] * 2,
+    (message,) = call(
+        functools.partial(far_half, -1.0 / paths_total, far, False),
+        [piece(count // 2, len(far), True)],
         columns,
         begun,
         tail,
         tail_other,
-        scratch=[pltpu.VMEM((len(far), count, rows, contracts), f32)],
-        flops=dates * paths * width * contracts // 2,
+        scratch=[pltpu.VMEM((count, rows, contracts), f32)],
+        flops=dates * paths * width * contracts // 4,
     )
     got = over_path(0, message)
-    firsts = call(
-        functools.partial(near_body, -1.0 / paths_total, near),
-        [piece(count, 1)] * len(near),
+    keep, *firsts = call(
+        functools.partial(near_body, -1.0 / paths_total, far, near),
+        [piece(count // 2, len(far), True)] + [piece(count, 1)] * len(near),
         columns,
         begun,
+        tail,
         tail_other,
         message,
         unread=1,
-        flops=dates * paths * width * contracts // 2,
+        scratch=[pltpu.VMEM((count, rows, contracts), f32)],
+        flops=3 * dates * paths * width * contracts // 4,
     )
     near_parts = [lax.ppermute(x, "date", date_pairs(chips, j)) if j else x for j, x in zip(near, firsts)]
     assert steps > 1

time: 39.7 us -> 39.6 us (level)
  no operation moved by 1% of the time
where the time goes in v10:
time: 39.6 us; the launch traced here: 39.5 us
  starting transfers between devices  19.5 us (49%)
  waiting for transfers between devices  13.7 us (35%)
  Pallas kernels  5.6 us (14%)
  between operations  0.74 us (2%)
    ppermute x3, starting transfers between devices, shards(): lax.ppermute(x, 'date', date_pairs(chips, j))  6.44 us
    ppermute x4, waiting for transfers between devices, over_path(): lax.ppermute(message, ('date', 'path'), path_pairs(chips, count, step, ne...  6.17 us
    ppermute x4, starting transfers between devices, over_path(): lax.ppermute(message, ('date', 'path'), path_pairs(chips, count, step, ne...  5.84 us
    pallas_call x15, Pallas kernels, call(): pl.pallas_call(kernel, out_shape=[jax.ShapeDtypeStruct(*o) for o in outs]...  5.6 us
    ppermute x1, starting transfers between devices, shards(): far = lax.ppermute(message, 'date', date_pairs(chips, 2))  3.4 us
    ppermute x1, starting transfers between devices, shards(): near = lax.ppermute(message, 'date', date_pairs(chips, 1))  3.02 us
    ppermute x1, waiting for transfers between devices, shards(): near = lax.ppermute(message, 'date', date_pairs(chips, 1))  2.3 us
    ppermute x3, waiting for transfers between devices, shards(): lax.ppermute(x, 'date', date_pairs(chips, j))  2.06 us
  transfers between devices with their start and end apart: 14, of which 8 were waited for; matrix products, arithmetic and copies ran while one was open for 0% of the time, Pallas kernels for 6%

profile of v10, /device:TPU:0, one launch (start us, length us, event | category | flops | bytes accessed | tf_op | source)
XLA Modules:
  0.0 39.5 jit_solution(12905116441156835058)
XLA Ops:
  0.6 1.8 %shard_map.67 = (f32[4,64,256]{2,1,0:T(8,128)S(1)}, bf16[2,64,2048]{2,1,0:T(8,128)(2,1)S(1)}, bf16[2048,256]{1,0:T(8,128)(2,1)S(1)}) custom-call(bf16[2,128,2048]{2,1,0:T(8,128)(2,1)} %refs_0_.3, bf16[2048,256]{1,0:T(8,128)(2,1)} %refs_1_.2, f32[2,128,256]{2,1,0:T(8,128)} %refs_1_.3, s32[2,256]{1,0:T(2,128)} %refs_2_.3), custom_call_target="tpu_custom_call" | custom-call | tf_op jit(solution)/shard_map/pallas_call | solution.py:42
  2.4 0.5 %collective-permute-start = (f32[4,64,256]{2,1,0:T(8,128)S(1)}, f32[4,64,256]{2,1,0:T(8,128)S(1)}, u32[]{:S(2)}, u32[]{:S(2)}) collective-permute-start(f32[4,64,256]{2,1,0:T(8,128)S(1)} %get-tuple-element.32), channel_id=1, source_target_pairs={{0,4},{4,0},{8,12},{12,8},{16,20},{20,16},{24,28},{28,24},{1,5},{5... | collective-permute-start | bytes 786440 | tf_op jit(solution)/shard_map/ppermute | solution.py:420
  3.0 1.4 %shard_map.68 = (f32[4,64,256]{2,1,0:T(8,128)S(1)}, bf16[2,128,2048]{2,1,0:T(8,128)(2,1)S(1)}) custom-call(bf16[2,128,2048]{2,1,0:T(8,128)(2,1)} %refs_0_.3, f32[2,128,256]{2,1,0:T(8,128)} %refs_1_.3, s32[2,256]{1,0:T(2,128)} %refs_2_.3, bf16[2048,256]{1,0:T(8,128)(2,1)S(1)} %get-tuple-element.28.refs_3_, bf16[2,64,2048]{2,1,0:T(8,128)(2,1)S(1)} %get-tuple-element.29.refs_4_), custom_call_target="tpu_custom_call" | custom-call | tf_op jit(solution)/shard_map/pallas_call | solution.py:42
  4.4 0.0 collective-permute-done.refs_1_
  4.4 0.1 shard_map.69
  4.5 0.1 shard_map.70
  4.7 0.1 collective-permute-start.1
  4.8 3.0 %collective-permute-start.4 = (f32[1,64,256]{2,1,0:T(8,128)S(1)}, f32[1,64,256]{2,1,0:T(8,128)S(1)}, u32[]{:S(2)}, u32[]{:S(2)}) collective-permute-start(f32[1,64,256]{2,1,0:T(8,128)S(1)} %get-tuple-element.33.refs_1_), channel_id=1, source_target_pairs={{0,8},{4,12},{8,0},{12,4},{16,24},{20,28},{24,16},{28,20},{1,9},{5... | collective-permute-start | bytes 196616 | tf_op jit(solution)/shard_map/ppermute | solution.py:451
  7.8 0.0 collective-permute-start.2
  7.8 0.0 collective-permute-start.3
  7.8 2.3 %collective-permute-done.4.refs_2_.refs_4_ = f32[1,64,256]{2,1,0:T(8,128)S(1)} collective-permute-done((f32[1,64,256]{2,1,0:T(8,128)S(1)}, f32[1,64,256]{2,1,0:T(8,128)S(1)}, u32[]{:S(2)}, u32[]{:S(2)}) %collective-permute-start.4) | collective-permute-done | bytes 65568 | tf_op jit(solution)/shard_map/ppermute | solution.py:451
  10.2 3.4 %collective-permute-start.5 = (f32[1,64,256]{2,1,0:T(8,128)S(1)}, f32[1,64,256]{2,1,0:T(8,128)S(1)}, u32[]{:S(2)}, u32[]{:S(2)}) collective-permute-start(f32[1,64,256]{2,1,0:T(8,128)S(1)} %shard_map.72), channel_id=1, source_target_pairs={{0,16},{4,20},{8,24},{12,28},{16,0},{20,4},{24,8},{28,12},{1,17},{... | collective-permute-start | bytes 196616 | tf_op jit(solution)/shard_map/ppermute | solution.py:455
  13.6 0.0 collective-permute-done.2.refs_2_.refs_6_
  13.6 0.0 collective-permute-done.3.refs_3_.refs_7_
  13.6 0.0 collective-permute-done.1.refs_1_
  13.6 0.3 shard_map.71.refs_8_.refs_0_
  13.9 1.9 %collective-permute-done.5.refs_5_ = f32[1,64,256]{2,1,0:T(8,128)S(1)} collective-permute-done((f32[1,64,256]{2,1,0:T(8,128)S(1)}, f32[1,64,256]{2,1,0:T(8,128)S(1)}, u32[]{:S(2)}, u32[]{:S(2)}) %collective-permute-start.5) | collective-permute-done | bytes 65568 | tf_op jit(solution)/shard_map/ppermute | solution.py:455
  15.8 0.2 shard_map.73.refs_1_.refs_2_
  16.0 0.1 collective-permute-start.6
  16.1 0.3 shard_map.74.refs_1_
  16.4 1.2 %collective-permute-done.6.refs_3_ = f32[264,256]{1,0:T(8,128)S(1)} collective-permute-done((f32[264,256]{1,0:T(8,128)S(1)}, f32[264,256]{1,0:T(8,128)S(1)}, u32[]{:S(2)}, u32[]{:S(2)}) %collective-permute-start.6) | collective-permute-done | bytes 270368 | tf_op jit(solution)/shard_map/ppermute | solution.py:499
  17.6 0.2 shard_map.75.refs_4_
  17.8 1.9 %collective-permute-start.7 = (f32[264,256]{1,0:T(8,128)S(1)}, f32[264,256]{1,0:T(8,128)S(1)}, u32[]{:S(2)}, u32[]{:S(2)}) collective-permute-start(f32[264,256]{1,0:T(8,128)S(1)} %shard_map.75.refs_4_), channel_id=1, source_target_pairs={{0,1},{1,0},{2,3},{3,2},{4,6},{5,7},{6,4},{7,5},{8,9},{9,8},{10,11... | collective-permute-start | bytes 811016 | tf_op jit(solution)/shard_map/ppermute | solution.py:508
  19.7 0.3 shard_map.76
  20.0 1.8 %collective-permute-start.9 = (f32[256,256]{1,0:T(8,128)S(1)}, f32[256,256]{1,0:T(8,128)S(1)}, u32[]{:S(2)}, u32[]{:S(2)}) collective-permute-start(f32[256,256]{1,0:T(8,128)S(1)} %get-tuple-element.42), channel_id=1, source_target_pairs={{0,8},{4,12},{8,0},{12,4},{16,24},{20,28},{24,16},{28,20},{1,9},{5... | collective-permute-start | bytes 786440 | tf_op jit(solution)/shard_map/ppermute | solution.py:551
  21.8 2.6 %collective-permute-done.7.refs_1_ = f32[264,256]{1,0:T(8,128)S(1)} collective-permute-done((f32[264,256]{1,0:T(8,128)S(1)}, f32[264,256]{1,0:T(8,128)S(1)}, u32[]{:S(2)}, u32[]{:S(2)}) %collective-permute-start.7) | collective-permute-done | bytes 270368 | tf_op jit(solution)/shard_map/ppermute | solution.py:508
  24.4 0.1 shard_map.77
  24.4 1.9 %collective-permute-start.8 = (f32[136,256]{1,0:T(8,128)S(1)}, f32[136,256]{1,0:T(8,128)S(1)}, u32[]{:S(2)}, u32[]{:S(2)}) collective-permute-start(f32[136,256]{1,0:T(8,128)S(1)} %get-tuple-element.40.refs_2_), channel_id=1, source_target_pairs={{0,2},{1,3},{2,0},{3,1},{4,5},{5,4},{6,7},{7,6},{8,10},{9,11},{10,... | collective-permute-start | bytes 417800 | tf_op jit(solution)/shard_map/ppermute | solution.py:508
  26.3 1.8 %collective-permute-done.9.refs_1_ = f32[256,256]{1,0:T(8,128)S(1)} collective-permute-done((f32[256,256]{1,0:T(8,128)S(1)}, f32[256,256]{1,0:T(8,128)S(1)}, u32[]{:S(2)}, u32[]{:S(2)}) %collective-permute-start.9) | collective-permute-done | bytes 262176 | tf_op jit(solution)/shard_map/ppermute | solution.py:551
  28.2 0.5 %collective-permute-start.12 = (f32[128,256]{1,0:T(8,128)S(1)}, f32[128,256]{1,0:T(8,128)S(1)}, u32[]{:S(2)}, u32[]{:S(2)}) collective-permute-start(f32[128,256]{1,0:T(8,128)S(1)} %get-tuple-element.43.refs_2_), channel_id=1, source_target_pairs={{0,2},{1,3},{2,0},{3,1},{4,5},{5,4},{6,7},{7,6},{8,10},{9,11},{10,... | collective-permute-start | bytes 393224 | tf_op jit(solution)/shard_map/ppermute | solution.py:508
  28.8 0.8 %collective-permute-done.8.refs_1_ = f32[136,256]{1,0:T(8,128)S(1)} collective-permute-done((f32[136,256]{1,0:T(8,128)S(1)}, f32[136,256]{1,0:T(8,128)S(1)}, u32[]{:S(2)}, u32[]{:S(2)}) %collective-permute-start.8) | collective-permute-done | bytes 139296 | tf_op jit(solution)/shard_map/ppermute | solution.py:508
  29.6 3.0 %collective-permute-start.10 = (f32[136,128]{1,0:T(8,128)S(1)}, f32[136,128]{1,0:T(8,128)S(1)}, u32[]{:S(2)}, u32[]{:S(2)}) collective-permute-start(f32[136,128]{1,0:T(8,128)S(1)} %get-tuple-element.45.refs_2_), channel_id=1, source_target_pairs={{0,16},{4,20},{8,24},{12,28},{16,0},{20,4},{24,8},{28,12},{1,17},{... | collective-permute-start | bytes 208904 | tf_op jit(solution)/shard_map/ppermute | solution.py:566
  32.6 1.6 %collective-permute-start.11 = (f32[136,128]{1,0:T(8,128)S(1)}, f32[136,128]{1,0:T(8,128)S(1)}, u32[]{:S(2)}, u32[]{:S(2)}) collective-permute-start(f32[136,128]{1,0:T(8,128)S(1)} %get-tuple-element.46), channel_id=1, source_target_pairs={{0,24},{4,28},{8,16},{12,20},{16,8},{20,12},{24,0},{28,4},{1,25},{... | collective-permute-start | bytes 208904 | tf_op jit(solution)/shard_map/ppermute | solution.py:566
  34.2 0.0 collective-permute-done.12.refs_1_
  34.3 1.5 %collective-permute-start.13 = (f32[64,256]{1,0:T(8,128)S(1)}, f32[64,256]{1,0:T(8,128)S(1)}, u32[]{:S(2)}, u32[]{:S(2)}) collective-permute-start(f32[64,256]{1,0:T(8,128)S(1)} %get-tuple-element.49), channel_id=1, source_target_pairs={{0,1},{1,0},{2,3},{3,2},{4,6},{5,7},{6,4},{7,5},{8,9},{9,8},{10,11... | collective-permute-start | bytes 196616 | tf_op jit(solution)/shard_map/ppermute | solution.py:508
  35.8 2.8 %collective-permute-done.13.refs_4_ = f32[64,256]{1,0:T(8,128)S(1)} collective-permute-done((f32[64,256]{1,0:T(8,128)S(1)}, f32[64,256]{1,0:T(8,128)S(1)}, u32[]{:S(2)}, u32[]{:S(2)}) %collective-permute-start.13) | collective-permute-done | bytes 65568 | tf_op jit(solution)/shard_map/ppermute | solution.py:508
  38.6 0.0 collective-permute-done.10.refs_1_
  38.6 0.2 collective-permute-done.11.refs_2_
  38.8 0.7 %shard_map.81 = (f32[64,256]{1,0:T(8,128)}, f32[1,256]{1,0:T(1,128)}, f32[1,256]{1,0:T(1,128)}) custom-call(f32[8,256]{1,0:T(8,128)S(1)} %get-tuple-element.44.refs_0_, f32[136,128]{1,0:T(8,128)S(1)} %collective-permute-done.10.refs_1_, f32[136,128]{1,0:T(8,128)S(1)} %collective-permute-done.11.refs_2_, f32[64,256]{1,0:T(8,128)S(1)} %get-tuple-element.48.refs_3_, ...), custom_call_target="tpu_custom_call" | custom-call | tf_op jit(solution)/shard_map/pallas_call | solution.py:42
  (4 shorter events, 0.1 us)
Async XLA Ops:
  2.4 2.0 %collective-permute-start = (f32[4,64,256]{2,1,0:T(8,128)S(1)}, f32[4,64,256]{2,1,0:T(8,128)S(1)}, u32[]{:S(2)}, u32[]{:S(2)}) collective-permute-start(f32[4,64,256]{2,1,0:T(8,128)S(1)} %get-tuple-element.32), channel_id=1, source_target_pairs={{0,4},{4,0},{8,12},{12,8},{16,20},{20,16},{24,28},{28,24},{1,5},{5... | collective-permute-start | bytes 786440 | tf_op jit(solution)/shard_map/ppermute | solution.py:420
  4.7 8.9 %collective-permute-start.1 = (f32[2,128,1024]{2,1,0:T(8,128)S(1)}, f32[2,128,1024]{2,1,0:T(8,128)S(1)}, u32[]{:S(2)}, u32[]{:S(2)}) collective-permute-start(f32[2,128,1024]{2,1,0:T(8,128)S(1)} %shard_map.70), channel_id=1, source_target_pairs={{0,4},{4,0},{8,12},{12,8},{16,20},{20,16},{24,28},{28,24},{1,5},{5... | collective-permute-start | bytes 3145736 | tf_op jit(solution)/shard_map/ppermute | solution.py:448
  4.8 5.4 %collective-permute-start.4 = (f32[1,64,256]{2,1,0:T(8,128)S(1)}, f32[1,64,256]{2,1,0:T(8,128)S(1)}, u32[]{:S(2)}, u32[]{:S(2)}) collective-permute-start(f32[1,64,256]{2,1,0:T(8,128)S(1)} %get-tuple-element.33.refs_1_), channel_id=1, source_target_pairs={{0,8},{4,12},{8,0},{12,4},{16,24},{20,28},{24,16},{28,20},{1,9},{5... | collective-permute-start | bytes 196616 | tf_op jit(solution)/shard_map/ppermute | solution.py:451
  7.8 5.8 %collective-permute-start.2 = (f32[64,256]{1,0:T(8,128)S(1)}, f32[64,256]{1,0:T(8,128)S(1)}, u32[]{:S(2)}, u32[]{:S(2)}) collective-permute-start(f32[64,256]{1,0:T(8,128)S(1)} %get-tuple-element.34.refs_0_.refs_3_), channel_id=1, source_target_pairs={{0,8},{4,12},{8,0},{12,4},{16,24},{20,28},{24,16},{28,20},{1,9},{5... | collective-permute-start | bytes 196616 | tf_op jit(solution)/shard_map/ppermute | solution.py:452
  7.8 5.8 %collective-permute-start.3 = (f32[64,256]{1,0:T(8,128)S(1)}, f32[64,256]{1,0:T(8,128)S(1)}, u32[]{:S(2)}, u32[]{:S(2)}) collective-permute-start(f32[64,256]{1,0:T(8,128)S(1)} %get-tuple-element.34.refs_0_.refs_3_), channel_id=1, source_target_pairs={{8,16},{12,20},{16,8},{20,12},{0,4},{4,0},{24,28},{28,24},{9,17},{... | collective-permute-start | bytes 196616 | tf_op jit(solution)/shard_map/ppermute | solution.py:453
  10.2 5.6 %collective-permute-start.5 = (f32[1,64,256]{2,1,0:T(8,128)S(1)}, f32[1,64,256]{2,1,0:T(8,128)S(1)}, u32[]{:S(2)}, u32[]{:S(2)}) collective-permute-start(f32[1,64,256]{2,1,0:T(8,128)S(1)} %shard_map.72), channel_id=1, source_target_pairs={{0,16},{4,20},{8,24},{12,28},{16,0},{20,4},{24,8},{28,12},{1,17},{... | collective-permute-start | bytes 196616 | tf_op jit(solution)/shard_map/ppermute | solution.py:455
  16.0 1.6 %collective-permute-start.6 = (f32[264,256]{1,0:T(8,128)S(1)}, f32[264,256]{1,0:T(8,128)S(1)}, u32[]{:S(2)}, u32[]{:S(2)}) collective-permute-start(f32[264,256]{1,0:T(8,128)S(1)} %shard_map.73.refs_1_.refs_2_), channel_id=1, source_target_pairs={{0,4},{4,0},{8,12},{12,8},{16,20},{20,16},{24,28},{28,24},{1,5},{5... | collective-permute-start | bytes 811016 | tf_op jit(solution)/shard_map/ppermute | solution.py:499
  17.8 6.5 %collective-permute-start.7 = (f32[264,256]{1,0:T(8,128)S(1)}, f32[264,256]{1,0:T(8,128)S(1)}, u32[]{:S(2)}, u32[]{:S(2)}) collective-permute-start(f32[264,256]{1,0:T(8,128)S(1)} %shard_map.75.refs_4_), channel_id=1, source_target_pairs={{0,1},{1,0},{2,3},{3,2},{4,6},{5,7},{6,4},{7,5},{8,9},{9,8},{10,11... | collective-permute-start | bytes 811016 | tf_op jit(solution)/shard_map/ppermute | solution.py:508
  20.0 8.2 %collective-permute-start.9 = (f32[256,256]{1,0:T(8,128)S(1)}, f32[256,256]{1,0:T(8,128)S(1)}, u32[]{:S(2)}, u32[]{:S(2)}) collective-permute-start(f32[256,256]{1,0:T(8,128)S(1)} %get-tuple-element.42), channel_id=1, source_target_pairs={{0,8},{4,12},{8,0},{12,4},{16,24},{20,28},{24,16},{28,20},{1,9},{5... | collective-permute-start | bytes 786440 | tf_op jit(solution)/shard_map/ppermute | solution.py:551
  24.4 5.1 %collective-permute-start.8 = (f32[136,256]{1,0:T(8,128)S(1)}, f32[136,256]{1,0:T(8,128)S(1)}, u32[]{:S(2)}, u32[]{:S(2)}) collective-permute-start(f32[136,256]{1,0:T(8,128)S(1)} %get-tuple-element.40.refs_2_), channel_id=1, source_target_pairs={{0,2},{1,3},{2,0},{3,1},{4,5},{5,4},{6,7},{7,6},{8,10},{9,11},{10,... | collective-permute-start | bytes 417800 | tf_op jit(solution)/shard_map/ppermute | solution.py:508
  28.2 6.0 %collective-permute-start.12 = (f32[128,256]{1,0:T(8,128)S(1)}, f32[128,256]{1,0:T(8,128)S(1)}, u32[]{:S(2)}, u32[]{:S(2)}) collective-permute-start(f32[128,256]{1,0:T(8,128)S(1)} %get-tuple-element.43.refs_2_), channel_id=1, source_target_pairs={{0,2},{1,3},{2,0},{3,1},{4,5},{5,4},{6,7},{7,6},{8,10},{9,11},{10,... | collective-permute-start | bytes 393224 | tf_op jit(solution)/shard_map/ppermute | solution.py:508
  29.6 9.0 %collective-permute-start.10 = (f32[136,128]{1,0:T(8,128)S(1)}, f32[136,128]{1,0:T(8,128)S(1)}, u32[]{:S(2)}, u32[]{:S(2)}) collective-permute-start(f32[136,128]{1,0:T(8,128)S(1)} %get-tuple-element.45.refs_2_), channel_id=1, source_target_pairs={{0,16},{4,20},{8,24},{12,28},{16,0},{20,4},{24,8},{28,12},{1,17},{... | collective-permute-start | bytes 208904 | tf_op jit(solution)/shard_map/ppermute | solution.py:566
  32.6 6.2 %collective-permute-start.11 = (f32[136,128]{1,0:T(8,128)S(1)}, f32[136,128]{1,0:T(8,128)S(1)}, u32[]{:S(2)}, u32[]{:S(2)}) collective-permute-start(f32[136,128]{1,0:T(8,128)S(1)} %get-tuple-element.46), channel_id=1, source_target_pairs={{0,24},{4,28},{8,16},{12,20},{16,8},{20,12},{24,0},{28,4},{1,25},{... | collective-permute-start | bytes 208904 | tf_op jit(solution)/shard_map/ppermute | solution.py:566
  34.3 4.3 %collective-permute-start.13 = (f32[64,256]{1,0:T(8,128)S(1)}, f32[64,256]{1,0:T(8,128)S(1)}, u32[]{:S(2)}, u32[]{:S(2)}) collective-permute-start(f32[64,256]{1,0:T(8,128)S(1)} %get-tuple-element.49), channel_id=1, source_target_pairs={{0,1},{1,0},{2,3},{3,2},{4,6},{5,7},{6,4},{7,5},{8,9},{9,8},{10,11... | collective-permute-start | bytes 196616 | tf_op jit(solution)/shard_map/ppermute | solution.py:508
